TPU v7x, 512 devices: a whole 4x8x8 slice. The times are simulated.
512 devices in a mesh: ctx: 16 (over y, z_lo), tp: 32 (over x, z_hi, core).
Axes of the slice: x: 4, y: 8, z: 8 (z_hi: 4, z_lo: 2; z = z_hi * 2 + z_lo), core: 2. Of those that a mesh axis runs over, the one named last changes fastest.
Arguments:
- x_in: bfloat16 [8192, 16384], P('ctx', 'tp'), may hold values from -6 to 6
- bc_in: bfloat16 [8192, 4096], P(('ctx', 'tp')), may hold values from -6 to 6
- conv_x: float32 [4, 16384], P(None, 'tp'), may hold values from -3 to 3
- conv_bc: float32 [4, 4096], replicated, may hold values from -3 to 3
- log_decay: float32 [8192, 256], P('ctx', 'tp'), may hold values from -2 to 0, as said below
- grad_y: bfloat16 [8192, 16384], P('ctx', 'tp'), may hold values from -0.009765625 to 0.009765625
Outputs:
- grad_x: bfloat16 [8192, 16384], P('ctx', 'tp')
- grad_bc: float32 [8192, 4096], P(('ctx', 'tp'))
- grad_decay: float32 [8192, 256], P('ctx', 'tp')
Inputs may be any that keep to these rules, and one draw needn't show every extreme that they name: `log_decay`: each entry is the logarithm of a decay factor of one head at one token.
All inputs are finite; a program needn't handle non-finite values.
Results may differ from a plain program's by a relative error of at most 0.00205.
Values may be sent and summed in bfloat16 or wider, within the bound.
No kernel may reach another device: no remote copies, remote signals or barrier semaphores. Data moves between devices by JAX's collectives and lax.ppermute only.
A program may use at most 128 MiB of HBM per device.

v0:
```python
import jax
import jax.numpy as jnp
from jax import lax
from jax.sharding import PartitionSpec as P

HEAD_DIM = 64
STATE = 256
CONV = 4
HEADS_GROUP = 32
BLOCK = 256


def shifted(array, axis, by):
    devices = lax.axis_size(axis)
    pairs = [(i, i + by) for i in range(devices) if 0 <= i + by < devices]
    return lax.ppermute(array, axis, pairs)


def entering(part, axis, combine, identity, reverse):
    count = lax.axis_size(axis)
    place = lax.axis_index(axis)
    ahead = count - 1 - place if reverse else place
    gathered = jax.tree.map(lambda a: lax.all_gather(a, axis), part)
    state = jax.tree.map(lambda a, e: jnp.zeros_like(a) + jnp.asarray(e, a.dtype), part, identity)

    def one(step, state):
        source = count - 1 - step if reverse else step
        return combine(
            state, jax.tree.map(lambda a: lax.dynamic_index_in_dim(a, source, 0, False), gathered)
        )

    return lax.fori_loop(0, ahead, one, state)


def conv_after(earlier, values, conv_taps):
    row_count = values.shape[0]
    joined = jnp.concatenate([earlier, values], axis=0).astype(jnp.float32)
    summed = conv_taps[0] * joined[0:row_count]
    for offset in range(1, CONV):
        summed = summed + conv_taps[offset] * joined[offset : offset + row_count]
    return summed


def conv_before(grad_rows, later_rows, conv_taps):
    row_count = grad_rows.shape[0]
    conv_lag = CONV - 1
    joined = jnp.concatenate([grad_rows, later_rows], axis=0)
    summed = conv_taps[0] * joined[conv_lag : conv_lag + row_count]
    for offset in range(1, CONV):
        summed = (
            summed + conv_taps[offset] * joined[conv_lag - offset : conv_lag - offset + row_count]
        )
    return summed


def silu_slope(values):
    sigmoid_gate = jax.nn.sigmoid(values)
    return sigmoid_gate * (1.0 + values * (1.0 - sigmoid_gate))


def fan_groups(rows, copies):
    row_count = rows.shape[0]
    group_count = rows.shape[1] // (2 * STATE)
    shaped = rows.reshape(row_count, group_count, 1, 2 * STATE)
    spread = jnp.broadcast_to(shaped, (row_count, group_count, copies, 2 * STATE))
    return spread.reshape(row_count, group_count * copies * 2 * STATE)


def fold_groups(terms, copies):
    row_count = terms.shape[0]
    group_count = terms.shape[1] // (2 * STATE * copies)
    shaped = terms.reshape(row_count, group_count, copies, 2 * STATE)
    return jnp.sum(shaped, axis=2).reshape(row_count, group_count * 2 * STATE)


def block_pass(carried_state, pieces):
    inputs, key_acts, queries, log_rates = pieces
    span_rows = log_rates.shape[0]
    cumulative = jnp.cumsum(log_rates, axis=0)
    row_index = jnp.arange(span_rows, dtype=jnp.int32)[:, None]
    col_index = jnp.arange(span_rows, dtype=jnp.int32)[None, :]
    causal = (row_index >= col_index)[:, :, None]
    gap_logs = jnp.where(causal, cumulative[:, None, :] - cumulative[None, :, :], 0.0)
    mixing = jnp.where(causal, jnp.exp(gap_logs), 0.0)
    scores = jnp.dot(
        queries, key_acts.T, preferred_element_type=jnp.float32, precision=lax.Precision.HIGHEST
    )
    within = jnp.einsum(
        "ijh,jhp->ihp", mixing * scores[:, :, None], inputs, precision=lax.Precision.HIGHEST
    )
    carried = (
        jnp.einsum("in,hpn->ihp", queries, carried_state, precision=lax.Precision.HIGHEST)
        * jnp.exp(cumulative)[:, :, None]
    )
    last_log = cumulative[-1]
    fading = jnp.exp(last_log[None, :] - cumulative)
    added = jnp.einsum(
        "jhp,jn->hpn", inputs * fading[:, :, None], key_acts, precision=lax.Precision.HIGHEST
    )
    new_state = jnp.exp(last_log)[:, None, None] * carried_state + added
    return (new_state, within + carried)


def state_space(inputs, key_acts, queries, log_rates, carried_state):
    row_count = inputs.shape[0]
    head_count = log_rates.shape[1]
    block_count = row_count // BLOCK
    shaped = (
        inputs.reshape(block_count, BLOCK, head_count, HEAD_DIM),
        key_acts.reshape(block_count, BLOCK, STATE),
        queries.reshape(block_count, BLOCK, STATE),
        log_rates.reshape(block_count, BLOCK, head_count),
    )
    final_state, outputs = lax.scan(block_pass, carried_state, shaped)
    return (outputs.reshape(row_count, head_count * HEAD_DIM), final_state)


def link_states(earlier, later):
    decay_early, state_early = earlier
    decay_late, state_late = later
    return (decay_early * decay_late, decay_late[:, None, None] * state_early + state_late)


def per_device(x_in, bc_in, conv_x, conv_bc, log_decay, grad_y):
    row_count = x_in.shape[0]
    head_count = log_decay.shape[1]
    conv_lag = CONV - 1
    copies = HEADS_GROUP // head_count
    bc_start = lax.axis_index("tp") // copies * (2 * STATE)
    group_taps = lax.dynamic_slice_in_dim(conv_bc, bc_start, 2 * STATE, 1)
    bc_rows = lax.all_to_all(
        fan_groups(bc_in, copies), "tp", split_axis=1, concat_axis=0, tiled=True
    )
    x_prev, bc_prev = shifted(
        (x_in[row_count - conv_lag :], bc_rows[row_count - conv_lag :]), "ctx", 1
    )
    bc_pre = conv_after(bc_prev, bc_rows, group_taps)
    bc_act = jax.nn.silu(bc_pre)
    x_pre = conv_after(x_prev, x_in, conv_x)
    x_act = jax.nn.silu(x_pre)
    key_acts = bc_act[:, :STATE]
    queries = bc_act[:, STATE:]
    upstream = grad_y.astype(jnp.float32)
    cumulative = jnp.cumsum(log_decay, axis=0)
    total_log = cumulative[-1]
    fading = jnp.exp(total_log[None, :] - cumulative)
    local_state = jnp.einsum(
        "thp,tn->hpn",
        x_act.reshape(row_count, head_count, HEAD_DIM) * fading[:, :, None],
        key_acts,
        precision=lax.Precision.HIGHEST,
    )
    local_grad = jnp.einsum(
        "thp,tn->hpn",
        upstream.reshape(row_count, head_count, HEAD_DIM) * jnp.exp(cumulative)[:, :, None],
        queries,
        precision=lax.Precision.HIGHEST,
    )
    decays = jnp.exp(total_log)
    neutral = (jnp.ones_like(decays), jnp.zeros_like(local_state))
    before_decay, incoming = entering((decays, local_state), "ctx", link_states, neutral, False)
    after_decay, outgoing = entering((decays, local_grad), "ctx", link_states, neutral, True)
    outputs, pullback = jax.vjp(state_space, x_act, key_acts, queries, log_decay, incoming)
    grad_acts, grad_keys, grad_queries, grad_logs, grad_start = pullback((upstream, outgoing))
    grad_bc_act = jnp.concatenate([grad_keys, grad_queries], axis=1)
    grad_x_pre = grad_acts * silu_slope(x_pre)
    grad_bc_pre = grad_bc_act * silu_slope(bc_pre)
    x_later, bc_later = shifted((grad_x_pre[:conv_lag], grad_bc_pre[:conv_lag]), "ctx", -1)
    group_terms = conv_before(grad_bc_pre, bc_later, group_taps)
    grad_bc = fold_groups(
        lax.all_to_all(group_terms, "tp", split_axis=0, concat_axis=1, tiled=True), copies
    )
    grad_x = conv_before(grad_x_pre, x_later, conv_x).astype(jnp.bfloat16)
    return (grad_x, grad_bc, grad_logs)


def solution(mesh):
    return jax.shard_map(
        per_device,
        mesh=mesh,
        in_specs=(
            P("ctx", "tp"),
            P(("ctx", "tp"), None),
            P(None, "tp"),
            P(),
            P("ctx", "tp"),
            P("ctx", "tp"),
        ),
        out_specs=(P("ctx", "tp"), P(("ctx", "tp"), None), P("ctx", "tp")),
        check_vma=False,
    )
```

profile of v0, /device:TPU:1, one launch (start us, length us, event | category | flops | bytes accessed | tf_op | source)
XLA Modules:
  0.0 566.8 jit_solution(10323165385264338301)
XLA Ops:
  9.0 14.4 %all-to-all-start = ((bf16[16,32,512]{2,0,1:T(8,128)(2,1)}), bf16[16,32,512]{2,0,1:T(8,128)(2,1)S(1)}, u32[]{:S(2)}, u32[]{:S(2)}) async-start(bf16[16,32,512]{2,0,1:T(8,128)(2,1)} %bitcast.14), calls=%async_computation | async-start | bytes 1048576 | tf_op jit(solution)/shard_map/all_to_all | solution.py:131
  24.2 3.1 collective-permute-start.1
  27.3 2.2 reduce-window.46
  31.5 9.9 %all-to-all-done = bf16[16,32,512]{2,0,1:T(8,128)(2,1)S(1)} async-done(((bf16[16,32,512]{2,0,1:T(8,128)(2,1)}), bf16[16,32,512]{2,0,1:T(8,128)(2,1)S(1)}, u32[]{:S(2)}, u32[]{:S(2)}) %all-to-all-start) | async-done | bytes 524320 | tf_op jit(solution)/shard_map/all_to_all | solution.py:131
  41.4 4.1 collective-permute-start
  45.5 1.7 fusion.111
  47.7 1.6 fusion.112
  49.3 1.8 fusion.109
  51.5 1.8 fusion.113
  53.4 1.6 reshape.276
  55.1 29.1 %all-gather.2 = f32[16,1,8]{2,1,0:T(1,128)S(1)} all-gather(f32[1,1,8]{2,1,0:T(1,128)S(1)} %bitcast.425), channel_id=1, replica_groups=mesh['ctx'=16,'tp'=32] {'ctx'}, dimensions={0}, use_global_device_ids=true | all-gather | bytes 544 | tf_op jit(solution)/shard_map/all_gather | solution.py:23
  85.1 148.4 %all-gather.8.cloned.1.call-done = f32[128,64,256]{2,1,0:T(8,128)} async-done(((f32[8,64,256]{2,1,0:T(8,128)}), f32[128,64,256]{2,1,0:T(8,128)}) %all-gather.8.cloned.1.call-update) | async-done | bytes 8388624 | tf_op jit(solution)/shard_map/all_gather | solution.py:23
  235.8 18.4 %while.95 = (s32[]{:T(128)}, f32[8,64,256]{2,1,0:T(8,128)S(1)}, f32[2,256,256,8]{2,3,1,0:T(8,128)}, f32[2,256,256]{1,2,0:T(8,128)}, f32[2,256,256,1]{2,1,3,0:T(8...) while((s32[]{:T(128)}, f32[8,64,256]{2,1,0:T(8,128)S(1)}, ...), condition=%wide.region_9.10_spmd.clone.clone, body=%wide.region_6.9_spmd.clone.clone.sunk | while | flops 1009518592 | bytes 38773344 | solution.py:114
  238.0 3.3 multiply_dynamic-update-slice_fusion.2
  247.2 3.3 multiply_dynamic-update-slice_fusion.2
  254.3 168.4 %all-gather.6.cloned.1.call-done = f32[128,64,256]{2,1,0:T(8,128)} async-done(((f32[8,64,256]{2,1,0:T(8,128)}), f32[128,64,256]{2,1,0:T(8,128)}) %all-gather.6.cloned.1.call-update) | async-done | bytes 8388624 | tf_op jit(solution)/shard_map/all_gather | solution.py:23
  422.7 18.8 %while.93 = (s32[]{:T(128)}, f32[8,64,256]{2,1,0:T(8,128)S(1)}, s32[]{:T(128)}, f32[16,8]{1,0:T(8,128)S(1)}, f32[16,8,64,256]{3,2,1,0:T(8,128)}, /*index=5*/s32[]{:T(128)}, s32[]{:T(128)}, s32[]{:T(128)}, s32[]{:T(128)}) while((s32[]{:T(128)}, f32[8,64,256]{2,1,0:T(8,128)S(1)}, s32[]{:T(128)}, f32[16,8]{1,0:T(8,128)S(1)}, ...), condition=%wide.region_3.4_spmd, body=%wide.region_2.3_spmd.sunk | while | flops 262150 | bytes 1573107 | solution.py:32
  422.7 1.2 bitcast_add_fusion.4
  424.0 1.2 bitcast_add_fusion.4
  425.2 1.2 bitcast_add_fusion.4
  426.5 1.2 bitcast_add_fusion.4
  427.7 1.2 bitcast_add_fusion.4
  429.0 1.2 bitcast_add_fusion.4
  430.2 1.2 bitcast_add_fusion.4
  431.5 1.2 bitcast_add_fusion.4
  432.7 1.2 bitcast_add_fusion.4
  434.0 1.2 bitcast_add_fusion.4
  435.2 1.2 bitcast_add_fusion.4
  436.5 1.2 bitcast_add_fusion.4
  437.8 1.2 bitcast_add_fusion.4
  439.0 1.2 bitcast_add_fusion.4
  440.3 1.2 bitcast_add_fusion.4
  444.9 64.2 %while.96 = (s32[]{:T(128)}, f32[8,64,256]{2,1,0:T(8,128)S(1)}, f32[2,256,8,64]{1,3,2,0:T(8,128)}, f32[2,256,256]{2,1,0:T(8,128)}, f32[2,256,256]{2,1,0:T(8,128)...) while((s32[]{:T(128)}, f32[8,64,256]{2,1,0:T(8,128)S(1)}, ...), condition=%wide.region_20.21_spmd.clone.clone, body=%wide.region_10.20_spmd.clone.clone.sunk | while | flops 2824679424 | bytes 65804252 | solution.py:114
  444.9 1.8 constant_dynamic-slice_fusion.10
  446.6 2.5 constant_dynamic-slice_fusion.12
  450.1 3.7 fusion.183
  453.9 1.4 fusion.181
  455.5 1.7 fusion.188
  459.9 2.5 reduce-window.62
  463.9 2.2 convolution_bitcast_fusion.6
  466.1 2.0 fusion.185
  468.1 2.0 convolution_bitcast_fusion.5
  473.0 2.0 fusion.182
  476.8 1.8 constant_dynamic-slice_fusion.10
  478.6 2.5 constant_dynamic-slice_fusion.12
  482.1 3.7 fusion.183
  485.9 1.4 fusion.181
  487.5 1.7 fusion.188
  491.9 2.5 reduce-window.62
  495.9 2.2 convolution_bitcast_fusion.6
  498.1 2.0 fusion.185
  500.1 2.0 convolution_bitcast_fusion.5
  505.0 2.0 fusion.182
  509.1 1.9 maximum_multiply_fusion
  511.0 1.4 collective-permute-start.3
  512.5 3.1 collective-permute-done.3
  515.6 1.5 fusion.90
  517.0 11.5 %all-to-all-start.1 = ((f32[32,16,512]{2,1,0:T(8,128)}), f32[32,16,512]{2,1,0:T(8,128)}, u32[]{:S(2)}, u32[]{:S(2)}) async-start(f32[32,16,512]{2,1,0:T(8,128)} %bitcast.34), calls=%async_computation.1 | async-start | bytes 2097152 | tf_op jit(solution)/shard_map/all_to_all | solution.py:171
  529.9 1.6 multiply_multiply_fusion
  531.5 1.3 collective-permute-start.2
  532.8 13.3 %collective-permute-done.2 = f32[3,512]{1,0:T(4,128)S(1)} collective-permute-done((f32[3,512]{1,0:T(4,128)S(1)}, f32[3,512]{1,0:T(4,128)S(1)}, u32[]{:S(2)}, u32[]{:S(2)}) %collective-permute-start.2) | collective-permute-done | bytes 6176 | tf_op jit(solution)/shard_map/ppermute | solution.py:16
  546.1 1.3 fusion.98
  547.4 10.5 %all-to-all-done.1 = f32[32,16,512]{2,1,0:T(8,128)} async-done(((f32[32,16,512]{2,1,0:T(8,128)}), f32[32,16,512]{2,1,0:T(8,128)}, u32[]{:S(2)}, u32[]{:S(2)}) %all-to-all-start.1) | async-done | bytes 1048608 | tf_op jit(solution)/shard_map/all_to_all | solution.py:171
  557.9 1.3 bitcast_reduce_fusion
  (244 shorter events, 45.7 us)
Async XLA Ops:
  7.2 24.2 %copy-start.13 = (bf16[512,512]{1,0:T(8,128)(2,1)S(1)}, bf16[512,512]{1,0:T(8,128)(2,1)}, u32[]{:S(2)}) copy-start(bf16[512,512]{1,0:T(8,128)(2,1)} %param.14) | copy-start | bytes 1572868
  7.2 22.8 %copy-start.34 = (f32[4,512]{1,0:T(4,128)S(1)}, f32[4,512]{1,0:T(4,128)}, u32[]{:S(2)}) copy-start(f32[4,512]{1,0:T(4,128)} %param.16) | copy-start | bytes 24580
  9.0 32.3 %all-to-all-start = ((bf16[16,32,512]{2,0,1:T(8,128)(2,1)}), bf16[16,32,512]{2,0,1:T(8,128)(2,1)S(1)}, u32[]{:S(2)}, u32[]{:S(2)}) async-start(bf16[16,32,512]{2,0,1:T(8,128)(2,1)} %bitcast.14), calls=%async_computation | async-start | bytes 1048576 | tf_op jit(solution)/shard_map/all_to_all | solution.py:131
  23.5 210.1 %all-gather.8.cloned.1.call-start = ((), (), s32[]{:S(2)}) async-start(), calls=%async_computation.3 | async-start | bytes 8912896 | tf_op jit(solution)/shard_map/all_gather | solution.py:23
  24.2 7.1 %collective-permute-start.1 = (bf16[3,512]{1,0:T(4,128)(2,1)S(1)}, bf16[3,512]{1,0:T(4,128)(2,1)S(1)}, u32[]{:S(2)}, u32[]{:S(2)}) collective-permute-start(bf16[3,512]{1,0:T(4,128)(2,1)S(1)} %slice.149), channel_id=1, source_target_pairs={{0,32},{32,64},{64,96},{96,128},{128,160},{160,192},{192,224},{224... | collective-permute-start | bytes 9224 | tf_op jit(solution)/shard_map/ppermute | solution.py:16
  30.0 17.1 %copy-start.18 = (f32[1,512]{1,0:T(1,128)}, f32[1,512]{1,0:T(1,128)S(1)}, u32[]{:S(2)}) copy-start(f32[1,512]{1,0:T(1,128)S(1)} %get-tuple-element.1569) | copy-start | bytes 6148
  30.0 17.1 %copy-start.20 = (f32[1,512]{1,0:T(1,128)}, f32[1,512]{1,0:T(1,128)S(1)}, u32[]{:S(2)}) copy-start(f32[1,512]{1,0:T(1,128)S(1)} %get-tuple-element.1570) | copy-start | bytes 6148
  30.1 17.1 %copy-start.22 = (f32[1,512]{1,0:T(1,128)}, f32[1,512]{1,0:T(1,128)S(1)}, u32[]{:S(2)}) copy-start(f32[1,512]{1,0:T(1,128)S(1)} %get-tuple-element.1571) | copy-start | bytes 6148
  30.1 17.1 %copy-start.24 = (f32[1,512]{1,0:T(1,128)}, f32[1,512]{1,0:T(1,128)S(1)}, u32[]{:S(2)}) copy-start(f32[1,512]{1,0:T(1,128)S(1)} %get-tuple-element.1572) | copy-start | bytes 6148
  31.1 16.6 %copy-start.26 = (f32[1,512]{1,0:T(1,128)}, f32[1,512]{1,0:T(1,128)S(1)}, u32[]{:S(2)}) copy-start(f32[1,512]{1,0:T(1,128)S(1)} %get-tuple-element.1565) | copy-start | bytes 6148
  31.1 16.6 %copy-start.28 = (f32[1,512]{1,0:T(1,128)}, f32[1,512]{1,0:T(1,128)S(1)}, u32[]{:S(2)}) copy-start(f32[1,512]{1,0:T(1,128)S(1)} %get-tuple-element.1566) | copy-start | bytes 6148
  31.1 16.6 %copy-start.30 = (f32[1,512]{1,0:T(1,128)}, f32[1,512]{1,0:T(1,128)S(1)}, u32[]{:S(2)}) copy-start(f32[1,512]{1,0:T(1,128)S(1)} %get-tuple-element.1567) | copy-start | bytes 6148
  31.1 16.6 %copy-start.32 = (f32[1,512]{1,0:T(1,128)}, f32[1,512]{1,0:T(1,128)S(1)}, u32[]{:S(2)}) copy-start(f32[1,512]{1,0:T(1,128)S(1)} %get-tuple-element.1568) | copy-start | bytes 6148
  41.4 6.1 %collective-permute-start = (bf16[3,512]{1,0:T(4,128)(2,1)S(1)}, bf16[3,512]{1,0:T(4,128)(2,1)S(1)}, u32[]{:S(2)}, u32[]{:S(2)}) collective-permute-start(bf16[3,512]{1,0:T(4,128)(2,1)S(1)} %slice.181), channel_id=1, source_target_pairs={{0,32},{32,64},{64,96},{96,128},{128,160},{160,192},{192,224},{224... | collective-permute-start | bytes 9224 | tf_op jit(solution)/shard_map/ppermute | solution.py:16
  49.3 1.9 copy-start.14
  51.1 371.5 %all-gather.6.cloned.1.call-start = ((), (), s32[]{:S(2)}) async-start(), calls=%async_computation.2 | async-start | bytes 8912896 | tf_op jit(solution)/shard_map/all_gather | solution.py:23
  233.6 2.3 copy-start.15
  238.0 4.2 copy-start.4
  238.0 4.2 copy-start.6
  241.3 1.6 copy-start.1
  242.2 1.6 copy-start.5
  242.9 1.4 copy-start.7
  242.9 1.1 copy-start.2
  247.2 4.1 copy-start.4
  247.2 4.2 copy-start.6
  250.5 1.6 copy-start.1
  251.4 1.6 copy-start.5
  252.0 1.4 copy-start.7
  252.1 1.1 copy-start.2
  444.9 4.3 copy-start.16
  444.9 4.3 copy-start.35
  462.5 7.7 %copy-start.11 = (f32[2,256,256]{2,1,0:T(8,128)S(1)}, f32[2,256,256]{2,1,0:T(8,128)}, u32[]{:S(2)}) copy-start(f32[2,256,256]{2,1,0:T(8,128)} %get-tuple-element.2114) | copy-start | bytes 1572868 | tf_op jit(solution)/shard_map/transpose(jvp())/while
  463.9 7.7 %copy-start.3 = (f32[2,256,256,8]{2,3,1,0:T(8,128)S(1)}, f32[2,256,256,8]{2,3,1,0:T(8,128)}, u32[]{:S(2)}) copy-start(f32[2,256,256,8]{2,3,1,0:T(8,128)} %get-tuple-element.2150) | copy-start | bytes 12582916 | tf_op jit(solution)/shard_map/transpose(jvp())/while
  470.8 0.8 copy-start.12
  471.6 1.0 copy-start
  471.6 1.4 copy-start.8
  471.8 4.2 copy-start.36
  473.0 3.8 copy-start.17
  475.0 1.0 copy-start.9
  476.8 4.3 copy-start.16
  476.8 4.3 copy-start.35
  494.5 7.7 %copy-start.11 = (f32[2,256,256]{2,1,0:T(8,128)S(1)}, f32[2,256,256]{2,1,0:T(8,128)}, u32[]{:S(2)}) copy-start(f32[2,256,256]{2,1,0:T(8,128)} %get-tuple-element.2114) | copy-start | bytes 1572868 | tf_op jit(solution)/shard_map/transpose(jvp())/while
  495.9 7.7 %copy-start.3 = (f32[2,256,256,8]{2,3,1,0:T(8,128)S(1)}, f32[2,256,256,8]{2,3,1,0:T(8,128)}, u32[]{:S(2)}) copy-start(f32[2,256,256,8]{2,3,1,0:T(8,128)} %get-tuple-element.2150) | copy-start | bytes 12582916 | tf_op jit(solution)/shard_map/transpose(jvp())/while
  502.8 0.8 copy-start.12
  503.6 1.0 copy-start
  503.6 1.4 copy-start.8
  503.7 4.2 copy-start.36
  505.0 3.8 copy-start.17
  506.9 1.0 copy-start.9
  509.0 6.5 %copy-start.27 = (f32[1,512]{1,0:T(1,128)S(1)}, f32[1,512]{1,0:T(1,128)}, u32[]{:S(2)}) copy-start(f32[1,512]{1,0:T(1,128)} %copy-done.26) | copy-start | bytes 6148
  509.0 6.5 %copy-start.29 = (f32[1,512]{1,0:T(1,128)S(1)}, f32[1,512]{1,0:T(1,128)}, u32[]{:S(2)}) copy-start(f32[1,512]{1,0:T(1,128)} %copy-done.28) | copy-start | bytes 6148
  509.0 6.5 %copy-start.31 = (f32[1,512]{1,0:T(1,128)S(1)}, f32[1,512]{1,0:T(1,128)}, u32[]{:S(2)}) copy-start(f32[1,512]{1,0:T(1,128)} %copy-done.30) | copy-start | bytes 6148
  509.1 6.5 %copy-start.33 = (f32[1,512]{1,0:T(1,128)S(1)}, f32[1,512]{1,0:T(1,128)}, u32[]{:S(2)}) copy-start(f32[1,512]{1,0:T(1,128)} %copy-done.32) | copy-start | bytes 6148
  511.0 17.5 %copy-start.10 = (f32[2,256,8,64]{1,3,2,0:T(8,128)S(1)}, f32[2,256,8,64]{1,3,2,0:T(8,128)}, u32[]{:S(2)}) copy-start(f32[2,256,8,64]{1,3,2,0:T(8,128)} %get-tuple-element.938) | copy-start | bytes 3145732
  511.0 4.5 collective-permute-start.3
  517.0 40.9 %all-to-all-start.1 = ((f32[32,16,512]{2,1,0:T(8,128)}), f32[32,16,512]{2,1,0:T(8,128)}, u32[]{:S(2)}, u32[]{:S(2)}) async-start(f32[32,16,512]{2,1,0:T(8,128)} %bitcast.34), calls=%async_computation.1 | async-start | bytes 2097152 | tf_op jit(solution)/shard_map/all_to_all | solution.py:171
  529.8 16.3 %copy-start.19 = (f32[1,512]{1,0:T(1,128)S(1)}, f32[1,512]{1,0:T(1,128)}, u32[]{:S(2)}) copy-start(f32[1,512]{1,0:T(1,128)} %copy-done.18) | copy-start | bytes 6148
  529.8 16.3 %copy-start.21 = (f32[1,512]{1,0:T(1,128)S(1)}, f32[1,512]{1,0:T(1,128)}, u32[]{:S(2)}) copy-start(f32[1,512]{1,0:T(1,128)} %copy-done.20) | copy-start | bytes 6148
  529.8 16.3 %copy-start.23 = (f32[1,512]{1,0:T(1,128)S(1)}, f32[1,512]{1,0:T(1,128)}, u32[]{:S(2)}) copy-start(f32[1,512]{1,0:T(1,128)} %copy-done.22) | copy-start | bytes 6148
  529.9 16.3 %copy-start.25 = (f32[1,512]{1,0:T(1,128)S(1)}, f32[1,512]{1,0:T(1,128)}, u32[]{:S(2)}) copy-start(f32[1,512]{1,0:T(1,128)} %copy-done.24) | copy-start | bytes 6148
  531.5 14.6 %collective-permute-start.2 = (f32[3,512]{1,0:T(4,128)S(1)}, f32[3,512]{1,0:T(4,128)S(1)}, u32[]{:S(2)}, u32[]{:S(2)}) collective-permute-start(f32[3,512]{1,0:T(4,128)S(1)} %slice.192), channel_id=1, source_target_pairs={{32,0},{64,32},{96,64},{128,96},{160,128},{192,160},{224,192},{256... | collective-permute-start | bytes 18440 | tf_op jit(solution)/shard_map/ppermute | solution.py:16
Sparse Core Ops, SparseCore 0:
  51.2 182.2 all-gather.7
  235.6 186.9 all-gather.5
where the time goes:
time: 569 us; the launch traced here: 567 us
  waiting for transfers between devices  354 us (62%)
  other arithmetic  55.2 us (10%)
  matrix products  38.5 us (7%)
  local copies, waits for them, and re-layouts  38.4 us (7%)
  starting transfers between devices  35.9 us (6%)
  blocking collectives  29.1 us (5%)
  between operations  14.6 us (3%)
    all_gather x2, waiting for transfers between devices, entering(): gathered = jax.tree.map(lambda a: lax.all_gather(a, axis), part)  317 us
    all_gather x1, blocking collectives, entering(): gathered = jax.tree.map(lambda a: lax.all_gather(a, axis), part)  29.1 us
    add x15, other arithmetic, link_states(): decay_late[:, None, None] * state_early + state_late  18.1 us
    ppermute x4, waiting for transfers between devices, shifted(): return lax.ppermute(array, axis, pairs)  16.6 us
    all_to_all x1, starting transfers between devices, per_device(): lax.all_to_all(fan_groups(bc_in, copies), 'tp', split_axis=1, concat_axis...  14.4 us
    all_to_all x1, starting transfers between devices, per_device(): lax.all_to_all(group_terms, 'tp', split_axis=0, concat_axis=1, tiled=True)  11.5 us
    dot_general x4, matrix products, block_pass(): jnp.einsum('ijh,jhp->ihp', mixing * scores[:, :, None], inputs, precision...  11.4 us
  transfers between devices with their start and end apart: 8, of which 7 were waited for; matrix products, arithmetic and copies ran while one was open for 6% of the time, Pallas kernels for 0%

commit v1 on v0

v1 whole, which is shorter than its diff:
```python
import functools

import jax
import jax.numpy as jnp
from jax import lax
from jax.experimental import pallas as pl
from jax.experimental.pallas import tpu as pltpu
from jax.sharding import Mesh, PartitionSpec as P

HEAD_DIM = 64
STATE = 256
CONV = 4
HEADS = 8
BLOCK = 256
ROWS = 512
COLS = HEADS * HEAD_DIM
BLOCKS = ROWS // BLOCK
HALO = 16
META = 128

F32 = jnp.float32
BF16 = jnp.bfloat16
NN = ((1,), (0,))
NT = ((1,), (1,))
TN = ((0,), (0,))
CTX = ("y", "zl")
TP = ("x", "zh", "core")


def mul(a, b, dims):
    return lax.dot_general(a, b, (dims, ((), ())), preferred_element_type=F32)


def split2(a):
    high = a.astype(BF16)
    return high, (a - high.astype(F32)).astype(BF16)


def split3(a):
    high = a.astype(BF16)
    rest = a - high.astype(F32)
    middle = rest.astype(BF16)
    return high, middle, (rest - middle.astype(F32)).astype(BF16)


def dot3(a, b, dims):
    return mul(a[0], b[0], dims) + (mul(a[0], b[1], dims) + mul(a[1], b[0], dims))


def exact_left(ones, b, dims):
    parts = split3(b)
    return mul(ones, parts[0], dims) + (mul(ones, parts[1], dims) + mul(ones, parts[2], dims))


def exact_right(a, ones, dims):
    parts = split3(a)
    return mul(parts[0], ones, dims) + (mul(parts[1], ones, dims) + mul(parts[2], ones, dims))


def expander(rows):
    head = lax.broadcasted_iota(jnp.int32, (rows, COLS), 0)
    col = lax.broadcasted_iota(jnp.int32, (rows, COLS), 1)
    return jnp.where((col >= head * HEAD_DIM) & (col < (head + 1) * HEAD_DIM), 1.0, 0.0).astype(BF16)


def row_col(shape=(BLOCK, BLOCK)):
    return (
        lax.broadcasted_iota(jnp.int32, shape, 0),
        lax.broadcasted_iota(jnp.int32, shape, 1),
    )


def sigmoid(v):
    return 1.0 / (1.0 + jnp.exp(-v))


def conv_silu(buf, prev, rows, taps):
    buf[0:8] = prev[HALO - 8 :].astype(F32)
    buf[8 : 8 + ROWS] = rows[...].astype(F32)
    pre = taps[0:1] * buf[5 : 5 + ROWS]
    for k in range(1, CONV):
        pre = pre + taps[k : k + 1] * buf[5 + k : 5 + k + ROWS]
    gate = sigmoid(pre)
    return pre * gate, gate * (1.0 + pre * (1.0 - gate))


def feature_kernel(x_ref, prev_ref, taps_ref, log_ref, grad_ref,
                   act_ref, slope_ref, fade_ref, grown_ref, cum_ref, cumt_ref, buf):
    act, slope = conv_silu(buf, prev_ref, x_ref, taps_ref)
    act_ref[...] = act
    slope_ref[...] = slope
    row, col = row_col()
    upper = jnp.where(row <= col, 1.0, 0.0).astype(BF16)
    lower = jnp.where(col <= row, 1.0, 0.0).astype(BF16)
    spread = expander(META)
    for b in range(BLOCKS):
        part = slice(b * BLOCK, (b + 1) * BLOCK)
        logs = log_ref[part]
        cum = exact_left(lower, logs, NN)
        cum_ref[part] = cum
        cumt_ref[b] = exact_right(logs, upper, TN)[0:8]
        last = cum[BLOCK - 1 : BLOCK]
        fade_ref[part] = exact_right(jnp.exp(last - cum), spread, NN)
        grown_ref[part] = grad_ref[part].astype(F32) * exact_right(jnp.exp(cum), spread, NN)


def power_scale(rows):
    top = jnp.max(jnp.abs(rows), axis=1, keepdims=True)
    return jnp.clip(14.0 - jnp.ceil(jnp.log2(jnp.maximum(top, 1e-30))), -100.0, 100.0)


def pack_rows(first, second, out, logs=None):
    lane = lax.broadcasted_iota(jnp.int32, (first.shape[0], META), 1)
    up_first = power_scale(first)
    up_second = power_scale(second)
    out[:, 0:COLS] = first * jnp.exp2(up_first)
    out[:, COLS : 2 * COLS] = second * jnp.exp2(up_second)
    meta = jnp.where(lane == 16, up_first, jnp.where(lane == 17, up_second, 0.0))
    if logs is not None:
        meta = jnp.where(lane < 16, logs, meta)
    out[:, 2 * COLS :] = meta


def state_kernel(bc_ref, prev_ref, taps_ref, act_ref, fade_ref, grown_ref, cum_ref,
                 bc_act_ref, slope_ref, early_ref, late_ref, pack_ref, buf):
    act, slope = conv_silu(buf, prev_ref, bc_ref, taps_ref)
    bc_act_ref[...] = act
    slope_ref[...] = slope
    spread = expander(META)
    states, grads, decays = [], [], []
    total = jnp.zeros((1, META), F32)
    for b in range(BLOCKS):
        part = slice(b * BLOCK, (b + 1) * BLOCK)
        keys = split2(act[part, 0:STATE])
        queries = split2(act[part, STATE:])
        states.append(dot3(keys, split2(act_ref[part] * fade_ref[part]), TN))
        grads.append(dot3(queries, split2(grown_ref[part]), TN))
        last = cum_ref[(b + 1) * BLOCK - 1 : (b + 1) * BLOCK]
        total = total + last
        decays.append(exact_right(jnp.broadcast_to(jnp.exp(last), (8, META)), spread, NN)[0:1])
    early_ref[...] = states[0]
    late_ref[...] = grads[1]
    state = decays[1] * states[0] + states[1]
    grad = grads[0] + decays[0] * grads[1]
    high = total.astype(BF16).astype(F32)
    low = total - high
    lane = lax.broadcasted_iota(jnp.int32, (1, META), 1)
    logs = jnp.where(lane < 8, high, pltpu.roll(low, 8, 1))
    pack_rows(state, grad, pack_ref, jnp.where(lane < 16, logs, 0.0))


def scan_kernel(places, got_ref, out_ref):
    piece = STATE // places
    spread = expander(META)
    lane = lax.broadcasted_iota(jnp.int32, (8, META), 1)

    def rows(p):
        return slice(p * piece, (p + 1) * piece)

    decays = []
    for p in range(places):
        meta = got_ref[p * piece : p * piece + 8, 2 * COLS :]
        logs = meta + pltpu.roll(meta, META - 8, 1)
        decay = jnp.where(lane < 8, jnp.exp(jnp.minimum(logs, 0.0)), 0.0)
        decays.append(exact_right(decay, spread, NN)[0:1])

    def part(p, which):
        up = got_ref[rows(p), 2 * COLS + 16 + which : 2 * COLS + 17 + which]
        return got_ref[rows(p), which * COLS : (which + 1) * COLS] * jnp.exp2(-up)

    coming = jnp.zeros((piece, COLS), F32)
    befores = []
    for p in range(places):
        befores.append(coming)
        coming = decays[p] * coming + part(p, 0)
    going = jnp.zeros((piece, COLS), F32)
    for p in reversed(range(places)):
        pack_rows(befores[p], going, out_ref.at[rows(p)])
        going = decays[p] * going + part(p, 1)


def block_kernel(act_ref, grad_ref, bc_ref, cum_ref, cumt_ref, dx_ref, dbc_ref, dlog_ref):
    row, col = row_col()
    causal = row <= col
    later = jnp.where(col >= row, 1.0, 0.0).astype(BF16)
    keys = split2(bc_ref[:, 0:STATE])
    queries = split2(bc_ref[:, STATE:])
    scores = dot3(keys, queries, NT)
    total = jnp.zeros((BLOCK, BLOCK), F32)
    across, down = [], []
    for h in range(HEADS):
        cols = slice(h * HEAD_DIM, (h + 1) * HEAD_DIM)
        gap = cumt_ref[0, h : h + 1, :] - cum_ref[:, h : h + 1]
        mixing = jnp.where(causal, jnp.exp(jnp.where(causal, gap, 0.0)), 0.0)
        grads = grad_ref[:, cols]
        values = split2(act_ref[:, cols])
        pairs = mixing * (mul(values[0], grads, NT) + mul(values[1], grads, NT))
        total = total + pairs
        weights = pairs * scores
        across.append(jnp.sum(weights, axis=0, keepdims=True))
        down.append(jnp.sum(weights, axis=1, keepdims=True))
        mixed = split2(mixing * scores)
        dx_ref[:, cols] = mul(mixed[0], grads, NN) + mul(mixed[1], grads, NN)
    pairs = split2(total)
    dbc_ref[:, 0:STATE] = dot3(pairs, queries, NN)
    dbc_ref[:, STATE:] = dot3(pairs, keys, TN)
    dlog_ref[...] = exact_left(later, jnp.concatenate(across, axis=0), NT) - exact_left(
        later, jnp.concatenate(down, axis=1), NN
    )


def carry_kernel(got_ref, early_ref, late_ref, act_ref, xslope_ref, fade_ref, grown_ref, cum_ref,
                 bc_ref, bslope_ref, dx_ref, dbc_ref, dlog_ref,
                 gx_ref, gbc_ref, glog_ref):
    row, col = row_col()
    later = jnp.where(col >= row, 1.0, 0.0).astype(BF16)
    before = jnp.where(col < row, 1.0, 0.0).astype(BF16)
    spread = expander(META)
    coming = got_ref[:, 0:COLS] * jnp.exp2(-got_ref[:, 2 * COLS + 16 : 2 * COLS + 17])
    going = got_ref[:, COLS : 2 * COLS] * jnp.exp2(-got_ref[:, 2 * COLS + 17 : 2 * COLS + 18])
    decays = []
    for b in range(BLOCKS):
        last = cum_ref[(b + 1) * BLOCK - 1 : (b + 1) * BLOCK]
        decays.append(exact_right(jnp.broadcast_to(jnp.exp(last), (8, META)), spread, NN)[0:1])
    comings = [coming, decays[0] * coming + early_ref[...]]
    goings = [decays[1] * going + late_ref[...], going]
    for b in range(BLOCKS):
        part = slice(b * BLOCK, (b + 1) * BLOCK)
        enter = split2(comings[b])
        leave = split2(goings[b])
        keys = split2(bc_ref[part, 0:STATE])
        queries = split2(bc_ref[part, STATE:])
        fade = fade_ref[part]
        grown = grown_ref[part]
        faded = act_ref[part] * fade
        reads = dot3(queries, enter, NN)
        pulls = dot3(keys, leave, NN)
        gx_ref[part] = (dx_ref[part] + fade * pulls) * xslope_ref[part]
        faded2 = split2(faded)
        grown2 = split2(grown)
        gbc_ref[part, 0:STATE] = (dbc_ref[part, 0:STATE] + dot3(faded2, leave, NT)) * bslope_ref[part, 0:STATE]
        gbc_ref[part, STATE:] = (dbc_ref[part, STATE:] + dot3(grown2, enter, NT)) * bslope_ref[part, STATE:]
        across = exact_right(grown * reads, spread, NT)
        down = exact_right(faded * pulls, spread, NT)
        both = jnp.sum(comings[b] * goings[b], axis=0, keepdims=True) * decays[b]
        both = exact_right(jnp.broadcast_to(both, (8, COLS)), spread, NT)[0:1]
        found = exact_left(later, across, NN) + exact_left(before, down, NN) + both
        glog_ref[part] = dlog_ref[part] + found[:, 0:HEADS]


def back_conv(buf, rows, halo, taps):
    buf[0:ROWS] = rows[...]
    buf[ROWS : ROWS + 8] = halo[...]
    out = taps[0:1] * buf[3 : 3 + ROWS]
    for k in range(1, CONV):
        out = out + taps[k : k + 1] * buf[3 - k : 3 - k + ROWS]
    return out


def grad_bc_kernel(rows_ref, halo_ref, taps_ref, out_ref, buf):
    out_ref[...] = back_conv(buf, rows_ref, halo_ref, taps_ref)


def grad_x_kernel(rows_ref, halo_ref, taps_ref, out_ref, buf):
    out_ref[...] = back_conv(buf, rows_ref, halo_ref, taps_ref).astype(BF16)


def call(kernel, outs, scratch=(), flops=1 << 26, size=1 << 22, **more):
    return pl.pallas_call(
        kernel,
        out_shape=[jax.ShapeDtypeStruct(shape, dtype) for shape, dtype in outs],
        scratch_shapes=list(scratch),
        compiler_params=pltpu.CompilerParams(vmem_limit_bytes=48 * 2**20),
        cost_estimate=pl.CostEstimate(flops=flops, bytes_accessed=size, transcendentals=0),
        **more,
    )


def shifted(array, by):
    devices = lax.axis_size(CTX)
    pairs = [(i, i + by) for i in range(devices) if 0 <= i + by < devices]
    return lax.ppermute(array, CTX, pairs)


def per_device(x_in, bc_in, conv_x, conv_bc, log_decay, grad_y):
    core = lax.axis_index("core")
    owners = lax.axis_size(("x", "zh"))
    places = lax.axis_size(CTX)
    groups = bc_in.shape[1] // (2 * STATE)
    own = bc_in.shape[0]
    fan = owners // groups
    group = lax.axis_index(("x", "zh")) // fan
    taps_bc = lax.dynamic_slice_in_dim(conv_bc, group * (2 * STATE), 2 * STATE, 1)
    swap = [(0, 1), (1, 0)]

    spread = jnp.broadcast_to(
        bc_in.reshape(own, groups, 1, 2 * STATE).transpose(1, 2, 0, 3), (groups, fan, own, 2 * STATE)
    ).reshape(owners, own, 2 * STATE)
    mine = lax.all_to_all(spread, ("x", "zh"), 0, 0, tiled=True)
    theirs = lax.ppermute(mine, "core", swap)
    bc_rows = jnp.where(
        core == 0, jnp.stack([mine, theirs], 1), jnp.stack([theirs, mine], 1)
    ).reshape(ROWS, 2 * STATE)

    x_prev = shifted(x_in[ROWS - HALO :], 1)
    bc_prev = shifted(bc_rows[ROWS - HALO :], 1)
    logs = jnp.pad(log_decay, ((0, 0), (0, META - HEADS)))
    wide = (ROWS, COLS)
    act, xslope, fade, grown, cum, cumt = call(
        feature_kernel,
        [(wide, F32)] * 4 + [((ROWS, META), F32), ((BLOCKS, 8, BLOCK), F32)],
        [pltpu.VMEM((ROWS + 8, COLS), F32)],
    )(x_in, x_prev, conv_x, logs, grad_y)
    packed = (STATE, 2 * COLS + META)
    bc_act, bslope, early, late, sent = call(
        state_kernel,
        [((ROWS, 2 * STATE), F32)] * 2 + [((STATE, COLS), F32)] * 2 + [(packed, F32)],
        [pltpu.VMEM((ROWS + 8, COLS), F32)],
    )(bc_rows, bc_prev, taps_bc, act, fade, grown, cum)
    got = lax.all_to_all(sent.astype(jnp.float16), CTX, 0, 0, tiled=True)

    def rows_of(width):
        return pl.BlockSpec((BLOCK, width), lambda b: (b, 0))

    dx, dbc, dlog = call(
        block_kernel,
        [(wide, F32), ((ROWS, 2 * STATE), F32), ((ROWS, HEADS), F32)],
        grid=(BLOCKS,),
        in_specs=[
            rows_of(COLS), rows_of(COLS), rows_of(2 * STATE), rows_of(META),
            pl.BlockSpec((1, 8, BLOCK), lambda b: (b, 0, 0)),
        ],
        out_specs=[rows_of(COLS), rows_of(2 * STATE), rows_of(HEADS)],
    )(act, grad_y, bc_act, cum, cumt)

    (back,) = call(functools.partial(scan_kernel, places), [(packed, F32)])(got.astype(F32))
    carried = lax.all_to_all(back.astype(jnp.float16), CTX, 0, 0, tiled=True).astype(F32)

    gx, gbc, glog = call(
        carry_kernel, [(wide, F32), ((ROWS, 2 * STATE), F32), ((ROWS, HEADS), F32)]
    )(carried, early, late, act, xslope, fade, grown, cum, bc_act, bslope, dx, dbc, dlog)

    bc_later = shifted(gbc[:8], -1)
    x_later = shifted(gx[:8], -1)
    (terms,) = call(
        grad_bc_kernel, [((ROWS, 2 * STATE), F32)], [pltpu.VMEM((ROWS + 8, 2 * STATE), F32)]
    )(gbc, bc_later, taps_bc)
    terms = terms.reshape(owners, 2, own, 2 * STATE)
    keep = lax.dynamic_index_in_dim(terms, core, 1, False)
    give = lax.dynamic_index_in_dim(terms, 1 - core, 1, False)
    summed = keep + lax.ppermute(give, "core", swap)
    parts = lax.all_to_all(summed, ("x", "zh"), 0, 0, tiled=True)
    grad_bc = jnp.sum(parts.reshape(groups, fan, own, 2 * STATE), axis=1)
    grad_bc = grad_bc.transpose(1, 0, 2).reshape(own, groups * 2 * STATE)
    (grad_x,) = call(
        grad_x_kernel, [(wide, BF16)], [pltpu.VMEM((ROWS + 8, COLS), F32)]
    )(gx, x_later, conv_x)
    return grad_x, grad_bc, glog


def solution(mesh):
    fine = Mesh(mesh.devices.reshape(8, 2, 4, 4, 2), CTX + TP)
    return jax.shard_map(
        per_device,
        mesh=fine,
        in_specs=(P(CTX, TP), P(CTX + TP, None), P(None, TP), P(), P(CTX, TP), P(CTX, TP)),
        out_specs=(P(CTX, TP), P(CTX + TP, None), P(CTX, TP)),
        check_vma=False,
    )
```

time: 569 us -> 151 us (0.27)
  waiting for transfers between devices: 354 us -> 27.3 us
  other arithmetic: 55.2 us -> 6.43 us
  matrix products: 38.5 us -> 0 us
  local copies, waits for them, and re-layouts: 38.4 us -> 12.8 us
  Pallas kernels: 0 us -> 23.7 us
  blocking collectives: 29.1 us -> 49.9 us
  between operations: 14.6 us -> 1.03 us
  starting transfers between devices: 35.9 us -> 28.6 us
    all_gather x2 -> x0, waiting for transfers between devices: 317 us -> none  [entering(): gathered = jax.tree.map(lambda a: lax.all_gather(a, axis), part)]
    all_to_all x0 -> x2, blocking collectives: none -> 49.9 us  [the longest x1 25 us: per_device(): got = lax.all_to_all(sent.astype(jnp.float16), CTX, 0, 0, tiled=True)]
    dot_general x24 -> x0, matrix products: 38.5 us -> none  [the longest x4 11.4 us: block_pass(): jnp.einsum('ijh,jhp->ihp', mixing * scores[:, :, None], inputs, precision...]
    all_gather x1 -> x0, blocking collectives: 29.1 us -> none  [entering(): gathered = jax.tree.map(lambda a: lax.all_gather(a, axis), part)]
    pallas_call x0 -> x7, Pallas kernels: none -> 23.7 us  [the longest x1 7.08 us: per_device(): call(carry_kernel, [(wide, F32), ((ROWS, 2 * STATE), F32), ((ROWS, HEADS)...]
    add x16 -> x1, other arithmetic: 19.6 us -> 0.87 us  [per_device(): summed = keep + lax.ppermute(give, 'core', swap)]
    all_to_all x2, starting transfers between devices: 25.9 us -> 8 us  [the longest x1 4.42 us: per_device(): lax.all_to_all(back.astype(jnp.float16), CTX, 0, 0, tiled=True).astype(F32)]
    unnamed x44 -> x51, local copies, waits for them, and re-layouts: 0.42 us -> 11.2 us
  transfers between devices with their start and end apart: 8 -> 8, of which waited for: 7 -> 5; matrix products, arithmetic and copies ran while one was open for 6% -> 1% of each run, Pallas kernels for 0% -> 6%
where the time goes in v1:
time: 151 us; the launch traced here: 150 us
  blocking collectives  49.9 us (33%)
  starting transfers between devices  28.6 us (19%)
  waiting for transfers between devices  27.3 us (18%)
  Pallas kernels  23.7 us (16%)
  local copies, waits for them, and re-layouts  12.8 us (8%)
  other arithmetic  6.43 us (4%)
    all_to_all x1, blocking collectives, per_device(): got = lax.all_to_all(sent.astype(jnp.float16), CTX, 0, 0, tiled=True)  25 us
    all_to_all x1, blocking collectives, per_device(): mine = lax.all_to_all(spread, ('x', 'zh'), 0, 0, tiled=True)  24.9 us
    ppermute x4, waiting for transfers between devices, shifted(): return lax.ppermute(array, CTX, pairs)  14.4 us
    unnamed x51, local copies, waits for them, and re-layouts  11.2 us
    all_to_all x1, waiting for transfers between devices, per_device(): lax.all_to_all(back.astype(jnp.float16), CTX, 0, 0, tiled=True).astype(F32)  9.34 us
    ppermute x4, starting transfers between devices, shifted(): return lax.ppermute(array, CTX, pairs)  8.84 us
    pallas_call x1, Pallas kernels, per_device(): call(carry_kernel, [(wide, F32), ((ROWS, 2 * STATE), F32), ((ROWS, HEADS)...  7.08 us
    ppermute x1, starting transfers between devices, per_device(): summed = keep + lax.ppermute(give, 'core', swap)  6.96 us
  transfers between devices with their start and end apart: 8, of which 5 were waited for; matrix products, arithmetic and copies ran while one was open for 1% of the time, Pallas kernels for 6%

profile of v1, /device:TPU:1, one launch (start us, length us, event | category | flops | bytes accessed | tf_op | source)
XLA Modules:
  0.0 149.8 jit_solution(17175581994570095111)
XLA Ops:
  0.6 0.0 copy-start
  0.6 1.0 copy.20
  1.6 0.0 copy-start.23
  1.7 0.0 copy-start.6
  1.7 0.0 copy-start.22
  1.7 24.9 %all_to_all.28 = bf16[16,16,512]{2,1,0:T(8,128)(2,1)S(1)} all-to-all(bf16[16,16,512]{2,1,0:T(8,128)(2,1)S(1)} %bitcast.37), channel_id=1, replica_groups=mesh['y'=8,'zl'=2,'x'=4,'zh'=4,'core'=2] {'x','zh'}, dimensions={0} | all-to-all | bytes 524288 | tf_op jit(solution)/shard_map/all_to_all | solution.py:299
  26.6 4.8 %collective-permute-start = (bf16[16,16,512]{2,1,0:T(8,128)(2,1)S(1)}, bf16[16,16,512]{2,1,0:T(8,128)(2,1)S(1)}, u32[]{:S(2)}, u32[]{:S(2)}) collective-permute-start(bf16[16,16,512]{2,1,0:T(8,128)(2,1)S(1)} %all_to_all.28), channel_id=1, source_target_pairs={{0,1},{1,0},{2,3},{3,2},{4,5},{5,4},{6,7},{7,6},{8,9},{9,8},{10,11... | collective-permute-start | bytes 786440 | tf_op jit(solution)/shard_map/ppermute | solution.py:300
  31.4 0.7 slice.13
  32.1 2.9 %collective-permute-start.2 = (bf16[16,512]{1,0:T(8,128)(2,1)S(1)}, bf16[16,512]{1,0:T(8,128)(2,1)S(1)}, u32[]{:S(2)}, u32[]{:S(2)}) collective-permute-start(bf16[16,512]{1,0:T(8,128)(2,1)S(1)} %slice.13), channel_id=1, source_target_pairs={{0,32},{32,64},{64,96},{96,128},{128,160},{160,192},{192,224},{224... | collective-permute-start | bytes 49160 | tf_op jit(solution)/shard_map/ppermute | solution.py:282
  35.0 0.0 collective-permute-done
  35.0 0.1 maximum_select_fusion
  35.1 0.0 copy-start.4
  35.1 0.8 copy-done.4
  35.9 3.4 %collective-permute-start.1 = (bf16[16,512]{1,0:T(8,128)(2,1)S(1)}, bf16[16,512]{1,0:T(8,128)(2,1)S(1)}, u32[]{:S(2)}, u32[]{:S(2)}) collective-permute-start(bf16[16,512]{1,0:T(8,128)(2,1)S(1)} %slice.16), channel_id=1, source_target_pairs={{0,32},{32,64},{64,96},{96,128},{128,160},{160,192},{192,224},{224... | collective-permute-start | bytes 49160 | tf_op jit(solution)/shard_map/ppermute | solution.py:282
  39.3 0.0 copy-done
  39.3 0.0 copy-done.23
  39.3 0.1 copy.16
  39.5 0.0 copy-start.5
  39.5 0.0 collective-permute-done.2.prev_ref
  39.5 0.0 copy-done.6
  39.5 0.0 copy-done.22
  39.5 0.0 copy-start.13
  39.5 1.1 copy-done.13
  40.6 3.1 %shard_map.85 = (f32[512,512]{1,0:T(8,128)S(1)}, f32[512,512]{1,0:T(8,128)S(1)}, f32[512,512]{1,0:T(8,128)S(1)}, f32[512,512]{1,0:T(8,128)S(1)}, f32[512,128]{1,0:T(8,128)S(1)}, /*index=5*/f32[2,8,256]{2,1,0:T(8,128)S(1)}) custom-call(bf16[512,512]{1,0:T(8,128)(2,1)S(1)} %copy-done.13, bf16[16,512]{1,0:T(8,128)(2,1)S(1)} %collective-permute-done.2.prev_ref, ...), custom_call_target="tpu_custom_call" | custom-call | flops 67108864 | bytes 4194304 | tf_op jit(solution)/shard_map/pallas_call | solution.py:309
  43.8 0.0 copy-start.2
  43.8 1.0 copy-done.2
  44.7 1.0 copy-done.8
  45.7 0.0 collective-permute-done.1.prev_ref
  45.7 0.0 copy-done.5
  45.7 5.2 %shard_map.86 = (f32[512,512]{1,0:T(8,128)S(1)}, f32[512,512]{1,0:T(8,128)S(1)}, f32[256,512]{1,0:T(8,128)S(1)}, f32[256,512]{1,0:T(8,128)S(1)}, f32[256,1152]{1,0:T(8,128)}) custom-call(bf16[512,512]{1,0:T(8,128)(2,1)S(1)} %bitcast.33, bf16[16,512]{1,0:T(8,128)(2,1)S(1)} %collective-permute-done.1.prev_ref, ...), custom_call_target="tpu_custom_call" | custom-call | flops 67108864 | bytes 4194304 | tf_op jit(solution)/shard_map/pallas_call | solution.py:315
  50.9 0.8 copy-done.16
  51.7 2.2 %convert_element_type.18 = f16[256,1152]{1,0:T(8,128)(2,1)S(1)} convert(f32[256,1152]{1,0:T(8,128)} %get-tuple-element.24) | non-fusion elementwise | flops 294912 | bytes 1769472 | tf_op jit(solution)/shard_map/convert_element_type | solution.py:320
  53.9 25.0 %all_to_all.29 = f16[16,16,1152]{2,1,0:T(8,128)(2,1)S(1)} all-to-all(f16[16,16,1152]{2,1,0:T(8,128)(2,1)S(1)} %bitcast.35), channel_id=1, replica_groups=mesh['y'=8,'zl'=2,'x'=4,'zh'=4,'core'=2] {'y','zl'}, dimensions={0} | all-to-all | bytes 1179648 | tf_op jit(solution)/shard_map/all_to_all | solution.py:320
  79.0 0.0 copy-done.10
  79.0 0.1 bitcast_convert_fusion.1.got_ref
  79.1 1.2 shard_map.87
  80.3 0.0 copy-start.7
  80.3 0.9 convert_element_type.21
  81.2 4.4 %all-to-all-start.2 = ((f16[16,16,1152]{2,1,0:T(8,128)(2,1)}), f16[16,16,1152]{2,1,0:T(8,128)(2,1)}, u32[]{:S(2)}, u32[]{:S(2)}) async-start(f16[16,16,1152]{2,1,0:T(8,128)(2,1)} %bitcast.34), calls=%async_computation.2 | async-start | bytes 1179648 | tf_op jit(solution)/shard_map/all_to_all | solution.py:337
  85.6 4.4 %shard_map.88 = (f32[512,512]{1,0:T(8,128)S(1)}, f32[512,512]{1,0:T(8,128)S(1)}, f32[512,8]{1,0:T(8,128)S(1)}) custom-call(f32[512,512]{1,0:T(8,128)S(1)} %get-tuple-element.20.act_ref, bf16[512,512]{1,0:T(8,128)(2,1)S(1)} %copy-done.7, f32[512,512]{1,0:T(8,128)S(1)} %get-tuple-element.28.bc_ref, f32[512,128]{1,0:T(8,128)S(1)} %get-tuple-element.23.cum_ref, ...), custom_call_target="tpu_custom_call" | custom-call | flops 67108864 | bytes 4194304 | tf_op jit(solution)/shard_map/pallas_call | solution.py:325
  90.0 1.0 copy-done.11
  91.0 1.1 copy-done.12
  92.1 9.3 %all-to-all-done.2 = f16[16,16,1152]{2,1,0:T(8,128)(2,1)} async-done(((f16[16,16,1152]{2,1,0:T(8,128)(2,1)}), f16[16,16,1152]{2,1,0:T(8,128)(2,1)}, u32[]{:S(2)}, u32[]{:S(2)}) %all-to-all-start.2) | async-done | bytes 589856 | tf_op jit(solution)/shard_map/all_to_all | solution.py:337
  101.4 2.3 %bitcast_convert_fusion.got_ref = f32[256,1152]{1,0:T(8,128)} fusion(f16[16,16,1152]{2,1,0:T(8,128)(2,1)} %all-to-all-done.2), kind=kLoop, calls=%fused_computation | loop fusion | flops 294912 | bytes 1769472 | tf_op jit(solution)/shard_map/convert_element_type | solution.py:337
  103.7 0.0 copy-done.18
  103.7 1.0 copy-done.17
  104.8 0.9 copy-done.19
  105.7 7.1 %shard_map.89 = (f32[512,512]{1,0:T(8,128)S(1)}, f32[512,512]{1,0:T(8,128)S(1)}, f32[512,8]{1,0:T(8,128)S(1)}) custom-call(f32[256,1152]{1,0:T(8,128)} %bitcast_convert_fusion.got_ref, f32[256,512]{1,0:T(8,128)S(1)} %copy-done.15, f32[256,512]{1,0:T(8,128)S(1)} %copy-done.17, f32[512,512]{1,0:T(8,128)S(1)} %get-tuple-element.20.act_ref, ...), custom_call_target="tpu_custom_call" | custom-call | flops 67108864 | bytes 4194304 | tf_op jit(solution)/shard_map/pallas_call | solution.py:339
  112.8 0.0 copy-start.20
  112.8 0.7 copy-done.20
  113.5 1.3 collective-permute-start.4
  114.8 3.2 %collective-permute-done.4.halo_ref = f32[8,512]{1,0:T(8,128)S(1)} collective-permute-done((f32[8,512]{1,0:T(8,128)S(1)}, f32[8,512]{1,0:T(8,128)S(1)}, u32[]{:S(2)}, u32[]{:S(2)}) %collective-permute-start.4) | collective-permute-done | bytes 16416 | tf_op jit(solution)/shard_map/ppermute | solution.py:282
  118.0 0.9 shard_map.91
  119.0 7.0 %collective-permute-start.5 = (f32[16,16,512]{2,1,0:T(8,128)S(1)}, f32[16,16,512]{2,1,0:T(8,128)S(1)}, u32[]{:S(2)}, u32[]{:S(2)}) collective-permute-start(f32[16,16,512]{2,1,0:T(8,128)S(1)} %dynamic-slice_bitcast_fusion), channel_id=1, source_target_pairs={{0,1},{1,0},{2,3},{3,2},{4,5},{5,4},{6,7},{7,6},{8,9},{9,8},{10,11... | collective-permute-start | bytes 1572872 | tf_op jit(solution)/shard_map/ppermute | solution.py:351
  126.0 0.0 copy-start.21
  126.0 1.5 %collective-permute-done.5 = f32[16,16,512]{2,1,0:T(8,128)S(1)} collective-permute-done((f32[16,16,512]{2,1,0:T(8,128)S(1)}, f32[16,16,512]{2,1,0:T(8,128)S(1)}, u32[]{:S(2)}, u32[]{:S(2)}) %collective-permute-start.5) | collective-permute-done | bytes 524320 | tf_op jit(solution)/shard_map/ppermute | solution.py:351
  127.5 0.9 bitcast_add_fusion
  128.3 3.6 %all-to-all-start.3 = ((f32[16,16,512]{2,1,0:T(8,128)}), f32[16,16,512]{2,1,0:T(8,128)S(1)}, u32[]{:S(2)}, u32[]{:S(2)}) async-start(f32[16,16,512]{2,1,0:T(8,128)} %bitcast_add_fusion), calls=%async_computation.3 | async-start | bytes 1048576 | tf_op jit(solution)/shard_map/all_to_all | solution.py:352
  131.9 1.3 collective-permute-start.3
  133.2 0.7 copy.18
  133.9 11.2 %collective-permute-done.3.halo_ref = f32[8,512]{1,0:T(8,128)S(1)} collective-permute-done((f32[8,512]{1,0:T(8,128)S(1)}, f32[8,512]{1,0:T(8,128)S(1)}, u32[]{:S(2)}, u32[]{:S(2)}) %collective-permute-start.3) | collective-permute-done | bytes 16416 | tf_op jit(solution)/shard_map/ppermute | solution.py:282
  145.2 1.8 %shard_map.90 = bf16[512,512]{1,0:T(8,128)(2,1)} custom-call(f32[512,512]{1,0:T(8,128)S(1)} %get-tuple-element.34.rows_ref, f32[8,512]{1,0:T(8,128)S(1)} %collective-permute-done.3.halo_ref, f32[4,512]{1,0:T(4,128)S(1)} %copy-done.22), custom_call_target="tpu_custom_call" | custom-call | flops 67108864 | bytes 4194304 | tf_op jit(solution)/shard_map/pallas_call | solution.py:355
  147.0 2.1 %all-to-all-done.3 = f32[16,16,512]{2,1,0:T(8,128)S(1)} async-done(((f32[16,16,512]{2,1,0:T(8,128)}), f32[16,16,512]{2,1,0:T(8,128)S(1)}, u32[]{:S(2)}, u32[]{:S(2)}) %all-to-all-start.3) | async-done | bytes 524320 | tf_op jit(solution)/shard_map/all_to_all | solution.py:352
  149.1 0.7 copy.19
  (29 shorter events, 0.2 us)
Async XLA Ops:
  0.6 38.7 %copy-start = (f32[4,4096]{1,0:T(4,128)S(1)}, f32[4,4096]{1,0:T(4,128)}, u32[]{:S(2)}) copy-start(f32[4,4096]{1,0:T(4,128)} %param.9) | copy-start | bytes 196612
  1.6 37.7 %copy-start.23 = (f32[512,8]{0,1:T(8,128)S(1)}, f32[512,8]{0,1:T(8,128)}, u32[]{:S(2)}) copy-start(f32[512,8]{0,1:T(8,128)} %param.10) | copy-start | bytes 49156
  1.7 37.8 %copy-start.6 = (bf16[512,512]{1,0:T(8,128)(2,1)S(1)}, bf16[512,512]{1,0:T(8,128)(2,1)}, u32[]{:S(2)}) copy-start(bf16[512,512]{1,0:T(8,128)(2,1)} %grad_ref.3) | copy-start | bytes 1572868
  1.7 37.8 %copy-start.22 = (f32[4,512]{1,0:T(4,128)S(1)}, f32[4,512]{1,0:T(4,128)}, u32[]{:S(2)}) copy-start(f32[4,512]{1,0:T(4,128)} %taps_ref.3) | copy-start | bytes 24580
  26.6 8.4 %collective-permute-start = (bf16[16,16,512]{2,1,0:T(8,128)(2,1)S(1)}, bf16[16,16,512]{2,1,0:T(8,128)(2,1)S(1)}, u32[]{:S(2)}, u32[]{:S(2)}) collective-permute-start(bf16[16,16,512]{2,1,0:T(8,128)(2,1)S(1)} %all_to_all.28), channel_id=1, source_target_pairs={{0,1},{1,0},{2,3},{3,2},{4,5},{5,4},{6,7},{7,6},{8,9},{9,8},{10,11... | collective-permute-start | bytes 786440 | tf_op jit(solution)/shard_map/ppermute | solution.py:300
  32.1 7.4 %collective-permute-start.2 = (bf16[16,512]{1,0:T(8,128)(2,1)S(1)}, bf16[16,512]{1,0:T(8,128)(2,1)S(1)}, u32[]{:S(2)}, u32[]{:S(2)}) collective-permute-start(bf16[16,512]{1,0:T(8,128)(2,1)S(1)} %slice.13), channel_id=1, source_target_pairs={{0,32},{32,64},{64,96},{96,128},{128,160},{160,192},{192,224},{224... | collective-permute-start | bytes 49160 | tf_op jit(solution)/shard_map/ppermute | solution.py:282
  35.1 0.8 copy-start.4
  35.9 9.9 %collective-permute-start.1 = (bf16[16,512]{1,0:T(8,128)(2,1)S(1)}, bf16[16,512]{1,0:T(8,128)(2,1)S(1)}, u32[]{:S(2)}, u32[]{:S(2)}) collective-permute-start(bf16[16,512]{1,0:T(8,128)(2,1)S(1)} %slice.16), channel_id=1, source_target_pairs={{0,32},{32,64},{64,96},{96,128},{128,160},{160,192},{192,224},{224... | collective-permute-start | bytes 49160 | tf_op jit(solution)/shard_map/ppermute | solution.py:282
  39.5 6.3 %copy-start.5 = (bf16[16,2,16,512]{3,2,1,0:T(8,128)(2,1)S(1)}, bf16[16,2,16,512]{3,2,1,0:T(8,128)(2,1)}, u32[]{:S(2)}) copy-start(bf16[16,2,16,512]{3,2,1,0:T(8,128)(2,1)} %copy-done.4) | copy-start | bytes 1572868
  39.5 1.1 copy-start.13
  43.8 1.0 copy-start.2
  44.7 1.0 copy-start.8
  45.7 5.2 %copy-start.1 = (f32[512,512]{1,0:T(8,128)}, f32[512,512]{1,0:T(8,128)S(1)}, u32[]{:S(2)}) copy-start(f32[512,512]{1,0:T(8,128)S(1)} %get-tuple-element.21.fade_ref) | copy-start | bytes 3145732
  50.9 0.8 copy-start.16
  51.7 27.2 %copy-start.10 = (f32[512,512]{1,0:T(8,128)}, f32[512,512]{1,0:T(8,128)S(1)}, u32[]{:S(2)}) copy-start(f32[512,512]{1,0:T(8,128)S(1)} %get-tuple-element.29.bslope_ref) | copy-start | bytes 3145732
  51.7 27.2 %copy-start.14 = (f32[256,512]{1,0:T(8,128)}, f32[256,512]{1,0:T(8,128)S(1)}, u32[]{:S(2)}) copy-start(f32[256,512]{1,0:T(8,128)S(1)} %get-tuple-element.25.early_ref) | copy-start | bytes 1572868
  51.7 33.9 %copy-start.3 = (f32[512,512]{1,0:T(8,128)}, f32[512,512]{1,0:T(8,128)S(1)}, u32[]{:S(2)}) copy-start(f32[512,512]{1,0:T(8,128)S(1)} %get-tuple-element.28.bc_ref) | copy-start | bytes 3145732
  80.3 5.3 %copy-start.7 = (bf16[512,512]{1,0:T(8,128)(2,1)S(1)}, bf16[512,512]{1,0:T(8,128)(2,1)}, u32[]{:S(2)}) copy-start(bf16[512,512]{1,0:T(8,128)(2,1)} %grad_ref.3) | copy-start | bytes 1572868
  81.2 20.3 %all-to-all-start.2 = ((f16[16,16,1152]{2,1,0:T(8,128)(2,1)}), f16[16,16,1152]{2,1,0:T(8,128)(2,1)}, u32[]{:S(2)}, u32[]{:S(2)}) async-start(f16[16,16,1152]{2,1,0:T(8,128)(2,1)} %bitcast.34), calls=%async_computation.2 | async-start | bytes 1179648 | tf_op jit(solution)/shard_map/all_to_all | solution.py:337
  90.0 1.0 copy-start.11
  91.0 1.1 copy-start.12
  92.1 11.6 %copy-start.18 = (f32[512,8]{1,0:T(8,128)}, f32[512,8]{1,0:T(8,128)S(1)}, u32[]{:S(2)}) copy-start(f32[512,8]{1,0:T(8,128)S(1)} %get-tuple-element.33.dlog_ref) | copy-start | bytes 49156
  101.4 2.3 %copy-start.9 = (f32[512,512]{1,0:T(8,128)S(1)}, f32[512,512]{1,0:T(8,128)}, u32[]{:S(2)}) copy-start(f32[512,512]{1,0:T(8,128)} %copy-done.8) | copy-start | bytes 3145732
  101.4 2.3 %copy-start.15 = (f32[256,512]{1,0:T(8,128)S(1)}, f32[256,512]{1,0:T(8,128)}, u32[]{:S(2)}) copy-start(f32[256,512]{1,0:T(8,128)} %copy-done.14) | copy-start | bytes 1572868
  103.7 1.0 copy-start.17
  104.8 0.9 copy-start.19
  112.8 0.7 copy-start.20
  113.5 4.5 %collective-permute-start.4 = (f32[8,512]{1,0:T(8,128)S(1)}, f32[8,512]{1,0:T(8,128)S(1)}, u32[]{:S(2)}, u32[]{:S(2)}) collective-permute-start(f32[8,512]{1,0:T(8,128)S(1)} %slice.15), channel_id=1, source_target_pairs={{32,0},{64,32},{96,64},{128,96},{160,128},{192,160},{224,192},{256... | collective-permute-start | bytes 49160 | tf_op jit(solution)/shard_map/ppermute | solution.py:282
  119.0 8.5 %collective-permute-start.5 = (f32[16,16,512]{2,1,0:T(8,128)S(1)}, f32[16,16,512]{2,1,0:T(8,128)S(1)}, u32[]{:S(2)}, u32[]{:S(2)}) collective-permute-start(f32[16,16,512]{2,1,0:T(8,128)S(1)} %dynamic-slice_bitcast_fusion), channel_id=1, source_target_pairs={{0,1},{1,0},{2,3},{3,2},{4,5},{5,4},{6,7},{7,6},{8,9},{9,8},{10,11... | collective-permute-start | bytes 1572872 | tf_op jit(solution)/shard_map/ppermute | solution.py:351
  126.0 7.3 %copy-start.21 = (f32[512,8]{1,0:T(8,128)S(1)}, f32[512,8]{1,0:T(8,128)}, u32[]{:S(2)}) copy-start(f32[512,8]{1,0:T(8,128)} %copy-done.20) | copy-start | bytes 49156
  128.3 20.7 %all-to-all-start.3 = ((f32[16,16,512]{2,1,0:T(8,128)}), f32[16,16,512]{2,1,0:T(8,128)S(1)}, u32[]{:S(2)}, u32[]{:S(2)}) async-start(f32[16,16,512]{2,1,0:T(8,128)} %bitcast_add_fusion), calls=%async_computation.3 | async-start | bytes 1048576 | tf_op jit(solution)/shard_map/all_to_all | solution.py:352
  131.9 13.2 %collective-permute-start.3 = (f32[8,512]{1,0:T(8,128)S(1)}, f32[8,512]{1,0:T(8,128)S(1)}, u32[]{:S(2)}, u32[]{:S(2)}) collective-permute-start(f32[8,512]{1,0:T(8,128)S(1)} %slice.14), channel_id=1, source_target_pairs={{32,0},{64,32},{96,64},{128,96},{160,128},{192,160},{224,192},{256... | collective-permute-start | bytes 49160 | tf_op jit(solution)/shard_map/ppermute | solution.py:282

commit v2 on v1

v2 whole, which is shorter than its diff:
```python
import functools

import jax
import jax.numpy as jnp
from jax import lax
from jax.experimental import pallas as pl
from jax.experimental.pallas import tpu as pltpu
from jax.sharding import Mesh, PartitionSpec as P

HEAD_DIM = 64
STATE = 256
CONV = 4
HEADS = 8
BLOCK = 256
ROWS = 512
COLS = HEADS * HEAD_DIM
BLOCKS = ROWS // BLOCK
HALO = 16
LANES = 128
META_ROWS = 8
STORE = 28

F32 = jnp.float32
BF16 = jnp.bfloat16
NN = ((1,), (0,))
NT = ((1,), (1,))
TN = ((0,), (0,))
CTX = ("y", "zl")
TP = ("x", "zh", "core")


def mul(a, b, dims):
    return lax.dot_general(a, b, (dims, ((), ())), preferred_element_type=F32)


def split2(a):
    high = a.astype(BF16)
    return high, (a - high.astype(F32)).astype(BF16)


def split3(a):
    high = a.astype(BF16)
    rest = a - high.astype(F32)
    middle = rest.astype(BF16)
    return high, middle, (rest - middle.astype(F32)).astype(BF16)


def dot3(a, b, dims):
    return mul(a[0], b[0], dims) + (mul(a[0], b[1], dims) + mul(a[1], b[0], dims))


def exact_left(ones, b, dims):
    parts = split3(b)
    return mul(ones, parts[0], dims) + (mul(ones, parts[1], dims) + mul(ones, parts[2], dims))


def exact_right(a, ones, dims):
    parts = split3(a)
    return mul(parts[0], ones, dims) + (mul(parts[1], ones, dims) + mul(parts[2], ones, dims))


def expander(rows):
    head = lax.broadcasted_iota(jnp.int32, (rows, COLS), 0)
    col = lax.broadcasted_iota(jnp.int32, (rows, COLS), 1)
    return jnp.where((col >= head * HEAD_DIM) & (col < (head + 1) * HEAD_DIM), 1.0, 0.0).astype(BF16)


def row_col(shape=(BLOCK, BLOCK)):
    return (
        lax.broadcasted_iota(jnp.int32, shape, 0),
        lax.broadcasted_iota(jnp.int32, shape, 1),
    )


def begin(sems, *pairs, first=0):
    copies = [pltpu.make_async_copy(a, b, sems.at[first + i]) for i, (a, b) in enumerate(pairs)]
    for copy in copies:
        copy.start()
    return copies


def finish(copies):
    for copy in copies:
        copy.wait()


def sigmoid(v):
    return 1.0 / (1.0 + jnp.exp(-v))


def conv(buf, prev, rows, taps):
    buf[0:8] = prev[HALO - 8 :].astype(F32)
    buf[8 : 8 + ROWS] = rows[...].astype(F32)
    pre = taps[0:1] * buf[5 : 5 + ROWS]
    for k in range(1, CONV):
        pre = pre + taps[k : k + 1] * buf[5 + k : 5 + k + ROWS]
    return pre


def group_conv(buf, prev, gathered, taps):
    cores, pairs, own, _ = gathered.shape
    buf[0:8] = prev[HALO - 8 :].astype(F32)
    for pair in range(pairs):
        for core in range(cores):
            at = 8 + (pair * cores + core) * own
            buf[at : at + own] = gathered[core, pair].astype(F32)
    pre = taps[0:1] * buf[5 : 5 + ROWS]
    for k in range(1, CONV):
        pre = pre + taps[k : k + 1] * buf[5 + k : 5 + k + ROWS]
    return pre


def fan_kernel(rows_hbm, out_ref, sems):
    groups = rows_hbm.shape[1] // (2 * STATE)
    fan = out_ref.shape[0] // groups
    copies = []
    for owner in range(out_ref.shape[0]):
        at = owner // fan * (2 * STATE)
        copies += begin(sems, (rows_hbm.at[:, at : at + 2 * STATE], out_ref.at[owner]), first=owner)
    finish(copies)


def fold_kernel(parts_ref, out_ref):
    groups = out_ref.shape[1] // (2 * STATE)
    fan = parts_ref.shape[0] // groups
    for group in range(groups):
        total = parts_ref[group * fan]
        for one in range(1, fan):
            total = total + parts_ref[group * fan + one]
        out_ref[:, group * 2 * STATE : (group + 1) * 2 * STATE] = total


def widen(values, spread):
    return exact_right(values, spread, NN)


def widen_row(row, spread):
    return widen(jnp.broadcast_to(row, (8, LANES)), spread)[0:1]


def head_sums(values, spread):
    high, low = split2(values)
    return mul(high, spread, NT) + mul(low, spread, NT)


def feature_kernel(x_ref, prev_ref, taps_ref, log_ref, grad_ref,
                   store, xf_hi, xf_lo, ge_hi, ge_lo, cum_ref, cumt_ref, buf, act_ref, slope_ref, sems):
    pre = conv(buf, prev_ref, x_ref, taps_ref)
    gate = sigmoid(pre)
    act = pre * gate
    act_ref[...] = act
    slope_ref[...] = gate * (1.0 + pre * (1.0 - gate))
    leaving = begin(sems, (act_ref, store.at[0]), (slope_ref, store.at[1]))
    row, col = row_col()
    upper = jnp.where(row <= col, 1.0, 0.0).astype(BF16)
    lower = jnp.where(col <= row, 1.0, 0.0).astype(BF16)
    spread = expander(LANES)
    cums = []
    for b in range(BLOCKS):
        part = slice(b * BLOCK, (b + 1) * BLOCK)
        logs = log_ref[:, part]
        padded = jnp.concatenate([logs, jnp.zeros((LANES - HEADS, BLOCK), F32)], axis=0)
        cums.append(exact_left(lower, padded, NT))
        cum_ref[part] = cums[b]
        cumt_ref[b] = exact_right(logs, upper, NN)
    lasts = [cum[BLOCK - 1 : BLOCK] for cum in cums]
    for b in range(BLOCKS):
        part = slice(b * BLOCK, (b + 1) * BLOCK)
        since = cums[b] + sum(lasts[:b], jnp.zeros((1, LANES), F32))
        until = lasts[b] - cums[b] + sum(lasts[b + 1 :], jnp.zeros((1, LANES), F32))
        xf_hi[part], xf_lo[part] = split2(act[part] * widen(jnp.exp(until), spread))
        ge_hi[part], ge_lo[part] = split2(grad_ref[part].astype(F32) * widen(jnp.exp(since), spread))
    finish(leaving)


def chunk_fade(cum_ref, rows, spread):
    parts = []
    for b in range(-(-rows // BLOCK)):
        until = -cum_ref[b * BLOCK : min((b + 1) * BLOCK, rows)]
        for later in range(b, BLOCKS):
            until = until + cum_ref[(later + 1) * BLOCK - 1 : (later + 1) * BLOCK]
        parts.append(widen(jnp.exp(until), spread))
    return parts[0] if len(parts) == 1 else jnp.concatenate(parts, axis=0)


def power_scale(values):
    top = jnp.max(jnp.max(jnp.abs(values), axis=1, keepdims=True), axis=0, keepdims=True)
    return jnp.clip(14.0 - jnp.ceil(jnp.log2(jnp.maximum(top, 1e-30))), -100.0, 100.0)


def pack_piece(first, second, out, place, logs):
    count = first.shape[0]
    start = place * piece_rows(count)
    ups = [power_scale(first), power_scale(second)]
    for which, array in enumerate((first, second)):
        scaled = array * jnp.exp2(ups[which])
        for t in range(COLS // LANES):
            at = start + (which * (COLS // LANES) + t) * count
            out[at : at + count] = scaled[:, t * LANES : (t + 1) * LANES]
    lane = lax.broadcasted_iota(jnp.int32, (META_ROWS, LANES), 1)
    meta = jnp.where(lane == 16, ups[0], jnp.where(lane == 17, ups[1], 0.0))
    out[start + piece_rows(count) - META_ROWS : start + piece_rows(count)] = jnp.where(lane < 16, logs, meta)


def piece_rows(count):
    return 2 * count * (COLS // LANES) + META_ROWS


def unpack_piece(got, place, count, which):
    start = place * piece_rows(count)
    meta = got[start + piece_rows(count) - META_ROWS : start + piece_rows(count)]
    down = jnp.exp2(-meta[0:1, 16 + which : 17 + which])
    first = start + which * (COLS // LANES) * count
    return [got[first + t * count : first + (t + 1) * count] * down for t in range(COLS // LANES)]


def state_kernel(places, bc_ref, prev_ref, taps_ref, xf_hi, xf_lo, ge_hi, ge_lo, cum_ref, pack_ref, buf):
    pre = group_conv(buf, prev_ref, bc_ref, taps_ref)
    act = pre * sigmoid(pre)
    keys = split2(act[:, 0:STATE])
    queries = split2(act[:, STATE:])
    state = dot3(keys, (xf_hi[...], xf_lo[...]), TN)
    grad = dot3(queries, (ge_hi[...], ge_lo[...]), TN)
    total = jnp.zeros((1, LANES), F32)
    for b in range(BLOCKS):
        total = total + cum_ref[(b + 1) * BLOCK - 1 : (b + 1) * BLOCK]
    high = total.astype(BF16).astype(F32)
    lane = lax.broadcasted_iota(jnp.int32, (1, LANES), 1)
    logs = jnp.where(lane < 8, high, pltpu.roll(total - high, 8, 1))
    count = STATE // places
    for p in range(places):
        rows = slice(p * count, (p + 1) * count)
        pack_piece(state[rows], grad[rows], pack_ref, p, logs)


def scan_kernel(places, got_ref, out_ref):
    count = STATE // places
    spread = expander(LANES)
    lane = lax.broadcasted_iota(jnp.int32, (META_ROWS, LANES), 1)
    tiles = COLS // LANES
    decays = []
    for p in range(places):
        end = (p + 1) * piece_rows(count)
        meta = got_ref[end - META_ROWS : end]
        logs = meta + pltpu.roll(meta, LANES - 8, 1)
        decay = jnp.where(lane < 8, jnp.exp(jnp.minimum(logs, 0.0)), 0.0)
        decays.append(widen(decay, spread)[0:1])
    coming = jnp.zeros((count, COLS), F32)
    befores = []
    for p in range(places):
        befores.append(coming)
        coming = decays[p] * coming + jnp.concatenate(unpack_piece(got_ref, p, count, 0), axis=1)
    going = jnp.zeros((count, COLS), F32)
    for p in reversed(range(places)):
        pack_piece(befores[p], going, out_ref, p, 0.0)
        going = decays[p] * going + jnp.concatenate(unpack_piece(got_ref, p, count, 1), axis=1)


def block_kernel(features, grad_ref, bc_ref, prev_ref, taps_ref, cum_ref, cumt_ref, store,
                 act_ref, dx_ref, dbc_ref, slope_ref, bc_act, dlog_ref, bc_hi, bc_lo, buf, sems):
    coming = begin(sems, (features.at[0], act_ref))
    pre = group_conv(buf, prev_ref, bc_ref, taps_ref)
    gate = sigmoid(pre)
    slope_ref[...] = gate * (1.0 + pre * (1.0 - gate))
    bc_act[...] = pre * gate
    leaving = begin(sems, (slope_ref, store.at[2]), (bc_act, store.at[3]), first=1)
    bc_hi[...], bc_lo[...] = split2(bc_act[...])
    finish(coming)
    row, col = row_col()
    causal = row <= col
    later = jnp.where(col >= row, 1.0, 0.0).astype(BF16)
    before = jnp.where(col < row, 1.0, 0.0).astype(BF16)
    spread = expander(LANES)
    for b in range(BLOCKS):
        part = slice(b * BLOCK, (b + 1) * BLOCK)
        keys = (bc_hi[part, 0:STATE], bc_lo[part, 0:STATE])
        queries = (bc_hi[part, STATE:], bc_lo[part, STATE:])
        scores = dot3(keys, queries, NT)
        total = jnp.zeros((BLOCK, BLOCK), F32)
        across, down = [], []
        for h in range(HEADS):
            cols = slice(h * HEAD_DIM, (h + 1) * HEAD_DIM)
            gap = cumt_ref[b, h : h + 1, :] - cum_ref[part, h : h + 1]
            mixing = jnp.where(causal, jnp.exp(jnp.where(causal, gap, 0.0)), 0.0)
            grads = grad_ref[part, cols]
            values = split2(act_ref[part, cols])
            pairs = mixing * (mul(values[0], grads, NT) + mul(values[1], grads, NT))
            total = total + pairs
            weights = pairs * scores
            across.append(jnp.sum(weights, axis=0, keepdims=True))
            down.append(jnp.sum(weights, axis=1, keepdims=True))
            mixed = split2(mixing * scores)
            dx_ref[part, cols] = mul(mixed[0], grads, NN) + mul(mixed[1], grads, NN)
        pairs = split2(total)
        dbc_ref[part, 0:STATE] = dot3(pairs, queries, NN)
        dbc_ref[part, STATE:] = dot3(pairs, keys, TN)
        dlog_ref[part, 0:HEADS] = exact_left(later, jnp.concatenate(across, axis=0), NT) - exact_left(
            later, jnp.concatenate(down, axis=1), NN
        )
    first, second = slice(0, BLOCK), slice(BLOCK, 2 * BLOCK)
    last = cum_ref[BLOCK - 1 : BLOCK]
    fade = widen(jnp.exp(last - cum_ref[first]), spread)
    faded = act_ref[first] * fade
    grown = grad_ref[second].astype(F32) * widen(jnp.exp(cum_ref[second]), spread)
    faded2, grown2 = split2(faded), split2(grown)
    keys = (bc_hi[first, 0:STATE], bc_lo[first, 0:STATE])
    queries = (bc_hi[second, STATE:], bc_lo[second, STATE:])
    scores = split2(dot3(keys, queries, NT))
    pairs = split2(dot3(faded2, grown2, NT))
    dbc_ref[first, 0:STATE] += dot3(pairs, queries, NN)
    dbc_ref[second, STATE:] += dot3(pairs, keys, TN)
    pulls = dot3(scores, grown2, NN)
    reads = dot3(scores, faded2, TN)
    dx_ref[first] += fade * pulls
    dlog_ref[first, 0:HEADS] += exact_left(before, head_sums(faded * pulls, spread), NN)[:, 0:HEADS]
    dlog_ref[second, 0:HEADS] += exact_left(later, head_sums(grown * reads, spread), NN)[:, 0:HEADS]
    leaving += begin(
        sems, (dx_ref, store.at[0]), (dbc_ref, store.at[1]), (dlog_ref, store.at[4, :, 0:LANES]), first=3
    )
    finish(leaving)


def unpack_states(places, got_ref, which, out):
    count = STATE // places
    for p in range(places):
        for t, tile in enumerate(unpack_piece(got_ref, p, count, which)):
            out[p * count : (p + 1) * count, t * LANES : (t + 1) * LANES] = tile


def open_kernel(places, got_ref, xf_hi, xf_lo, ge_hi, ge_lo, cum_ref, features, blocks,
                store, both_ref, halo_ref, coming, going, states, dx, dbc, slope, bc_act, xslope, sems):
    top = slice(0, HALO)
    arriving = begin(
        sems, (blocks.at[0, top], dx), (blocks.at[1, top], dbc), (blocks.at[2, top], slope),
        (blocks.at[3, top], bc_act), (features.at[1, top], xslope),
    )
    unpack_states(places, got_ref, 0, coming)
    unpack_states(places, got_ref, 1, going)
    enter = split2(coming[...])
    leave = split2(going[...])
    states[0, 0:STATE], states[0, STATE:] = enter
    states[1, 0:STATE], states[1, STATE:] = leave
    leaving = begin(sems, (states, store.at[0:2]), first=5)
    both_ref[...] = jnp.broadcast_to(jnp.sum(coming[...] * going[...], axis=0, keepdims=True), (8, COLS))
    fade = chunk_fade(cum_ref, HALO, expander(LANES))
    finish(arriving)
    pulls = dot3(split2(bc_act[:, 0:STATE]), leave, NN)
    keys = dbc[:, 0:STATE] + dot3((xf_hi[top], xf_lo[top]), leave, NT)
    queries = dbc[:, STATE:] + dot3((ge_hi[top], ge_lo[top]), enter, NT)
    gx = (dx[...] + fade * pulls) * xslope[...]
    halo_ref[:, 0:COLS] = gx[0:8]
    halo_ref[:, COLS : COLS + STATE] = (keys * slope[:, 0:STATE])[0:8]
    halo_ref[:, COLS + STATE :] = (queries * slope[:, STATE:])[0:8]
    finish(leaving)


def group_kernel(xf_hi, xf_lo, ge_hi, ge_lo, blocks, store, gbc_ref, states, dbc_ref, slope_ref, sems):
    first = begin(sems, (store.at[0:2], states))
    arriving = begin(sems, (blocks.at[1], dbc_ref), (blocks.at[2], slope_ref), first=1)
    finish(first)
    keys = dot3((xf_hi[...], xf_lo[...]), (states[1, 0:STATE], states[1, STATE:]), NT)
    queries = dot3((ge_hi[...], ge_lo[...]), (states[0, 0:STATE], states[0, STATE:]), NT)
    finish(arriving)
    gbc_ref[:, 0:STATE] = (dbc_ref[:, 0:STATE] + keys) * slope_ref[:, 0:STATE]
    gbc_ref[:, STATE:] = (dbc_ref[:, STATE:] + queries) * slope_ref[:, STATE:]


def back_conv(buf, taps):
    out = taps[0:1] * buf[3 : 3 + ROWS]
    for k in range(1, CONV):
        out = out + taps[k : k + 1] * buf[3 - k : 3 - k + ROWS]
    return out


def grad_bc_kernel(own, core_ref, rows_ref, halo_ref, taps_ref, keep_ref, give_ref, buf, terms):
    buf[0:ROWS] = rows_ref[...]
    buf[ROWS : ROWS + 8] = halo_ref[:, COLS:]
    terms[...] = back_conv(buf, taps_ref)
    core = core_ref[0]
    for pair in range(ROWS // (2 * own)):
        at = pair * 2 * own
        keep_ref[pair] = terms[pl.ds(pl.multiple_of(at + core * own, own), own)]
        give_ref[pair] = terms[pl.ds(pl.multiple_of(at + (1 - core) * own, own), own)]


def carry_kernel(xf_hi, xf_lo, ge_hi, ge_lo, cum_ref, features, blocks, store, both_ref, halo_ref, taps_ref,
                 grad_ref, glog_ref, buf, states, bc_act, dx_ref, xslope_ref, dlog_ref, sems):
    arriving = begin(
        sems, (store.at[0:2], states), (blocks.at[3], bc_act), (blocks.at[0], dx_ref),
        (features.at[1], xslope_ref), (blocks.at[4, :, 0:LANES], dlog_ref),
    )
    spread = expander(LANES)
    fade = chunk_fade(cum_ref, ROWS, spread)
    finish(arriving)
    pulls = dot3(split2(bc_act[:, 0:STATE]), (states[1, 0:STATE], states[1, STATE:]), NN)
    buf[0:ROWS] = (dx_ref[...] + fade * pulls) * xslope_ref[...]
    buf[ROWS : ROWS + 8] = halo_ref[:, 0:COLS]
    grad_ref[...] = back_conv(buf, taps_ref).astype(BF16)
    reads = dot3(split2(bc_act[:, STATE:]), (states[0, 0:STATE], states[0, STATE:]), NN)
    grown = ge_hi[...].astype(F32) + ge_lo[...].astype(F32)
    faded = xf_hi[...].astype(F32) + xf_lo[...].astype(F32)
    across = head_sums(grown * reads, spread)
    down = head_sums(faded * pulls, spread)
    last = jnp.zeros((1, LANES), F32)
    for b in range(BLOCKS):
        last = last + cum_ref[(b + 1) * BLOCK - 1 : (b + 1) * BLOCK]
    both = head_sums(both_ref[...], spread)[0:1] * jnp.exp(last)
    row, col = row_col((ROWS, ROWS))
    later = jnp.where(col >= row, 1.0, 0.0).astype(BF16)
    before = jnp.where(col < row, 1.0, 0.0).astype(BF16)
    found = dlog_ref[...] + exact_left(later, across, NN) + exact_left(before, down, NN) + both
    glog_ref[...] = jnp.transpose(found)[0:HEADS]


def call(kernel, outs, scratch=(), hbm_in=(), hbm_out=(), smem=(), count=0, sems=0, vmem=40, flops=1 << 26, size=1 << 22):
    def place(i, far):
        return pl.BlockSpec(memory_space=pltpu.SMEM if i in smem else pltpu.HBM if i in far else pltpu.VMEM)

    return pl.pallas_call(
        kernel,
        out_shape=[jax.ShapeDtypeStruct(shape, dtype) for shape, dtype in outs],
        in_specs=[place(i, hbm_in) for i in range(count)],
        out_specs=[
            pl.BlockSpec(memory_space=pltpu.HBM if i in hbm_out else pltpu.VMEM) for i in range(len(outs))
        ],
        scratch_shapes=[pltpu.VMEM(shape, dtype) for shape, dtype in scratch]
        + ([pltpu.SemaphoreType.DMA((sems,))] if sems else []),
        compiler_params=pltpu.CompilerParams(vmem_limit_bytes=vmem * 2**20),
        cost_estimate=pl.CostEstimate(flops=flops, bytes_accessed=size, transcendentals=0),
    )


def shifted(array, by):
    devices = lax.axis_size(CTX)
    pairs = [(i, i + by) for i in range(devices) if 0 <= i + by < devices]
    return lax.ppermute(array, CTX, pairs)


def per_device(x_in, bc_in, conv_x, conv_bc, log_decay, grad_y):
    core = lax.axis_index("core")
    owners = lax.axis_size(("x", "zh"))
    places = lax.axis_size(CTX)
    groups = bc_in.shape[1] // (2 * STATE)
    own = bc_in.shape[0]
    fan = owners // groups
    group = lax.axis_index(("x", "zh")) // fan
    taps_bc = lax.dynamic_slice_in_dim(conv_bc, group * (2 * STATE), 2 * STATE, 1)
    swap = [(0, 1), (1, 0)]

    (spread,) = call(
        fan_kernel, [((owners, own, 2 * STATE), BF16)], hbm_in=(0,), count=1, sems=owners, vmem=62
    )(bc_in)
    mine = lax.all_to_all(spread, ("x", "zh"), 0, 0, tiled=True)
    x_prev = shifted(x_in[ROWS - HALO :], 1)
    wide = (ROWS, COLS)
    padded = ((ROWS + 8, COLS), F32)
    store = (STORE,) + wide
    made = call(
        feature_kernel,
        [(store, F32)] + [(wide, BF16)] * 4 + [((ROWS, LANES), F32), ((BLOCKS, 8, BLOCK), F32)],
        [padded, (wide, F32), (wide, F32)], hbm_out=(0,), count=5, sems=2,
    )(x_in, x_prev, conv_x, log_decay.T, grad_y)
    mine, made = lax.optimization_barrier((mine, made))
    features, xf_hi, xf_lo, ge_hi, ge_lo, cum, cumt = made
    scaled = (xf_hi, xf_lo, ge_hi, ge_lo)
    bc_rows = lax.all_gather(mine, "core")
    bc_prev = shifted(bc_rows[1, owners - 1], 1)
    packed = (places * piece_rows(STATE // places), LANES)
    (sent,) = call(functools.partial(state_kernel, places), [(packed, F32)], [padded], count=8)(
        bc_rows, bc_prev, taps_bc, *scaled, cum
    )
    got = lax.all_to_all(sent.astype(jnp.float16), CTX, 0, 0, tiled=True)
    (blocks,) = call(
        block_kernel, [(store, F32)],
        [(wide, F32)] * 5 + [((ROWS, LANES), F32)] + [(wide, BF16)] * 2 + [padded],
        hbm_in=(0,), hbm_out=(0,), count=7, sems=6,
    )(features, grad_y, bc_rows, bc_prev, taps_bc, cum, cumt)

    (back,) = call(functools.partial(scan_kernel, places), [(packed, F32)], count=1)(got.astype(F32))
    carried = lax.all_to_all(back.astype(jnp.float16), CTX, 0, 0, tiled=True).astype(F32)

    half = (STATE, COLS)
    top = (HALO, COLS)
    pair = ((2,) + wide, BF16)
    states, both, first = call(
        functools.partial(open_kernel, places),
        [((2 * STORE,) + wide, BF16), ((8, COLS), F32), ((8, COLS + 2 * STATE), F32)],
        [(half, F32)] * 2 + [pair] + [(top, F32)] * 5,
        hbm_in=(6, 7), hbm_out=(0,), count=8, sems=6,
    )(carried, *scaled, cum, features, blocks)
    halo = shifted(first, -1)
    (gbc,) = call(
        group_kernel, [(wide, F32)], [pair] + [(wide, F32)] * 2, hbm_in=(4, 5), count=6, sems=3
    )(*scaled, blocks, states)
    piece = (owners, own, 2 * STATE)
    keep, give = call(
        functools.partial(grad_bc_kernel, own), [(piece, F32)] * 2, [padded, (wide, F32)], smem=(0,), count=4
    )(core.reshape(1), gbc, halo, taps_bc)
    summed = keep + lax.ppermute(give, "core", swap)
    parts = lax.all_to_all(summed, ("x", "zh"), 0, 0, tiled=True)
    grad_x, glog = call(
        carry_kernel,
        [(wide, BF16), ((HEADS, ROWS), F32)],
        [padded, pair] + [(wide, F32)] * 3 + [((ROWS, LANES), F32)],
        hbm_in=(5, 6, 7), count=11, sems=5,
    )(*scaled, cum, features, blocks, states, both, halo, conv_x)
    (grad_bc,) = call(fold_kernel, [((own, groups * 2 * STATE), F32)], count=1)(parts)
    return grad_x, grad_bc, glog.T


def solution(mesh):
    fine = Mesh(mesh.devices.reshape(8, 2, 4, 4, 2), CTX + TP)
    return jax.shard_map(
        per_device,
        mesh=fine,
        in_specs=(P(CTX, TP), P(CTX + TP, None), P(None, TP), P(), P(CTX, TP), P(CTX, TP)),
        out_specs=(P(CTX, TP), P(CTX + TP, None), P(CTX, TP)),
        check_vma=False,
    )
```

time: 151 us -> 133 us (0.88)
  blocking collectives: 49.9 us -> 32.9 us
  starting transfers between devices: 28.6 us -> 42.1 us
  waiting for transfers between devices: 27.3 us -> 16.8 us
  local copies, waits for them, and re-layouts: 12.8 us -> 4.25 us
  Pallas kernels: 23.7 us -> 30.4 us
  other arithmetic: 6.43 us -> 3.09 us
    all_to_all x1 -> x0, blocking collectives: 24.9 us -> none  [per_device(): mine = lax.all_to_all(spread, ('x', 'zh'), 0, 0, tiled=True)]
    all_to_all x0 -> x1, starting transfers between devices: none -> 13.4 us  [per_device(): mine = lax.all_to_all(spread, ('x', 'zh'), 0, 0, tiled=True)]
    ppermute x4 -> x3, waiting for transfers between devices: 14.4 us -> 2.56 us  [shifted(): return lax.ppermute(array, CTX, pairs)]
    unnamed x51 -> x16, local copies, waits for them, and re-layouts: 11.2 us -> 3.52 us
    all_to_all x1, waiting for transfers between devices: 2.06 us -> 9.24 us  [per_device(): parts = lax.all_to_all(summed, ('x', 'zh'), 0, 0, tiled=True)]
    pallas_call x7 -> x10, Pallas kernels: 23.7 us -> 30.4 us  [the longest x1 9.33 us: per_device(): call(block_kernel, [(store, F32)], [(wide, F32)] * 5 + [((ROWS, LANES), F...]
    all_to_all x1, waiting for transfers between devices: 9.34 us -> 3.2 us  [per_device(): lax.all_to_all(back.astype(jnp.float16), CTX, 0, 0, tiled=True).astype(F32)]
    all_to_all x1, starting transfers between devices: 3.57 us -> 9.33 us  [per_device(): parts = lax.all_to_all(summed, ('x', 'zh'), 0, 0, tiled=True)]
  transfers between devices with their start and end apart: 8 -> 7, of which waited for: 5 -> 7; matrix products, arithmetic and copies ran while one was open for 1% -> 1% of each run, Pallas kernels for 6% -> 17%
where the time goes in v2:
time: 133 us; the launch traced here: 130 us
  starting transfers between devices  42.1 us (32%)
  blocking collectives  32.9 us (25%)
  Pallas kernels  30.4 us (23%)
  waiting for transfers between devices  16.8 us (13%)
  local copies, waits for them, and re-layouts  4.25 us (3%)
  other arithmetic  3.09 us (2%)
    all_to_all x1, blocking collectives, per_device(): got = lax.all_to_all(sent.astype(jnp.float16), CTX, 0, 0, tiled=True)  27.8 us
    all_to_all x1, starting transfers between devices, per_device(): mine = lax.all_to_all(spread, ('x', 'zh'), 0, 0, tiled=True)  13.4 us
    all_to_all x1, starting transfers between devices, per_device(): parts = lax.all_to_all(summed, ('x', 'zh'), 0, 0, tiled=True)  9.33 us
    pallas_call x1, Pallas kernels, per_device(): call(block_kernel, [(store, F32)], [(wide, F32)] * 5 + [((ROWS, LANES), F...  9.33 us
    all_to_all x1, waiting for transfers between devices, per_device(): parts = lax.all_to_all(summed, ('x', 'zh'), 0, 0, tiled=True)  9.24 us
    ppermute x1, starting transfers between devices, per_device(): summed = keep + lax.ppermute(give, 'core', swap)  8.13 us
    ppermute x3, starting transfers between devices, shifted(): return lax.ppermute(array, CTX, pairs)  6.76 us
    pallas_call x1, Pallas kernels, per_device(): call(carry_kernel, [(wide, BF16), ((HEADS, ROWS), F32)], [padded, pair] +...  6.24 us
  transfers between devices with their start and end apart: 7, of which 7 were waited for; matrix products, arithmetic and copies ran while one was open for 1% of the time, Pallas kernels for 17%

profile of v2, /device:TPU:1, one launch (start us, length us, event | category | flops | bytes accessed | tf_op | source)
XLA Modules:
  0.0 130.4 jit_solution(4332915170630586186)
XLA Ops:
  0.6 0.0 copy-start
  0.6 0.0 copy-start.2
  0.7 1.8 %shard_map.85 = bf16[16,16,512]{2,1,0:T(8,128)(2,1)} custom-call(bf16[16,4096]{1,0:T(8,128)(2,1)} %rows_hbm.1), custom_call_target="tpu_custom_call" | custom-call | flops 67108864 | bytes 4194304 | tf_op jit(solution)/shard_map/pallas_call | solution.py:450
  2.4 13.4 %all-to-all-start = ((bf16[16,16,512]{2,1,0:T(8,128)(2,1)}), bf16[16,16,512]{2,1,0:T(8,128)(2,1)S(1)}, u32[]{:S(2)}, u32[]{:S(2)}) async-start(bf16[16,16,512]{2,1,0:T(8,128)(2,1)} %shard_map.85), calls=%async_computation | async-start | bytes 524288 | tf_op jit(solution)/shard_map/all_to_all | solution.py:453
  15.9 0.7 slice.6
  16.6 3.1 %collective-permute-start = (bf16[16,512]{1,0:T(8,128)(2,1)S(1)}, bf16[16,512]{1,0:T(8,128)(2,1)S(1)}, u32[]{:S(2)}, u32[]{:S(2)}) collective-permute-start(bf16[16,512]{1,0:T(8,128)(2,1)S(1)} %slice.6), channel_id=1, source_target_pairs={{0,32},{32,64},{64,96},{96,128},{128,160},{160,192},{192,224},{224... | collective-permute-start | bytes 49160 | tf_op jit(solution)/shard_map/ppermute | solution.py:436
  19.7 0.8 collective-permute-done.prev_ref
  20.5 0.0 copy-done.2
  20.5 0.0 copy-start.4
  20.6 1.0 copy-done.4
  21.6 0.0 copy-start.5
  21.6 0.7 copy-done.5
  22.3 0.0 copy-start.7
  22.3 0.7 copy-done.7
  23.0 4.1 %shard_map.86 = (f32[28,512,512]{2,1,0:T(8,128)}, bf16[512,512]{1,0:T(8,128)(2,1)S(1)}, bf16[512,512]{1,0:T(8,128)(2,1)S(1)}, bf16[512,512]{1,0:T(8,128)(2,1)S(1...) custom-call(bf16[512,512]{1,0:T(8,128)(2,1)S(1)} %copy-done.4, ...), custom_call_target="tpu_custom_call" | custom-call | flops 67108864 | bytes 4194304 | tf_op jit(solution)/shard_map/pallas_call | solution.py:458
  27.1 0.3 all-to-all-done
  27.4 5.1 %all-gather = bf16[32,16,512]{2,1,0:T(8,128)(2,1)S(1)} all-gather(bf16[16,16,512]{2,1,0:T(8,128)(2,1)S(1)} %all-to-all-done), channel_id=2, replica_groups=mesh['y'=8,'zl'=2,'x'=4,'zh'=4,'core'=2] {'core'}, dimensions={0}, use_global_device_ids=true | all-gather | bytes 786432 | tf_op jit(solution)/shard_map/all_gather | solution.py:466
  32.5 2.4 %collective-permute-start.1 = (bf16[16,512]{1,0:T(8,128)(2,1)S(1)}, bf16[16,512]{1,0:T(8,128)(2,1)S(1)}, u32[]{:S(2)}, u32[]{:S(2)}) collective-permute-start(bf16[16,512]{1,0:T(8,128)(2,1)S(1)} %slice_bitcast_fusion), channel_id=1, source_target_pairs={{0,32},{32,64},{64,96},{96,128},{128,160},{160,192},{192,224},{224... | collective-permute-start | bytes 49160 | tf_op jit(solution)/shard_map/ppermute | solution.py:436
  34.9 0.0 copy-done
  34.9 0.8 collective-permute-done.1.prev_ref
  35.8 1.8 %shard_map.88 = f32[2176,128]{1,0:T(8,128)S(1)} custom-call(bf16[2,16,16,512]{3,2,1,0:T(8,128)(2,1)S(1)} %bitcast.15, bf16[16,512]{1,0:T(8,128)(2,1)S(1)} %collective-permute-done.1.prev_ref, f32[4,512]{1,0:T(4,128)S(1)} %constant_dynamic-slice_fusion.taps_ref, bf16[512,512]{1,0:T(8,128)(2,1)S(1)} %get-tuple-element.32.xf_hi, ...), custom_call_target="tpu_custom_call" | custom-call | flops 67108864 | bytes 4194304 | tf_op jit(solution)/shard_map/pallas_call | solution.py:469
  37.6 0.1 convert_element_type.16
  37.7 27.8 %all_to_all.28 = f16[16,136,128]{2,1,0:T(8,128)(2,1)S(1)} all-to-all(f16[16,136,128]{2,1,0:T(8,128)(2,1)S(1)} %bitcast.18), channel_id=1, replica_groups=mesh['y'=8,'zl'=2,'x'=4,'zh'=4,'core'=2] {'y','zl'}, dimensions={0} | all-to-all | bytes 1114112 | tf_op jit(solution)/shard_map/all_to_all | solution.py:472
  65.5 0.1 bitcast_convert_fusion.1.got_ref
  65.6 1.2 shard_map.89
  66.8 0.9 convert_element_type.19
  67.7 4.4 %all-to-all-start.2 = ((f16[16,136,128]{2,1,0:T(8,128)(2,1)}), f16[16,136,128]{2,1,0:T(8,128)(2,1)}, u32[]{:S(2)}, u32[]{:S(2)}) async-start(f16[16,136,128]{2,1,0:T(8,128)(2,1)} %bitcast.5), calls=%async_computation.2 | async-start | bytes 1114112 | tf_op jit(solution)/shard_map/all_to_all | solution.py:480
  72.1 0.0 copy-start.3
  72.1 1.0 copy-done.3
  73.1 9.3 %shard_map.87.blocks = f32[28,512,512]{2,1,0:T(8,128)} custom-call(f32[28,512,512]{2,1,0:T(8,128)} %get-tuple-element.37.features, bf16[512,512]{1,0:T(8,128)(2,1)S(1)} %copy-done.3, bf16[2,16,16,512]{3,2,1,0:T(8,128)(2,1)S(1)} %bitcast.16, bf16[16,512]{1,0:T(8,128)(2,1)S(1)} %collective-permute-done.1.prev_ref, ...), custom_call_target="tpu_custom_call" | custom-call | flops 67108864 | bytes 4194304 | tf_op jit(solution)/shard_map/pallas_call | solution.py:473
  82.5 3.2 %all-to-all-done.2 = f16[16,136,128]{2,1,0:T(8,128)(2,1)} async-done(((f16[16,136,128]{2,1,0:T(8,128)(2,1)}), f16[16,136,128]{2,1,0:T(8,128)(2,1)}, u32[]{:S(2)}, u32[]{:S(2)}) %all-to-all-start.2) | async-done | bytes 557088 | tf_op jit(solution)/shard_map/all_to_all | solution.py:480
  85.7 1.1 bitcast_convert_fusion.got_ref
  86.8 1.8 %shard_map.90 = (bf16[56,512,512]{2,1,0:T(8,128)(2,1)}, f32[8,512]{1,0:T(8,128)S(1)}, f32[8,1024]{1,0:T(8,128)S(1)}) custom-call(f32[2176,128]{1,0:T(8,128)S(1)} %bitcast_convert_fusion.got_ref, bf16[512,512]{1,0:T(8,128)(2,1)S(1)} %get-tuple-element.32.xf_hi, bf16[512,512]{1,0:T(8,128)(2,1)S(1)} %get-tuple-element.33.xf_lo, ...), custom_call_target="tpu_custom_call" | custom-call | flops 67108864 | bytes 4194304 | tf_op jit(solution)/shard_map/pallas_call | solution.py:485
  88.6 1.3 collective-permute-start.2
  89.9 2.4 %shard_map.92.rows_ref = f32[512,512]{1,0:T(8,128)S(1)} custom-call(bf16[512,512]{1,0:T(8,128)(2,1)S(1)} %get-tuple-element.32.xf_hi, bf16[512,512]{1,0:T(8,128)(2,1)S(1)} %get-tuple-element.33.xf_lo, bf16[512,512]{1,0:T(8,128)(2,1)S(1)} %get-tuple-element.34.ge_hi, bf16[512,512]{1,0:T(8,128)(2,1)S(1)} %get-tuple-element.35.ge_lo, ...), custom_call_target="tpu_custom_call" | custom-call | flops 67108864 | bytes 4194304 | tf_op jit(solution)/shard_map/pallas_call | solution.py:492
  92.4 0.9 collective-permute-done.2.halo_ref
  93.3 1.0 shard_map.93
  94.3 8.1 %collective-permute-start.3 = (f32[16,16,512]{2,1,0:T(8,128)S(1)}, f32[16,16,512]{2,1,0:T(8,128)S(1)}, u32[]{:S(2)}, u32[]{:S(2)}) collective-permute-start(f32[16,16,512]{2,1,0:T(8,128)S(1)} %get-tuple-element.45), channel_id=1, source_target_pairs={{0,1},{1,0},{2,3},{3,2},{4,5},{5,4},{6,7},{7,6},{8,9},{9,8},{10,11... | collective-permute-start | bytes 1572872 | tf_op jit(solution)/shard_map/ppermute | solution.py:499
  102.4 1.5 %collective-permute-done.3 = f32[16,16,512]{2,1,0:T(8,128)S(1)} collective-permute-done((f32[16,16,512]{2,1,0:T(8,128)S(1)}, f32[16,16,512]{2,1,0:T(8,128)S(1)}, u32[]{:S(2)}, u32[]{:S(2)}) %collective-permute-start.3) | collective-permute-done | bytes 524320 | tf_op jit(solution)/shard_map/ppermute | solution.py:499
  103.9 0.0 copy-start.6
  103.9 0.9 add.12
  104.8 9.3 %all-to-all-start.3 = ((f32[16,16,512]{2,1,0:T(8,128)}), f32[16,16,512]{2,1,0:T(8,128)S(1)}, u32[]{:S(2)}, u32[]{:S(2)}) async-start(f32[16,16,512]{2,1,0:T(8,128)} %add.12), calls=%async_computation.3 | async-start | bytes 1048576 | tf_op jit(solution)/shard_map/all_to_all | solution.py:500
  114.2 0.0 copy-done.6
  114.2 0.0 copy-start.1
  114.2 6.2 %shard_map.91 = (bf16[512,512]{1,0:T(8,128)(2,1)}, f32[8,512]{1,0:T(8,128)}) custom-call(bf16[512,512]{1,0:T(8,128)(2,1)S(1)} %get-tuple-element.32.xf_hi, bf16[512,512]{1,0:T(8,128)(2,1)S(1)} %get-tuple-element.33.xf_lo, bf16[512,512]{1,0:T(8,128)(2,1)S(1)} %get-tuple-element.34.ge_hi, bf16[512,512]{1,0:T(8,128)(2,1)S(1)} %get-tuple-element.35.ge_lo, ...), custom_call_target="tpu_custom_call" | custom-call | flops 67108864 | bytes 4194304 | tf_op jit(solution)/shard_map/pallas_call | solution.py:501
  120.4 9.2 %all-to-all-done.3.parts_ref = f32[16,16,512]{2,1,0:T(8,128)S(1)} async-done(((f32[16,16,512]{2,1,0:T(8,128)}), f32[16,16,512]{2,1,0:T(8,128)S(1)}, u32[]{:S(2)}, u32[]{:S(2)}) %all-to-all-start.3) | async-done | bytes 524320 | tf_op jit(solution)/shard_map/all_to_all | solution.py:500
  129.7 0.7 shard_map.94
  130.4 0.0 copy-done.1
  (2 shorter events, 0.0 us)
Async XLA Ops:
  0.6 34.3 %copy-start = (f32[4,4096]{1,0:T(4,128)S(1)}, f32[4,4096]{1,0:T(4,128)}, u32[]{:S(2)}) copy-start(f32[4,4096]{1,0:T(4,128)} %param.9) | copy-start | bytes 196612
  0.6 19.9 %copy-start.2 = (bf16[512,512]{1,0:T(8,128)(2,1)S(1)}, bf16[512,512]{1,0:T(8,128)(2,1)}, u32[]{:S(2)}) copy-start(bf16[512,512]{1,0:T(8,128)(2,1)} %grad_ref.3) | copy-start | bytes 1572868
  2.4 24.9 %all-to-all-start = ((bf16[16,16,512]{2,1,0:T(8,128)(2,1)}), bf16[16,16,512]{2,1,0:T(8,128)(2,1)S(1)}, u32[]{:S(2)}, u32[]{:S(2)}) async-start(bf16[16,16,512]{2,1,0:T(8,128)(2,1)} %shard_map.85), calls=%async_computation | async-start | bytes 524288 | tf_op jit(solution)/shard_map/all_to_all | solution.py:453
  16.6 3.9 %collective-permute-start = (bf16[16,512]{1,0:T(8,128)(2,1)S(1)}, bf16[16,512]{1,0:T(8,128)(2,1)S(1)}, u32[]{:S(2)}, u32[]{:S(2)}) collective-permute-start(bf16[16,512]{1,0:T(8,128)(2,1)S(1)} %slice.6), channel_id=1, source_target_pairs={{0,32},{32,64},{64,96},{96,128},{128,160},{160,192},{192,224},{224... | collective-permute-start | bytes 49160 | tf_op jit(solution)/shard_map/ppermute | solution.py:436
  20.5 1.0 copy-start.4
  21.6 0.7 copy-start.5
  22.3 0.7 copy-start.7
  32.5 3.2 %collective-permute-start.1 = (bf16[16,512]{1,0:T(8,128)(2,1)S(1)}, bf16[16,512]{1,0:T(8,128)(2,1)S(1)}, u32[]{:S(2)}, u32[]{:S(2)}) collective-permute-start(bf16[16,512]{1,0:T(8,128)(2,1)S(1)} %slice_bitcast_fusion), channel_id=1, source_target_pairs={{0,32},{32,64},{64,96},{96,128},{128,160},{160,192},{192,224},{224... | collective-permute-start | bytes 49160 | tf_op jit(solution)/shard_map/ppermute | solution.py:436
  67.7 18.0 %all-to-all-start.2 = ((f16[16,136,128]{2,1,0:T(8,128)(2,1)}), f16[16,136,128]{2,1,0:T(8,128)(2,1)}, u32[]{:S(2)}, u32[]{:S(2)}) async-start(f16[16,136,128]{2,1,0:T(8,128)(2,1)} %bitcast.5), calls=%async_computation.2 | async-start | bytes 1114112 | tf_op jit(solution)/shard_map/all_to_all | solution.py:480
  72.1 1.0 copy-start.3
  88.6 4.7 %collective-permute-start.2 = (f32[8,1024]{1,0:T(8,128)S(1)}, f32[8,1024]{1,0:T(8,128)S(1)}, u32[]{:S(2)}, u32[]{:S(2)}) collective-permute-start(f32[8,1024]{1,0:T(8,128)S(1)} %get-tuple-element.42), channel_id=1, source_target_pairs={{32,0},{64,32},{96,64},{128,96},{160,128},{192,160},{224,192},{256... | collective-permute-start | bytes 98312 | tf_op jit(solution)/shard_map/ppermute | solution.py:436
  94.3 9.7 %collective-permute-start.3 = (f32[16,16,512]{2,1,0:T(8,128)S(1)}, f32[16,16,512]{2,1,0:T(8,128)S(1)}, u32[]{:S(2)}, u32[]{:S(2)}) collective-permute-start(f32[16,16,512]{2,1,0:T(8,128)S(1)} %get-tuple-element.45), channel_id=1, source_target_pairs={{0,1},{1,0},{2,3},{3,2},{4,5},{5,4},{6,7},{7,6},{8,9},{9,8},{10,11... | collective-permute-start | bytes 1572872 | tf_op jit(solution)/shard_map/ppermute | solution.py:499
  103.9 10.2 %copy-start.6 = (f32[4,512]{1,0:T(4,128)S(1)}, f32[4,512]{1,0:T(4,128)}, u32[]{:S(2)}) copy-start(f32[4,512]{1,0:T(4,128)} %taps_ref.3) | copy-start | bytes 24580
  104.8 24.9 %all-to-all-start.3 = ((f32[16,16,512]{2,1,0:T(8,128)}), f32[16,16,512]{2,1,0:T(8,128)S(1)}, u32[]{:S(2)}, u32[]{:S(2)}) async-start(f32[16,16,512]{2,1,0:T(8,128)} %add.12), calls=%async_computation.3 | async-start | bytes 1048576 | tf_op jit(solution)/shard_map/all_to_all | solution.py:500
  114.2 16.2 %copy-start.1 = (f32[4,4096]{1,0:T(4,128)S(1)}, f32[4,4096]{1,0:T(4,128)}, u32[]{:S(2)}) copy-start(f32[4,4096]{1,0:T(4,128)} %param.9) | copy-start | bytes 196612

commit v3 on v2

--- a/solution.py
+++ b/solution.py
@@ -99,7 +99,7 @@
 
 def group_conv(buf, prev, gathered, taps):
     cores, pairs, own, _ = gathered.shape
-    buf[0:8] = prev[HALO - 8 :].astype(F32)
+    buf[0:8] = prev[0][HALO - 8 :].astype(F32) + prev[1][HALO - 8 :].astype(F32)
     for pair in range(pairs):
         for core in range(cores):
             at = 8 + (pair * cores + core) * own
@@ -120,16 +120,6 @@
     finish(copies)
 
 
-def fold_kernel(parts_ref, out_ref):
-    groups = out_ref.shape[1] // (2 * STATE)
-    fan = parts_ref.shape[0] // groups
-    for group in range(groups):
-        total = parts_ref[group * fan]
-        for one in range(1, fan):
-            total = total + parts_ref[group * fan + one]
-        out_ref[:, group * 2 * STATE : (group + 1) * 2 * STATE] = total
-
-
 def widen(values, spread):
     return exact_right(values, spread, NN)
 
@@ -143,33 +133,31 @@
     return mul(high, spread, NT) + mul(low, spread, NT)
 
 
-def feature_kernel(x_ref, prev_ref, taps_ref, log_ref, grad_ref,
-                   store, xf_hi, xf_lo, ge_hi, ge_lo, cum_ref, cumt_ref, buf, act_ref, slope_ref, sems):
+def decay_kernel(log_ref, grad_ref, ge_hi, ge_lo, cum_ref, cumt_ref):
+    row, col = row_col()
+    upper = jnp.where(row <= col, 1.0, 0.0).astype(BF16)
+    lower = jnp.where(col <= row, 1.0, 0.0).astype(BF16)
+    spread = expander(LANES)
+    before = jnp.zeros((1, LANES), F32)
+    for b in range(BLOCKS):
+        part = slice(b * BLOCK, (b + 1) * BLOCK)
+        logs = log_ref[:, part]
+        padded = jnp.concatenate([logs, jnp.zeros((LANES - HEADS, BLOCK), F32)], axis=0)
+        cum = exact_left(lower, padded, NT)
+        cum_ref[part] = cum
+        cumt_ref[b] = exact_right(logs, upper, NN)
+        ge_hi[part], ge_lo[part] = split2(grad_ref[part].astype(F32) * widen(jnp.exp(before + cum), spread))
+        before = before + cum[BLOCK - 1 : BLOCK]
+
+
+def feature_kernel(x_ref, prev_ref, taps_ref, cum_ref, store, xf_hi, xf_lo, buf, act_ref, slope_ref, sems):
     pre = conv(buf, prev_ref, x_ref, taps_ref)
     gate = sigmoid(pre)
     act = pre * gate
     act_ref[...] = act
     slope_ref[...] = gate * (1.0 + pre * (1.0 - gate))
     leaving = begin(sems, (act_ref, store.at[0]), (slope_ref, store.at[1]))
-    row, col = row_col()
-    upper = jnp.where(row <= col, 1.0, 0.0).astype(BF16)
-    lower = jnp.where(col <= row, 1.0, 0.0).astype(BF16)
-    spread = expander(LANES)
-    cums = []
-    for b in range(BLOCKS):
-        part = slice(b * BLOCK, (b + 1) * BLOCK)
-        logs = log_ref[:, part]
-        padded = jnp.concatenate([logs, jnp.zeros((LANES - HEADS, BLOCK), F32)], axis=0)
-        cums.append(exact_left(lower, padded, NT))
-        cum_ref[part] = cums[b]
-        cumt_ref[b] = exact_right(logs, upper, NN)
-    lasts = [cum[BLOCK - 1 : BLOCK] for cum in cums]
-    for b in range(BLOCKS):
-        part = slice(b * BLOCK, (b + 1) * BLOCK)
-        since = cums[b] + sum(lasts[:b], jnp.zeros((1, LANES), F32))
-        until = lasts[b] - cums[b] + sum(lasts[b + 1 :], jnp.zeros((1, LANES), F32))
-        xf_hi[part], xf_lo[part] = split2(act[part] * widen(jnp.exp(until), spread))
-        ge_hi[part], ge_lo[part] = split2(grad_ref[part].astype(F32) * widen(jnp.exp(since), spread))
+    xf_hi[...], xf_lo[...] = split2(act * chunk_fade(cum_ref, ROWS, expander(LANES)))
     finish(leaving)
 
 
@@ -214,8 +202,8 @@
     return [got[first + t * count : first + (t + 1) * count] * down for t in range(COLS // LANES)]
 
 
-def state_kernel(places, bc_ref, prev_ref, taps_ref, xf_hi, xf_lo, ge_hi, ge_lo, cum_ref, pack_ref, buf):
-    pre = group_conv(buf, prev_ref, bc_ref, taps_ref)
+def state_kernel(places, bc_ref, prev_0, prev_1, taps_ref, xf_hi, xf_lo, ge_hi, ge_lo, cum_ref, pack_ref, buf):
+    pre = group_conv(buf, (prev_0, prev_1), bc_ref, taps_ref)
     act = pre * sigmoid(pre)
     keys = split2(act[:, 0:STATE])
     queries = split2(act[:, STATE:])
@@ -231,6 +219,41 @@
     for p in range(places):
         rows = slice(p * count, (p + 1) * count)
         pack_piece(state[rows], grad[rows], pack_ref, p, logs)
+
+
+def term_rows(own):
+    return own * (2 * STATE // LANES) + META_ROWS
+
+
+def sum_kernel(keep_ref, got_ref, out_ref):
+    own = keep_ref.shape[1]
+    for owner in range(keep_ref.shape[0]):
+        start = owner * term_rows(own)
+        terms = keep_ref[owner] + got_ref[owner]
+        up = power_scale(terms)
+        scaled = terms * jnp.exp2(up)
+        for t in range(2 * STATE // LANES):
+            out_ref[start + t * own : start + (t + 1) * own] = scaled[:, t * LANES : (t + 1) * LANES]
+        end = start + term_rows(own)
+        out_ref[end - META_ROWS : end] = jnp.broadcast_to(up, (META_ROWS, LANES))
+
+
+def fold_kernel(parts_ref, out_ref):
+    own = out_ref.shape[0]
+    groups = out_ref.shape[1] // (2 * STATE)
+    fan = parts_ref.shape[0] // term_rows(own) // groups
+    for group in range(groups):
+        downs = []
+        for one in range(fan):
+            end = (group * fan + one + 1) * term_rows(own)
+            downs.append(jnp.exp2(-parts_ref[end - META_ROWS : end - META_ROWS + 1]))
+        for t in range(2 * STATE // LANES):
+            total = jnp.zeros((own, LANES), F32)
+            for one in range(fan):
+                start = (group * fan + one) * term_rows(own) + t * own
+                total = total + parts_ref[start : start + own] * downs[one]
+            at = group * 2 * STATE + t * LANES
+            out_ref[:, at : at + LANES] = total
 
 
 def scan_kernel(places, got_ref, out_ref):
@@ -256,10 +279,10 @@
         going = decays[p] * going + jnp.concatenate(unpack_piece(got_ref, p, count, 1), axis=1)
 
 
-def block_kernel(features, grad_ref, bc_ref, prev_ref, taps_ref, cum_ref, cumt_ref, store,
+def block_kernel(features, grad_ref, bc_ref, prev_0, prev_1, taps_ref, cum_ref, cumt_ref, store,
                  act_ref, dx_ref, dbc_ref, slope_ref, bc_act, dlog_ref, bc_hi, bc_lo, buf, sems):
     coming = begin(sems, (features.at[0], act_ref))
-    pre = group_conv(buf, prev_ref, bc_ref, taps_ref)
+    pre = group_conv(buf, (prev_0, prev_1), bc_ref, taps_ref)
     gate = sigmoid(pre)
     slope_ref[...] = gate * (1.0 + pre * (1.0 - gate))
     bc_act[...] = pre * gate
@@ -455,26 +478,33 @@
     wide = (ROWS, COLS)
     padded = ((ROWS + 8, COLS), F32)
     store = (STORE,) + wide
+    ge_hi, ge_lo, cum, cumt = call(
+        decay_kernel, [(wide, BF16)] * 2 + [((ROWS, LANES), F32), ((BLOCKS, HEADS, BLOCK), F32)], count=2
+    )(log_decay.T, grad_y)
     made = call(
-        feature_kernel,
-        [(store, F32)] + [(wide, BF16)] * 4 + [((ROWS, LANES), F32), ((BLOCKS, 8, BLOCK), F32)],
-        [padded, (wide, F32), (wide, F32)], hbm_out=(0,), count=5, sems=2,
-    )(x_in, x_prev, conv_x, log_decay.T, grad_y)
+        feature_kernel, [(store, F32)] + [(wide, BF16)] * 2, [padded, (wide, F32), (wide, F32)],
+        hbm_out=(0,), count=4, sems=2,
+    )(x_in, x_prev, conv_x, cum)
     mine, made = lax.optimization_barrier((mine, made))
-    features, xf_hi, xf_lo, ge_hi, ge_lo, cum, cumt = made
+    features, xf_hi, xf_lo = made
     scaled = (xf_hi, xf_lo, ge_hi, ge_lo)
+    bc_prev = [
+        lax.ppermute(
+            mine[owners - 1], CTX + ("core",), [(2 * i + 1, 2 * (i + 1) + to) for i in range(places - 1)]
+        )
+        for to in (0, 1)
+    ]
     bc_rows = lax.all_gather(mine, "core")
-    bc_prev = shifted(bc_rows[1, owners - 1], 1)
     packed = (places * piece_rows(STATE // places), LANES)
-    (sent,) = call(functools.partial(state_kernel, places), [(packed, F32)], [padded], count=8)(
-        bc_rows, bc_prev, taps_bc, *scaled, cum
+    (sent,) = call(functools.partial(state_kernel, places), [(packed, F32)], [padded], count=9)(
+        bc_rows, *bc_prev, taps_bc, *scaled, cum
     )
     got = lax.all_to_all(sent.astype(jnp.float16), CTX, 0, 0, tiled=True)
     (blocks,) = call(
         block_kernel, [(store, F32)],
         [(wide, F32)] * 5 + [((ROWS, LANES), F32)] + [(wide, BF16)] * 2 + [padded],
-        hbm_in=(0,), hbm_out=(0,), count=7, sems=6,
-    )(features, grad_y, bc_rows, bc_prev, taps_bc, cum, cumt)
+        hbm_in=(0,), hbm_out=(0,), count=8, sems=6,
+    )(features, grad_y, bc_rows, *bc_prev, taps_bc, cum, cumt)
 
     (back,) = call(functools.partial(scan_kernel, places), [(packed, F32)], count=1)(got.astype(F32))
     carried = lax.all_to_all(back.astype(jnp.float16), CTX, 0, 0, tiled=True).astype(F32)
@@ -496,8 +526,10 @@
     keep, give = call(
         functools.partial(grad_bc_kernel, own), [(piece, F32)] * 2, [padded, (wide, F32)], smem=(0,), count=4
     )(core.reshape(1), gbc, halo, taps_bc)
-    summed = keep + lax.ppermute(give, "core", swap)
-    parts = lax.all_to_all(summed, ("x", "zh"), 0, 0, tiled=True)
+    (summed,) = call(sum_kernel, [((owners * term_rows(own), LANES), F32)], count=2)(
+        keep, lax.ppermute(give, "core", swap)
+    )
+    parts = lax.all_to_all(summed.astype(jnp.float16), ("x", "zh"), 0, 0, tiled=True).astype(F32)
     grad_x, glog = call(
         carry_kernel,
         [(wide, BF16), ((HEADS, ROWS), F32)],

time: 133 us -> 122 us (0.917); the launches traced: 130 us -> 121 us
  blocking collectives: 32.9 us -> 25.6 us
  waiting for transfers between devices: 16.8 us -> 14.2 us
  starting transfers between devices: 42.1 us -> 44.2 us
  local copies, waits for them, and re-layouts: 4.25 us -> 2.52 us
    ppermute x1 -> x3, starting transfers between devices: 8.13 us -> 14.6 us  [the longest x1 8.31 us: per_device(): lax.ppermute(give, 'core', swap)]
    all_to_all x1, blocking collectives: 27.8 us -> 23.4 us  [per_device(): got = lax.all_to_all(sent.astype(jnp.float16), CTX, 0, 0, tiled=True)]
    all_to_all x1, waiting for transfers between devices: 9.24 us -> 6.09 us  [per_device(): lax.all_to_all(summed.astype(jnp.float16), ('x', 'zh'), 0, 0, tiled=True)]
    all_gather x1, blocking collectives: 5.14 us -> 2.18 us  [per_device(): bc_rows = lax.all_gather(mine, 'core')]
    ppermute x3 -> x2, starting transfers between devices: 6.76 us -> 4.38 us  [shifted(): return lax.ppermute(array, CTX, pairs)]
    all_to_all x1, starting transfers between devices: 9.33 us -> 7.15 us  [per_device(): lax.all_to_all(summed.astype(jnp.float16), ('x', 'zh'), 0, 0, tiled=True)]
    all_to_all x1, waiting for transfers between devices: 0.3 us -> 2.45 us  [per_device(): mine = lax.all_to_all(spread, ('x', 'zh'), 0, 0, tiled=True)]
    unnamed x16 -> x14, local copies, waits for them, and re-layouts: 3.52 us -> 1.78 us
  transfers between devices with their start and end apart: 7 -> 8, of which waited for: 7 -> 5; matrix products, arithmetic and copies ran while one was open for 1% -> 1% of each run, Pallas kernels for 17% -> 19%
where the time goes in v3:
time: 122 us; the launch traced here: 121 us
  starting transfers between devices  44.2 us (36%)
  Pallas kernels  31 us (25%)
  blocking collectives  25.6 us (21%)
  waiting for transfers between devices  14.2 us (12%)
  other arithmetic  3.02 us (2%)
  local copies, waits for them, and re-layouts  2.52 us (2%)
    all_to_all x1, blocking collectives, per_device(): got = lax.all_to_all(sent.astype(jnp.float16), CTX, 0, 0, tiled=True)  23.4 us
    all_to_all x1, starting transfers between devices, per_device(): mine = lax.all_to_all(spread, ('x', 'zh'), 0, 0, tiled=True)  13.4 us
    pallas_call x1, Pallas kernels, per_device(): call(block_kernel, [(store, F32)], [(wide, F32)] * 5 + [((ROWS, LANES), F...  9.38 us
    ppermute x1, starting transfers between devices, per_device(): lax.ppermute(give, 'core', swap)  8.31 us
    all_to_all x1, starting transfers between devices, per_device(): lax.all_to_all(summed.astype(jnp.float16), ('x', 'zh'), 0, 0, tiled=True)  7.15 us
    pallas_call x1, Pallas kernels, per_device(): call(carry_kernel, [(wide, BF16), ((HEADS, ROWS), F32)], [padded, pair] +...  6.28 us
    ppermute x2, starting transfers between devices, per_device(): lax.ppermute(mine[owners - 1], CTX + ('core',), [(2 * i + 1, 2 * (i + 1)...  6.27 us
    all_to_all x1, waiting for transfers between devices, per_device(): lax.all_to_all(summed.astype(jnp.float16), ('x', 'zh'), 0, 0, tiled=True)  6.09 us
  transfers between devices with their start and end apart: 8, of which 5 were waited for; matrix products, arithmetic and copies ran while one was open for 1% of the time, Pallas kernels for 19%

profile of v3, /device:TPU:1, one launch (start us, length us, event | category | flops | bytes accessed | tf_op | source)
XLA Modules:
  0.0 121.4 jit_solution(8105562232607929125)
XLA Ops:
  0.6 0.0 copy-start
  0.6 0.0 copy-start.2
  0.7 0.0 copy-start.4
  0.7 0.0 copy-start.5
  0.7 1.8 %shard_map.85 = bf16[16,16,512]{2,1,0:T(8,128)(2,1)} custom-call(bf16[16,4096]{1,0:T(8,128)(2,1)} %rows_hbm.1), custom_call_target="tpu_custom_call" | custom-call | flops 67108864 | bytes 4194304 | tf_op jit(solution)/shard_map/pallas_call | solution.py:473
  2.5 13.4 %all-to-all-start = ((bf16[16,16,512]{2,1,0:T(8,128)(2,1)}), bf16[16,16,512]{2,1,0:T(8,128)(2,1)S(1)}, u32[]{:S(2)}, u32[]{:S(2)}) async-start(bf16[16,16,512]{2,1,0:T(8,128)(2,1)} %shard_map.85), calls=%async_computation | async-start | bytes 524288 | tf_op jit(solution)/shard_map/all_to_all | solution.py:476
  15.9 0.7 slice.7
  16.6 3.1 %collective-permute-start = (bf16[16,512]{1,0:T(8,128)(2,1)S(1)}, bf16[16,512]{1,0:T(8,128)(2,1)S(1)}, u32[]{:S(2)}, u32[]{:S(2)}) collective-permute-start(bf16[16,512]{1,0:T(8,128)(2,1)S(1)} %slice.7), channel_id=1, source_target_pairs={{0,32},{32,64},{64,96},{96,128},{128,160},{160,192},{192,224},{224... | collective-permute-start | bytes 49160 | tf_op jit(solution)/shard_map/ppermute | solution.py:459
  19.8 0.0 copy-done
  19.8 0.0 copy-done.2
  19.8 0.0 copy-start.6
  19.8 0.7 copy-done.6
  20.5 1.1 shard_map.86
  21.6 0.0 collective-permute-done.prev_ref
  21.6 0.0 copy-done.4
  21.6 0.0 copy-done.5
  21.6 3.4 %shard_map.87 = (f32[28,512,512]{2,1,0:T(8,128)}, bf16[512,512]{1,0:T(8,128)(2,1)S(1)}, bf16[512,512]{1,0:T(8,128)(2,1)S(1)}) custom-call(bf16[512,512]{1,0:T(8,128)(2,1)S(1)} %copy-done.4, bf16[16,512]{1,0:T(8,128)(2,1)S(1)} %collective-permute-done.prev_ref, f32[4,512]{1,0:T(4,128)S(1)} %copy-done.5, f32[512,128]{1,0:T(8,128)S(1)} %get-tuple-element.21.cum_ref), custom_call_target="tpu_custom_call" | custom-call | flops 67108864 | bytes 4194304 | tf_op jit(solution)/shard_map/pallas_call | solution.py:484
  25.0 2.5 %all-to-all-done = bf16[16,16,512]{2,1,0:T(8,128)(2,1)S(1)} async-done(((bf16[16,16,512]{2,1,0:T(8,128)(2,1)}), bf16[16,16,512]{2,1,0:T(8,128)(2,1)S(1)}, u32[]{:S(2)}, u32[]{:S(2)}) %all-to-all-start) | async-done | bytes 262176 | tf_op jit(solution)/shard_map/all_to_all | solution.py:476
  27.4 4.1 %collective-permute-start.2 = (bf16[16,512]{1,0:T(8,128)(2,1)S(1)}, bf16[16,512]{1,0:T(8,128)(2,1)S(1)}, u32[]{:S(2)}, u32[]{:S(2)}) collective-permute-start(bf16[16,512]{1,0:T(8,128)(2,1)S(1)} %slice_bitcast_fusion), channel_id=1, source_target_pairs={{1,33},{33,65},{65,97},{97,129},{129,161},{161,193},{193,225},{225... | collective-permute-start | bytes 49160 | tf_op jit(solution)/shard_map/ppermute | solution.py:492
  31.5 2.2 %collective-permute-start.1 = (bf16[16,512]{1,0:T(8,128)(2,1)S(1)}, bf16[16,512]{1,0:T(8,128)(2,1)S(1)}, u32[]{:S(2)}, u32[]{:S(2)}) collective-permute-start(bf16[16,512]{1,0:T(8,128)(2,1)S(1)} %slice_bitcast_fusion), channel_id=1, source_target_pairs={{1,32},{33,64},{65,96},{97,128},{129,160},{161,192},{193,224},{225... | collective-permute-start | bytes 49160 | tf_op jit(solution)/shard_map/ppermute | solution.py:492
  33.7 2.2 %all-gather = bf16[32,16,512]{2,1,0:T(8,128)(2,1)S(1)} all-gather(bf16[16,16,512]{2,1,0:T(8,128)(2,1)S(1)} %all-to-all-done), channel_id=2, replica_groups=mesh['y'=8,'zl'=2,'x'=4,'zh'=4,'core'=2] {'core'}, dimensions={0}, use_global_device_ids=true | all-gather | bytes 786432 | tf_op jit(solution)/shard_map/all_gather | solution.py:497
  35.9 0.0 collective-permute-done.2.prev_1
  35.9 0.0 collective-permute-done.1.prev_0
  35.9 1.8 %shard_map.89 = f32[2176,128]{1,0:T(8,128)S(1)} custom-call(bf16[2,16,16,512]{3,2,1,0:T(8,128)(2,1)S(1)} %bitcast.18, bf16[16,512]{1,0:T(8,128)(2,1)S(1)} %collective-permute-done.1.prev_0, bf16[16,512]{1,0:T(8,128)(2,1)S(1)} %collective-permute-done.2.prev_1, f32[4,512]{1,0:T(4,128)S(1)} %constant_dynamic-slice_fusion.taps_ref, ...), custom_call_target="tpu_custom_call" | custom-call | flops 67108864 | bytes 4194304 | tf_op jit(solution)/shard_map/pallas_call | solution.py:499
  37.7 0.1 convert_element_type.24
  37.8 23.4 %all_to_all.32 = f16[16,136,128]{2,1,0:T(8,128)(2,1)S(1)} all-to-all(f16[16,136,128]{2,1,0:T(8,128)(2,1)S(1)} %bitcast.21), channel_id=1, replica_groups=mesh['y'=8,'zl'=2,'x'=4,'zh'=4,'core'=2] {'y','zl'}, dimensions={0} | all-to-all | bytes 1114112 | tf_op jit(solution)/shard_map/all_to_all | solution.py:502
  61.2 0.1 bitcast_convert_fusion.1.got_ref
  61.3 1.2 %shard_map.90 = f32[2176,128]{1,0:T(8,128)S(1)} custom-call(f32[2176,128]{1,0:T(8,128)S(1)} %bitcast_convert_fusion.1.got_ref), custom_call_target="tpu_custom_call" | custom-call | flops 67108864 | bytes 4194304 | tf_op jit(solution)/shard_map/pallas_call | solution.py:509
  62.6 0.9 convert_element_type.27
  63.4 4.6 %all-to-all-start.2 = ((f16[16,136,128]{2,1,0:T(8,128)(2,1)}), f16[16,136,128]{2,1,0:T(8,128)(2,1)}, u32[]{:S(2)}, u32[]{:S(2)}) async-start(f16[16,136,128]{2,1,0:T(8,128)(2,1)} %bitcast.5), calls=%async_computation.2 | async-start | bytes 1114112 | tf_op jit(solution)/shard_map/all_to_all | solution.py:510
  68.1 0.0 copy-start.3
  68.1 1.0 copy-done.3
  69.1 9.4 %shard_map.88.blocks = f32[28,512,512]{2,1,0:T(8,128)} custom-call(f32[28,512,512]{2,1,0:T(8,128)} %get-tuple-element.29.features, bf16[512,512]{1,0:T(8,128)(2,1)S(1)} %copy-done.3, bf16[2,16,16,512]{3,2,1,0:T(8,128)(2,1)S(1)} %bitcast.19, bf16[16,512]{1,0:T(8,128)(2,1)S(1)} %collective-permute-done.1.prev_0, ...), custom_call_target="tpu_custom_call" | custom-call | flops 67108864 | bytes 4194304 | tf_op jit(solution)/shard_map/pallas_call | solution.py:503
  78.5 3.2 %all-to-all-done.2 = f16[16,136,128]{2,1,0:T(8,128)(2,1)} async-done(((f16[16,136,128]{2,1,0:T(8,128)(2,1)}), f16[16,136,128]{2,1,0:T(8,128)(2,1)}, u32[]{:S(2)}, u32[]{:S(2)}) %all-to-all-start.2) | async-done | bytes 557088 | tf_op jit(solution)/shard_map/all_to_all | solution.py:510
  81.7 1.1 bitcast_convert_fusion.got_ref
  82.9 1.8 %shard_map.91 = (bf16[56,512,512]{2,1,0:T(8,128)(2,1)}, f32[8,512]{1,0:T(8,128)S(1)}, f32[8,1024]{1,0:T(8,128)S(1)}) custom-call(f32[2176,128]{1,0:T(8,128)S(1)} %bitcast_convert_fusion.got_ref, bf16[512,512]{1,0:T(8,128)(2,1)S(1)} %get-tuple-element.25.xf_hi, bf16[512,512]{1,0:T(8,128)(2,1)S(1)} %get-tuple-element.26.xf_lo, ...), custom_call_target="tpu_custom_call" | custom-call | flops 67108864 | bytes 4194304 | tf_op jit(solution)/shard_map/pallas_call | solution.py:515
  84.6 1.3 %collective-permute-start.3 = (f32[8,1024]{1,0:T(8,128)S(1)}, f32[8,1024]{1,0:T(8,128)S(1)}, u32[]{:S(2)}, u32[]{:S(2)}) collective-permute-start(f32[8,1024]{1,0:T(8,128)S(1)} %get-tuple-element.34), channel_id=1, source_target_pairs={{32,0},{64,32},{96,64},{128,96},{160,128},{192,160},{224,192},{256... | collective-permute-start | bytes 98312 | tf_op jit(solution)/shard_map/ppermute | solution.py:459
  85.9 2.4 %shard_map.93.rows_ref = f32[512,512]{1,0:T(8,128)S(1)} custom-call(bf16[512,512]{1,0:T(8,128)(2,1)S(1)} %get-tuple-element.25.xf_hi, bf16[512,512]{1,0:T(8,128)(2,1)S(1)} %get-tuple-element.26.xf_lo, bf16[512,512]{1,0:T(8,128)(2,1)S(1)} %get-tuple-element.27.ge_hi, bf16[512,512]{1,0:T(8,128)(2,1)S(1)} %get-tuple-element.28.ge_lo, ...), custom_call_target="tpu_custom_call" | custom-call | flops 67108864 | bytes 4194304 | tf_op jit(solution)/shard_map/pallas_call | solution.py:522
  88.4 0.9 collective-permute-done.3.halo_ref
  89.3 1.0 shard_map.94
  90.3 8.3 %collective-permute-start.4 = (f32[16,16,512]{2,1,0:T(8,128)S(1)}, f32[16,16,512]{2,1,0:T(8,128)S(1)}, u32[]{:S(2)}, u32[]{:S(2)}) collective-permute-start(f32[16,16,512]{2,1,0:T(8,128)S(1)} %get-tuple-element.37), channel_id=1, source_target_pairs={{0,1},{1,0},{2,3},{3,2},{4,5},{5,4},{6,7},{7,6},{8,9},{9,8},{10,11... | collective-permute-start | bytes 1572872 | tf_op jit(solution)/shard_map/ppermute | solution.py:530
  98.6 1.5 %collective-permute-done.4.got_ref = f32[16,16,512]{2,1,0:T(8,128)S(1)} collective-permute-done((f32[16,16,512]{2,1,0:T(8,128)S(1)}, f32[16,16,512]{2,1,0:T(8,128)S(1)}, u32[]{:S(2)}, u32[]{:S(2)}) %collective-permute-start.4) | collective-permute-done | bytes 524320 | tf_op jit(solution)/shard_map/ppermute | solution.py:530
  100.1 0.2 shard_map.95
  100.3 0.8 convert_element_type.30
  101.1 7.2 %all-to-all-start.3 = ((f16[16,72,128]{2,1,0:T(8,128)(2,1)}), f16[16,72,128]{2,1,0:T(8,128)(2,1)S(1)}, u32[]{:S(2)}, u32[]{:S(2)}) async-start(f16[16,72,128]{2,1,0:T(8,128)(2,1)} %bitcast.8), calls=%async_computation.3 | async-start | bytes 589824 | tf_op jit(solution)/shard_map/all_to_all | solution.py:532
  108.2 0.0 copy-start.1
  108.2 6.3 %shard_map.92 = (bf16[512,512]{1,0:T(8,128)(2,1)}, f32[8,512]{1,0:T(8,128)}) custom-call(bf16[512,512]{1,0:T(8,128)(2,1)S(1)} %get-tuple-element.25.xf_hi, bf16[512,512]{1,0:T(8,128)(2,1)S(1)} %get-tuple-element.26.xf_lo, bf16[512,512]{1,0:T(8,128)(2,1)S(1)} %get-tuple-element.27.ge_hi, bf16[512,512]{1,0:T(8,128)(2,1)S(1)} %get-tuple-element.28.ge_lo, ...), custom_call_target="tpu_custom_call" | custom-call | flops 67108864 | bytes 4194304 | tf_op jit(solution)/shard_map/pallas_call | solution.py:533
  114.5 6.1 %all-to-all-done.3 = f16[16,72,128]{2,1,0:T(8,128)(2,1)S(1)} async-done(((f16[16,72,128]{2,1,0:T(8,128)(2,1)}), f16[16,72,128]{2,1,0:T(8,128)(2,1)S(1)}, u32[]{:S(2)}, u32[]{:S(2)}) %all-to-all-start.3) | async-done | bytes 294944 | tf_op jit(solution)/shard_map/all_to_all | solution.py:532
  120.6 0.1 bitcast_convert_fusion.2.parts_ref
  120.7 0.7 shard_map.96
  121.4 0.0 copy-done.1
  (2 shorter events, 0.0 us)
Async XLA Ops:
  0.6 19.1 %copy-start = (f32[4,4096]{1,0:T(4,128)S(1)}, f32[4,4096]{1,0:T(4,128)}, u32[]{:S(2)}) copy-start(f32[4,4096]{1,0:T(4,128)} %param.9) | copy-start | bytes 196612
  0.6 19.1 %copy-start.2 = (bf16[512,512]{1,0:T(8,128)(2,1)S(1)}, bf16[512,512]{1,0:T(8,128)(2,1)}, u32[]{:S(2)}) copy-start(bf16[512,512]{1,0:T(8,128)(2,1)} %grad_ref.3) | copy-start | bytes 1572868
  0.7 20.9 %copy-start.4 = (bf16[512,512]{1,0:T(8,128)(2,1)S(1)}, bf16[512,512]{1,0:T(8,128)(2,1)}, u32[]{:S(2)}) copy-start(bf16[512,512]{1,0:T(8,128)(2,1)} %x_ref.1) | copy-start | bytes 1572868
  0.7 20.9 %copy-start.5 = (f32[4,512]{1,0:T(4,128)S(1)}, f32[4,512]{1,0:T(4,128)}, u32[]{:S(2)}) copy-start(f32[4,512]{1,0:T(4,128)} %taps_ref.3) | copy-start | bytes 24580
  2.5 24.9 %all-to-all-start = ((bf16[16,16,512]{2,1,0:T(8,128)(2,1)}), bf16[16,16,512]{2,1,0:T(8,128)(2,1)S(1)}, u32[]{:S(2)}, u32[]{:S(2)}) async-start(bf16[16,16,512]{2,1,0:T(8,128)(2,1)} %shard_map.85), calls=%async_computation | async-start | bytes 524288 | tf_op jit(solution)/shard_map/all_to_all | solution.py:476
  16.6 4.9 %collective-permute-start = (bf16[16,512]{1,0:T(8,128)(2,1)S(1)}, bf16[16,512]{1,0:T(8,128)(2,1)S(1)}, u32[]{:S(2)}, u32[]{:S(2)}) collective-permute-start(bf16[16,512]{1,0:T(8,128)(2,1)S(1)} %slice.7), channel_id=1, source_target_pairs={{0,32},{32,64},{64,96},{96,128},{128,160},{160,192},{192,224},{224... | collective-permute-start | bytes 49160 | tf_op jit(solution)/shard_map/ppermute | solution.py:459
  19.8 0.7 copy-start.6
  27.4 8.5 %collective-permute-start.2 = (bf16[16,512]{1,0:T(8,128)(2,1)S(1)}, bf16[16,512]{1,0:T(8,128)(2,1)S(1)}, u32[]{:S(2)}, u32[]{:S(2)}) collective-permute-start(bf16[16,512]{1,0:T(8,128)(2,1)S(1)} %slice_bitcast_fusion), channel_id=1, source_target_pairs={{1,33},{33,65},{65,97},{97,129},{129,161},{161,193},{193,225},{225... | collective-permute-start | bytes 49160 | tf_op jit(solution)/shard_map/ppermute | solution.py:492
  31.5 4.4 %collective-permute-start.1 = (bf16[16,512]{1,0:T(8,128)(2,1)S(1)}, bf16[16,512]{1,0:T(8,128)(2,1)S(1)}, u32[]{:S(2)}, u32[]{:S(2)}) collective-permute-start(bf16[16,512]{1,0:T(8,128)(2,1)S(1)} %slice_bitcast_fusion), channel_id=1, source_target_pairs={{1,32},{33,64},{65,96},{97,128},{129,160},{161,192},{193,224},{225... | collective-permute-start | bytes 49160 | tf_op jit(solution)/shard_map/ppermute | solution.py:492
  63.4 18.3 %all-to-all-start.2 = ((f16[16,136,128]{2,1,0:T(8,128)(2,1)}), f16[16,136,128]{2,1,0:T(8,128)(2,1)}, u32[]{:S(2)}, u32[]{:S(2)}) async-start(f16[16,136,128]{2,1,0:T(8,128)(2,1)} %bitcast.5), calls=%async_computation.2 | async-start | bytes 1114112 | tf_op jit(solution)/shard_map/all_to_all | solution.py:510
  68.1 1.0 copy-start.3
  84.6 4.7 %collective-permute-start.3 = (f32[8,1024]{1,0:T(8,128)S(1)}, f32[8,1024]{1,0:T(8,128)S(1)}, u32[]{:S(2)}, u32[]{:S(2)}) collective-permute-start(f32[8,1024]{1,0:T(8,128)S(1)} %get-tuple-element.34), channel_id=1, source_target_pairs={{32,0},{64,32},{96,64},{128,96},{160,128},{192,160},{224,192},{256... | collective-permute-start | bytes 98312 | tf_op jit(solution)/shard_map/ppermute | solution.py:459
  90.3 9.8 %collective-permute-start.4 = (f32[16,16,512]{2,1,0:T(8,128)S(1)}, f32[16,16,512]{2,1,0:T(8,128)S(1)}, u32[]{:S(2)}, u32[]{:S(2)}) collective-permute-start(f32[16,16,512]{2,1,0:T(8,128)S(1)} %get-tuple-element.37), channel_id=1, source_target_pairs={{0,1},{1,0},{2,3},{3,2},{4,5},{5,4},{6,7},{7,6},{8,9},{9,8},{10,11... | collective-permute-start | bytes 1572872 | tf_op jit(solution)/shard_map/ppermute | solution.py:530
  101.1 19.6 %all-to-all-start.3 = ((f16[16,72,128]{2,1,0:T(8,128)(2,1)}), f16[16,72,128]{2,1,0:T(8,128)(2,1)S(1)}, u32[]{:S(2)}, u32[]{:S(2)}) async-start(f16[16,72,128]{2,1,0:T(8,128)(2,1)} %bitcast.8), calls=%async_computation.3 | async-start | bytes 589824 | tf_op jit(solution)/shard_map/all_to_all | solution.py:532
  108.2 13.2 %copy-start.1 = (f32[4,4096]{1,0:T(4,128)S(1)}, f32[4,4096]{1,0:T(4,128)}, u32[]{:S(2)}) copy-start(f32[4,4096]{1,0:T(4,128)} %param.9) | copy-start | bytes 196612

commit v4 on v3

--- a/solution.py
+++ b/solution.py
@@ -18,7 +18,7 @@
 HALO = 16
 LANES = 128
 META_ROWS = 8
-STORE = 28
+STORE = 26
 
 F32 = jnp.float32
 BF16 = jnp.bfloat16
@@ -178,16 +178,15 @@
 
 def pack_piece(first, second, out, place, logs):
     count = first.shape[0]
-    start = place * piece_rows(count)
     ups = [power_scale(first), power_scale(second)]
     for which, array in enumerate((first, second)):
         scaled = array * jnp.exp2(ups[which])
         for t in range(COLS // LANES):
-            at = start + (which * (COLS // LANES) + t) * count
-            out[at : at + count] = scaled[:, t * LANES : (t + 1) * LANES]
+            at = (which * (COLS // LANES) + t) * count
+            out[place, at : at + count] = scaled[:, t * LANES : (t + 1) * LANES]
     lane = lax.broadcasted_iota(jnp.int32, (META_ROWS, LANES), 1)
     meta = jnp.where(lane == 16, ups[0], jnp.where(lane == 17, ups[1], 0.0))
-    out[start + piece_rows(count) - META_ROWS : start + piece_rows(count)] = jnp.where(lane < 16, logs, meta)
+    out[place, piece_rows(count) - META_ROWS :] = jnp.where(lane < 16, logs, meta)
 
 
 def piece_rows(count):
@@ -195,11 +194,10 @@
 
 
 def unpack_piece(got, place, count, which):
-    start = place * piece_rows(count)
-    meta = got[start + piece_rows(count) - META_ROWS : start + piece_rows(count)]
+    meta = got[place, piece_rows(count) - META_ROWS :]
     down = jnp.exp2(-meta[0:1, 16 + which : 17 + which])
-    first = start + which * (COLS // LANES) * count
-    return [got[first + t * count : first + (t + 1) * count] * down for t in range(COLS // LANES)]
+    first = which * (COLS // LANES) * count
+    return [got[place, first + t * count : first + (t + 1) * count] * down for t in range(COLS // LANES)]
 
 
 def state_kernel(places, bc_ref, prev_0, prev_1, taps_ref, xf_hi, xf_lo, ge_hi, ge_lo, cum_ref, pack_ref, buf):
@@ -228,30 +226,27 @@
 def sum_kernel(keep_ref, got_ref, out_ref):
     own = keep_ref.shape[1]
     for owner in range(keep_ref.shape[0]):
-        start = owner * term_rows(own)
         terms = keep_ref[owner] + got_ref[owner]
         up = power_scale(terms)
         scaled = terms * jnp.exp2(up)
         for t in range(2 * STATE // LANES):
-            out_ref[start + t * own : start + (t + 1) * own] = scaled[:, t * LANES : (t + 1) * LANES]
-        end = start + term_rows(own)
-        out_ref[end - META_ROWS : end] = jnp.broadcast_to(up, (META_ROWS, LANES))
+            out_ref[owner, t * own : (t + 1) * own] = scaled[:, t * LANES : (t + 1) * LANES]
+        out_ref[owner, term_rows(own) - META_ROWS :] = jnp.broadcast_to(up, (META_ROWS, LANES))
 
 
 def fold_kernel(parts_ref, out_ref):
     own = out_ref.shape[0]
     groups = out_ref.shape[1] // (2 * STATE)
-    fan = parts_ref.shape[0] // term_rows(own) // groups
+    fan = parts_ref.shape[0] // groups
     for group in range(groups):
         downs = []
         for one in range(fan):
-            end = (group * fan + one + 1) * term_rows(own)
-            downs.append(jnp.exp2(-parts_ref[end - META_ROWS : end - META_ROWS + 1]))
+            end = term_rows(own)
+            downs.append(jnp.exp2(-parts_ref[group * fan + one, end - META_ROWS : end - META_ROWS + 1]))
         for t in range(2 * STATE // LANES):
             total = jnp.zeros((own, LANES), F32)
             for one in range(fan):
-                start = (group * fan + one) * term_rows(own) + t * own
-                total = total + parts_ref[start : start + own] * downs[one]
+                total = total + parts_ref[group * fan + one, t * own : (t + 1) * own] * downs[one]
             at = group * 2 * STATE + t * LANES
             out_ref[:, at : at + LANES] = total
 
@@ -263,8 +258,7 @@
     tiles = COLS // LANES
     decays = []
     for p in range(places):
-        end = (p + 1) * piece_rows(count)
-        meta = got_ref[end - META_ROWS : end]
+        meta = got_ref[p, piece_rows(count) - META_ROWS :]
         logs = meta + pltpu.roll(meta, LANES - 8, 1)
         decay = jnp.where(lane < 8, jnp.exp(jnp.minimum(logs, 0.0)), 0.0)
         decays.append(widen(decay, spread)[0:1])
@@ -279,7 +273,38 @@
         going = decays[p] * going + jnp.concatenate(unpack_piece(got_ref, p, count, 1), axis=1)
 
 
-def block_kernel(features, grad_ref, bc_ref, prev_0, prev_1, taps_ref, cum_ref, cumt_ref, store,
+def diagonal(b, act_ref, grad_ref, cum_ref, cumt_ref, bc_hi, bc_lo, dx_ref, dbc_ref, dlog_ref):
+    row, col = row_col()
+    causal = row <= col
+    later = jnp.where(col >= row, 1.0, 0.0).astype(BF16)
+    part = slice(b * BLOCK, (b + 1) * BLOCK)
+    keys = (bc_hi[part, 0:STATE], bc_lo[part, 0:STATE])
+    queries = (bc_hi[part, STATE:], bc_lo[part, STATE:])
+    scores = dot3(keys, queries, NT)
+    total = jnp.zeros((BLOCK, BLOCK), F32)
+    across, down = [], []
+    for h in range(HEADS):
+        cols = slice(h * HEAD_DIM, (h + 1) * HEAD_DIM)
+        gap = cumt_ref[b, h : h + 1, :] - cum_ref[part, h : h + 1]
+        mixing = jnp.where(causal, jnp.exp(jnp.where(causal, gap, 0.0)), 0.0)
+        grads = grad_ref[part, cols]
+        values = split2(act_ref[part, cols])
+        pairs = mixing * (mul(values[0], grads, NT) + mul(values[1], grads, NT))
+        total = total + pairs
+        weights = pairs * scores
+        across.append(jnp.sum(weights, axis=0, keepdims=True))
+        down.append(jnp.sum(weights, axis=1, keepdims=True))
+        mixed = split2(mixing * scores)
+        dx_ref[part, cols] = mul(mixed[0], grads, NN) + mul(mixed[1], grads, NN)
+    pairs = split2(total)
+    dbc_ref[part, 0:STATE] = dot3(pairs, queries, NN)
+    dbc_ref[part, STATE:] = dot3(pairs, keys, TN)
+    dlog_ref[part, 0:HEADS] = exact_left(later, jnp.concatenate(across, axis=0), NT) - exact_left(
+        later, jnp.concatenate(down, axis=1), NN
+    )
+
+
+def first_kernel(features, grad_ref, bc_ref, prev_0, prev_1, taps_ref, cum_ref, cumt_ref, store,
                  act_ref, dx_ref, dbc_ref, slope_ref, bc_act, dlog_ref, bc_hi, bc_lo, buf, sems):
     coming = begin(sems, (features.at[0], act_ref))
     pre = group_conv(buf, (prev_0, prev_1), bc_ref, taps_ref)
@@ -289,37 +314,30 @@
     leaving = begin(sems, (slope_ref, store.at[2]), (bc_act, store.at[3]), first=1)
     bc_hi[...], bc_lo[...] = split2(bc_act[...])
     finish(coming)
+    diagonal(0, act_ref, grad_ref, cum_ref, cumt_ref, bc_hi, bc_lo, dx_ref, dbc_ref, dlog_ref)
+    rows = slice(0, BLOCK)
+    leaving += begin(
+        sems, (dx_ref.at[rows], store.at[0, rows]), (dbc_ref.at[rows], store.at[1, rows]),
+        (dlog_ref.at[rows], store.at[4, rows, 0:LANES]), first=3,
+    )
+    finish(leaving)
+
+
+def second_kernel(features, early, grad_ref, cum_ref, cumt_ref, store,
+                  act_ref, dx_ref, dbc_ref, bc_act, dlog_ref, bc_hi, bc_lo, sems):
+    rows = slice(0, BLOCK)
+    coming = begin(
+        sems, (features.at[0], act_ref), (early.at[3], bc_act), (early.at[0, rows], dx_ref.at[rows]),
+        (early.at[1, rows], dbc_ref.at[rows]), (early.at[4, rows, 0:LANES], dlog_ref.at[rows]),
+    )
+    leaving = begin(sems, (early.at[2], store.at[2]), (early.at[3], store.at[3]), first=5)
+    finish(coming)
+    bc_hi[...], bc_lo[...] = split2(bc_act[...])
+    diagonal(1, act_ref, grad_ref, cum_ref, cumt_ref, bc_hi, bc_lo, dx_ref, dbc_ref, dlog_ref)
     row, col = row_col()
-    causal = row <= col
     later = jnp.where(col >= row, 1.0, 0.0).astype(BF16)
     before = jnp.where(col < row, 1.0, 0.0).astype(BF16)
     spread = expander(LANES)
-    for b in range(BLOCKS):
-        part = slice(b * BLOCK, (b + 1) * BLOCK)
-        keys = (bc_hi[part, 0:STATE], bc_lo[part, 0:STATE])
-        queries = (bc_hi[part, STATE:], bc_lo[part, STATE:])
-        scores = dot3(keys, queries, NT)
-        total = jnp.zeros((BLOCK, BLOCK), F32)
-        across, down = [], []
-        for h in range(HEADS):
-            cols = slice(h * HEAD_DIM, (h + 1) * HEAD_DIM)
-            gap = cumt_ref[b, h : h + 1, :] - cum_ref[part, h : h + 1]
-            mixing = jnp.where(causal, jnp.exp(jnp.where(causal, gap, 0.0)), 0.0)
-            grads = grad_ref[part, cols]
-            values = split2(act_ref[part, cols])
-            pairs = mixing * (mul(values[0], grads, NT) + mul(values[1], grads, NT))
-            total = total + pairs
-            weights = pairs * scores
-            across.append(jnp.sum(weights, axis=0, keepdims=True))
-            down.append(jnp.sum(weights, axis=1, keepdims=True))
-            mixed = split2(mixing * scores)
-            dx_ref[part, cols] = mul(mixed[0], grads, NN) + mul(mixed[1], grads, NN)
-        pairs = split2(total)
-        dbc_ref[part, 0:STATE] = dot3(pairs, queries, NN)
-        dbc_ref[part, STATE:] = dot3(pairs, keys, TN)
-        dlog_ref[part, 0:HEADS] = exact_left(later, jnp.concatenate(across, axis=0), NT) - exact_left(
-            later, jnp.concatenate(down, axis=1), NN
-        )
     first, second = slice(0, BLOCK), slice(BLOCK, 2 * BLOCK)
     last = cum_ref[BLOCK - 1 : BLOCK]
     fade = widen(jnp.exp(last - cum_ref[first]), spread)
@@ -338,7 +356,7 @@
     dlog_ref[first, 0:HEADS] += exact_left(before, head_sums(faded * pulls, spread), NN)[:, 0:HEADS]
     dlog_ref[second, 0:HEADS] += exact_left(later, head_sums(grown * reads, spread), NN)[:, 0:HEADS]
     leaving += begin(
-        sems, (dx_ref, store.at[0]), (dbc_ref, store.at[1]), (dlog_ref, store.at[4, :, 0:LANES]), first=3
+        sems, (dx_ref, store.at[0]), (dbc_ref, store.at[1]), (dlog_ref, store.at[4, :, 0:LANES]), first=7
     )
     finish(leaving)
 
@@ -435,7 +453,7 @@
     glog_ref[...] = jnp.transpose(found)[0:HEADS]
 
 
-def call(kernel, outs, scratch=(), hbm_in=(), hbm_out=(), smem=(), count=0, sems=0, vmem=40, flops=1 << 26, size=1 << 22):
+def call(kernel, outs, scratch=(), hbm_in=(), hbm_out=(), smem=(), fused=(), count=0, sems=0, vmem=40, flops=1 << 26, size=1 << 22):
     def place(i, far):
         return pl.BlockSpec(memory_space=pltpu.SMEM if i in smem else pltpu.HBM if i in far else pltpu.VMEM)
 
@@ -448,7 +466,10 @@
         ],
         scratch_shapes=[pltpu.VMEM(shape, dtype) for shape, dtype in scratch]
         + ([pltpu.SemaphoreType.DMA((sems,))] if sems else []),
-        compiler_params=pltpu.CompilerParams(vmem_limit_bytes=vmem * 2**20),
+        compiler_params=pltpu.CompilerParams(
+            vmem_limit_bytes=vmem * 2**20,
+            allow_input_fusion=[i in fused for i in range(count)] if fused else None,
+        ),
         cost_estimate=pl.CostEstimate(flops=flops, bytes_accessed=size, transcendentals=0),
     )
 
@@ -495,18 +516,24 @@
         for to in (0, 1)
     ]
     bc_rows = lax.all_gather(mine, "core")
-    packed = (places * piece_rows(STATE // places), LANES)
+    packed = (places, piece_rows(STATE // places), LANES)
     (sent,) = call(functools.partial(state_kernel, places), [(packed, F32)], [padded], count=9)(
         bc_rows, *bc_prev, taps_bc, *scaled, cum
     )
     got = lax.all_to_all(sent.astype(jnp.float16), CTX, 0, 0, tiled=True)
+    (early,) = call(
+        first_kernel, [(store, F32)],
+        [(wide, F32)] * 5 + [((ROWS, LANES), F32)] + [(wide, BF16)] * 2 + [padded],
+        hbm_in=(0,), hbm_out=(0,), count=8, sems=6, flops=1 << 32,
+    )(features, grad_y, bc_rows, *bc_prev, taps_bc, cum, cumt)
+    got, early = lax.optimization_barrier((got, early))
+    (back,) = call(functools.partial(scan_kernel, places), [(packed, F32)], fused=(0,), count=1)(got.astype(F32))
+    early, back = lax.optimization_barrier((early, back))
     (blocks,) = call(
-        block_kernel, [(store, F32)],
-        [(wide, F32)] * 5 + [((ROWS, LANES), F32)] + [(wide, BF16)] * 2 + [padded],
-        hbm_in=(0,), hbm_out=(0,), count=8, sems=6,
-    )(features, grad_y, bc_rows, *bc_prev, taps_bc, cum, cumt)
-
-    (back,) = call(functools.partial(scan_kernel, places), [(packed, F32)], count=1)(got.astype(F32))
+        second_kernel, [(store, F32)],
+        [(wide, F32)] * 4 + [((ROWS, LANES), F32)] + [(wide, BF16)] * 2,
+        hbm_in=(0, 1), hbm_out=(0,), count=5, sems=10, flops=1 << 32,
+    )(features, early, grad_y, cum, cumt)
     carried = lax.all_to_all(back.astype(jnp.float16), CTX, 0, 0, tiled=True).astype(F32)
 
     half = (STATE, COLS)
@@ -516,7 +543,7 @@
         functools.partial(open_kernel, places),
         [((2 * STORE,) + wide, BF16), ((8, COLS), F32), ((8, COLS + 2 * STATE), F32)],
         [(half, F32)] * 2 + [pair] + [(top, F32)] * 5,
-        hbm_in=(6, 7), hbm_out=(0,), count=8, sems=6,
+        hbm_in=(6, 7), hbm_out=(0,), fused=(0,), count=8, sems=6,
     )(carried, *scaled, cum, features, blocks)
     halo = shifted(first, -1)
     (gbc,) = call(
@@ -526,7 +553,7 @@
     keep, give = call(
         functools.partial(grad_bc_kernel, own), [(piece, F32)] * 2, [padded, (wide, F32)], smem=(0,), count=4
     )(core.reshape(1), gbc, halo, taps_bc)
-    (summed,) = call(sum_kernel, [((owners * term_rows(own), LANES), F32)], count=2)(
+    (summed,) = call(sum_kernel, [((owners, term_rows(own), LANES), F32)], count=2)(
         keep, lax.ppermute(give, "core", swap)
     )
     parts = lax.all_to_all(summed.astype(jnp.float16), ("x", "zh"), 0, 0, tiled=True).astype(F32)
@@ -536,7 +563,7 @@
         [padded, pair] + [(wide, F32)] * 3 + [((ROWS, LANES), F32)],
         hbm_in=(5, 6, 7), count=11, sems=5,
     )(*scaled, cum, features, blocks, states, both, halo, conv_x)
-    (grad_bc,) = call(fold_kernel, [((own, groups * 2 * STATE), F32)], count=1)(parts)
+    (grad_bc,) = call(fold_kernel, [((own, groups * 2 * STATE), F32)], fused=(0,), count=1)(parts)
     return grad_x, grad_bc, glog.T
 
 

time: 122 us -> 178 us (1.46); the launches traced: 121 us -> 175 us
  Pallas kernels: 31 us -> 90.9 us
  blocking collectives: 25.6 us -> 2.18 us
  starting transfers between devices: 44.2 us -> 52.1 us
  local copies, waits for them, and re-layouts: 2.52 us -> 7.11 us
  waiting for transfers between devices: 14.2 us -> 17 us
  other arithmetic: 3.02 us -> 4.81 us
    pallas_call x4 -> x5, Pallas kernels: 11.5 us -> 71.4 us  [the longest x1 64.7 us: per_device(): call(second_kernel, [(store, F32)], [(wide, F32)] * 4 + [((ROWS, LANES),...]
    all_to_all x1 -> x0, blocking collectives: 23.4 us -> none  [per_device(): got = lax.all_to_all(sent.astype(jnp.float16), CTX, 0, 0, tiled=True)]
    all_to_all x0 -> x1, waiting for transfers between devices: none -> 8.5 us  [per_device(): got = lax.all_to_all(sent.astype(jnp.float16), CTX, 0, 0, tiled=True)]
    all_to_all x0 -> x1, starting transfers between devices: none -> 7.76 us  [per_device(): got = lax.all_to_all(sent.astype(jnp.float16), CTX, 0, 0, tiled=True)]
    unnamed x14 -> x22, local copies, waits for them, and re-layouts: 1.78 us -> 6.38 us
    all_to_all x1, waiting for transfers between devices: 3.2 us -> 0.01 us  [per_device(): lax.all_to_all(back.astype(jnp.float16), CTX, 0, 0, tiled=True).astype(F32)]
    all_to_all x1, waiting for transfers between devices: 2.45 us -> 0.01 us  [per_device(): mine = lax.all_to_all(spread, ('x', 'zh'), 0, 0, tiled=True)]
  transfers between devices with their start and end apart: 8 -> 9, of which waited for: 5 -> 4; matrix products, arithmetic and copies ran while one was open for 1% -> 0% of each run, Pallas kernels for 19% -> 47%
where the time goes in v4:
time: 178 us; the launch traced here: 175 us
  Pallas kernels  90.9 us (51%)
  starting transfers between devices  52.1 us (29%)
  waiting for transfers between devices  17 us (10%)
  local copies, waits for them, and re-layouts  7.11 us (4%)
  other arithmetic  4.81 us (3%)
  blocking collectives  2.18 us (1%)
    pallas_call x1, Pallas kernels, per_device(): call(second_kernel, [(store, F32)], [(wide, F32)] * 4 + [((ROWS, LANES),...  64.7 us
    all_to_all x1, starting transfers between devices, per_device(): mine = lax.all_to_all(spread, ('x', 'zh'), 0, 0, tiled=True)  13.4 us
    all_to_all x1, starting transfers between devices, per_device(): lax.all_to_all(summed.astype(jnp.float16), ('x', 'zh'), 0, 0, tiled=True)  8.93 us
    all_to_all x1, waiting for transfers between devices, per_device(): got = lax.all_to_all(sent.astype(jnp.float16), CTX, 0, 0, tiled=True)  8.5 us
    all_to_all x1, starting transfers between devices, per_device(): got = lax.all_to_all(sent.astype(jnp.float16), CTX, 0, 0, tiled=True)  7.76 us
    ppermute x1, starting transfers between devices, per_device(): lax.ppermute(give, 'core', swap)  6.97 us
    unnamed x22, local copies, waits for them, and re-layouts  6.38 us
    pallas_call x1, Pallas kernels, per_device(): call(carry_kernel, [(wide, BF16), ((HEADS, ROWS), F32)], [padded, pair] +...  6.22 us
  transfers between devices with their start and end apart: 9, of which 4 were waited for; matrix products, arithmetic and copies ran while one was open for 0% of the time, Pallas kernels for 47%

profile of v4, /device:TPU:1, one launch (start us, length us, event | category | flops | bytes accessed | tf_op | source)
XLA Modules:
  0.0 174.9 jit_solution(9926125566801090354)
XLA Ops:
  0.6 0.0 copy-start
  0.6 1.8 %shard_map.85 = bf16[16,16,512]{2,1,0:T(8,128)(2,1)} custom-call(bf16[16,4096]{1,0:T(8,128)(2,1)} %rows_hbm.1), custom_call_target="tpu_custom_call" | custom-call | flops 67108864 | bytes 4194304 | tf_op jit(solution)/shard_map/pallas_call | solution.py:494
  2.4 13.4 %all-to-all-start = ((bf16[16,16,512]{2,1,0:T(8,128)(2,1)}), bf16[16,16,512]{2,1,0:T(8,128)(2,1)S(1)}, u32[]{:S(2)}, u32[]{:S(2)}) async-start(bf16[16,16,512]{2,1,0:T(8,128)(2,1)} %shard_map.85), calls=%async_computation | async-start | bytes 524288 | tf_op jit(solution)/shard_map/all_to_all | solution.py:497
  15.9 0.7 slice.7
  16.6 3.1 %collective-permute-start = (bf16[16,512]{1,0:T(8,128)(2,1)S(1)}, bf16[16,512]{1,0:T(8,128)(2,1)S(1)}, u32[]{:S(2)}, u32[]{:S(2)}) collective-permute-start(bf16[16,512]{1,0:T(8,128)(2,1)S(1)} %slice.7), channel_id=1, source_target_pairs={{0,32},{32,64},{64,96},{96,128},{128,160},{160,192},{192,224},{224... | collective-permute-start | bytes 49160 | tf_op jit(solution)/shard_map/ppermute | solution.py:480
  19.7 0.0 copy-done
  19.7 0.0 copy-start.2
  19.7 1.0 copy-done.2
  20.8 0.0 copy-start.10
  20.8 0.7 copy-done.10
  21.5 1.1 shard_map.86
  22.5 0.0 collective-permute-done.prev_ref
  22.6 0.0 copy-start.7
  22.6 1.0 copy-done.7
  23.6 0.0 copy-start.8
  23.6 0.7 copy-done.8
  24.3 3.4 %shard_map.87 = (f32[26,512,512]{2,1,0:T(8,128)}, bf16[512,512]{1,0:T(8,128)(2,1)S(1)}, bf16[512,512]{1,0:T(8,128)(2,1)S(1)}) custom-call(bf16[512,512]{1,0:T(8,128)(2,1)S(1)} %copy-done.7, bf16[16,512]{1,0:T(8,128)(2,1)S(1)} %collective-permute-done.prev_ref, f32[4,512]{1,0:T(4,128)S(1)} %copy-done.8, f32[512,128]{1,0:T(8,128)S(1)} %get-tuple-element.25.cum_ref), custom_call_target="tpu_custom_call" | custom-call | flops 67108864 | bytes 4194304 | tf_op jit(solution)/shard_map/pallas_call | solution.py:505
  27.7 0.0 all-to-all-done
  27.7 3.8 %collective-permute-start.2 = (bf16[16,512]{1,0:T(8,128)(2,1)S(1)}, bf16[16,512]{1,0:T(8,128)(2,1)S(1)}, u32[]{:S(2)}, u32[]{:S(2)}) collective-permute-start(bf16[16,512]{1,0:T(8,128)(2,1)S(1)} %slice_bitcast_fusion), channel_id=1, source_target_pairs={{1,33},{33,65},{65,97},{97,129},{129,161},{161,193},{193,225},{225... | collective-permute-start | bytes 49160 | tf_op jit(solution)/shard_map/ppermute | solution.py:513
  31.5 2.2 %collective-permute-start.1 = (bf16[16,512]{1,0:T(8,128)(2,1)S(1)}, bf16[16,512]{1,0:T(8,128)(2,1)S(1)}, u32[]{:S(2)}, u32[]{:S(2)}) collective-permute-start(bf16[16,512]{1,0:T(8,128)(2,1)S(1)} %slice_bitcast_fusion), channel_id=1, source_target_pairs={{1,32},{33,64},{65,96},{97,128},{129,160},{161,192},{193,224},{225... | collective-permute-start | bytes 49160 | tf_op jit(solution)/shard_map/ppermute | solution.py:513
  33.7 2.2 %all-gather = bf16[32,16,512]{2,1,0:T(8,128)(2,1)S(1)} all-gather(bf16[16,16,512]{2,1,0:T(8,128)(2,1)S(1)} %all-to-all-done), channel_id=2, replica_groups=mesh['y'=8,'zl'=2,'x'=4,'zh'=4,'core'=2] {'core'}, dimensions={0}, use_global_device_ids=true | all-gather | bytes 786432 | tf_op jit(solution)/shard_map/all_gather | solution.py:518
  35.8 0.0 collective-permute-done.2.prev_1
  35.8 0.0 collective-permute-done.1.prev_0
  35.8 1.8 %shard_map.88 = f32[16,136,128]{2,1,0:T(8,128)S(1)} custom-call(bf16[2,16,16,512]{3,2,1,0:T(8,128)(2,1)S(1)} %bitcast.6, bf16[16,512]{1,0:T(8,128)(2,1)S(1)} %collective-permute-done.1.prev_0, bf16[16,512]{1,0:T(8,128)(2,1)S(1)} %collective-permute-done.2.prev_1, f32[4,512]{1,0:T(4,128)S(1)} %constant_dynamic-slice_fusion.taps_ref, ...), custom_call_target="tpu_custom_call" | custom-call | flops 67108864 | bytes 4194304 | tf_op jit(solution)/shard_map/pallas_call | solution.py:520
  37.7 0.0 copy-start.5
  37.7 0.8 copy-done.5
  38.4 0.9 convert_element_type.18
  39.3 7.8 %all-to-all-start.1 = ((f16[16,136,128]{2,1,0:T(8,128)(2,1)}), f16[16,136,128]{2,1,0:T(8,128)(2,1)}, u32[]{:S(2)}, u32[]{:S(2)}) async-start(f16[16,136,128]{2,1,0:T(8,128)(2,1)} %convert_element_type.18), calls=%async_computation.1 | async-start | bytes 1114112 | tf_op jit(solution)/shard_map/all_to_all | solution.py:523
  47.1 0.0 copy-start.3
  47.1 1.0 copy-done.3
  48.1 0.0 copy-start.6
  48.1 1.0 copy-done.6
  49.2 0.0 copy-start.4
  49.2 4.6 %shard_map.89.early = f32[26,512,512]{2,1,0:T(8,128)} custom-call(f32[26,512,512]{2,1,0:T(8,128)} %get-tuple-element.33.features, bf16[512,512]{1,0:T(8,128)(2,1)S(1)} %copy-done.3, bf16[2,16,16,512]{3,2,1,0:T(8,128)(2,1)S(1)} %bitcast.7, bf16[16,512]{1,0:T(8,128)(2,1)S(1)} %collective-permute-done.1.prev_0, ...), custom_call_target="tpu_custom_call" | custom-call | flops 4294967296 | bytes 4194304 | tf_op jit(solution)/shard_map/pallas_call | solution.py:524
  53.8 8.5 %all-to-all-done.1 = f16[16,136,128]{2,1,0:T(8,128)(2,1)} async-done(((f16[16,136,128]{2,1,0:T(8,128)(2,1)}), f16[16,136,128]{2,1,0:T(8,128)(2,1)}, u32[]{:S(2)}, u32[]{:S(2)}) %all-to-all-start.1) | async-done | bytes 557088 | tf_op jit(solution)/shard_map/all_to_all | solution.py:523
  62.3 1.1 convert_element_type.19.got_ref
  63.4 1.2 shard_map.90
  64.6 0.9 convert_element_type.20
  65.5 4.6 %all-to-all-start.2 = ((f16[16,136,128]{2,1,0:T(8,128)(2,1)}), f16[16,136,128]{2,1,0:T(8,128)(2,1)}, u32[]{:S(2)}, u32[]{:S(2)}) async-start(f16[16,136,128]{2,1,0:T(8,128)(2,1)} %convert_element_type.20), calls=%async_computation.2 | async-start | bytes 1114112 | tf_op jit(solution)/shard_map/all_to_all | solution.py:537
  70.1 0.0 copy-done.4
  70.2 64.7 %shard_map.91.blocks = f32[26,512,512]{2,1,0:T(8,128)} custom-call(f32[26,512,512]{2,1,0:T(8,128)} %get-tuple-element.33.features, f32[26,512,512]{2,1,0:T(8,128)} %shard_map.89.early, bf16[512,512]{1,0:T(8,128)(2,1)S(1)} %copy-done.4, f32[512,128]{1,0:T(8,128)S(1)} %get-tuple-element.25.cum_ref, f32[2,8,256]{2,1,0:T(8,128)S(1)} %get-tuple-element.35.cumt_ref), custom_call_target="tpu_custom_call" | custom-call | flops 4294967296 | bytes 4194304 | tf_op jit(solution)/shard_map/pallas_call | solution.py:532
  134.9 0.0 all-to-all-done.2
  134.9 1.1 convert_element_type.21.got_ref
  136.0 1.8 %shard_map.92 = (bf16[52,512,512]{2,1,0:T(8,128)(2,1)}, f32[8,512]{1,0:T(8,128)S(1)}, f32[8,1024]{1,0:T(8,128)S(1)}) custom-call(f32[16,136,128]{2,1,0:T(8,128)S(1)} %convert_element_type.21.got_ref, bf16[512,512]{1,0:T(8,128)(2,1)S(1)} %get-tuple-element.29.xf_hi, bf16[512,512]{1,0:T(8,128)(2,1)S(1)} %get-tuple-element.30.xf_lo, ...), custom_call_target="tpu_custom_call" | custom-call | flops 67108864 | bytes 4194304 | tf_op jit(solution)/shard_map/pallas_call | solution.py:542
  137.8 1.3 collective-permute-start.3
  139.1 0.0 copy-start.9
  139.1 2.4 %shard_map.94.rows_ref = f32[512,512]{1,0:T(8,128)S(1)} custom-call(bf16[512,512]{1,0:T(8,128)(2,1)S(1)} %get-tuple-element.29.xf_hi, bf16[512,512]{1,0:T(8,128)(2,1)S(1)} %get-tuple-element.30.xf_lo, bf16[512,512]{1,0:T(8,128)(2,1)S(1)} %get-tuple-element.31.ge_hi, bf16[512,512]{1,0:T(8,128)(2,1)S(1)} %get-tuple-element.32.ge_lo, ...), custom_call_target="tpu_custom_call" | custom-call | flops 67108864 | bytes 4194304 | tf_op jit(solution)/shard_map/pallas_call | solution.py:549
  141.6 0.9 collective-permute-done.3.halo_ref
  142.5 1.0 shard_map.95
  143.5 7.0 %collective-permute-start.4 = (f32[16,16,512]{2,1,0:T(8,128)S(1)}, f32[16,16,512]{2,1,0:T(8,128)S(1)}, u32[]{:S(2)}, u32[]{:S(2)}) collective-permute-start(f32[16,16,512]{2,1,0:T(8,128)S(1)} %get-tuple-element.45), channel_id=1, source_target_pairs={{0,1},{1,0},{2,3},{3,2},{4,5},{5,4},{6,7},{7,6},{8,9},{9,8},{10,11... | collective-permute-start | bytes 1572872 | tf_op jit(solution)/shard_map/ppermute | solution.py:557
  150.5 1.5 collective-permute-done.4.got_ref
  152.0 0.2 shard_map.96
  152.1 0.8 convert_element_type.22
  152.9 8.9 %all-to-all-start.3 = ((f16[16,72,128]{2,1,0:T(8,128)(2,1)}), f16[16,72,128]{2,1,0:T(8,128)(2,1)S(1)}, u32[]{:S(2)}, u32[]{:S(2)}) async-start(f16[16,72,128]{2,1,0:T(8,128)(2,1)} %convert_element_type.22), calls=%async_computation.3 | async-start | bytes 589824 | tf_op jit(solution)/shard_map/all_to_all | solution.py:559
  161.8 0.0 copy-start.1
  161.9 0.0 copy-done.9
  161.9 6.2 %shard_map.93 = (bf16[512,512]{1,0:T(8,128)(2,1)}, f32[8,512]{1,0:T(8,128)}) custom-call(bf16[512,512]{1,0:T(8,128)(2,1)S(1)} %get-tuple-element.29.xf_hi, bf16[512,512]{1,0:T(8,128)(2,1)S(1)} %get-tuple-element.30.xf_lo, bf16[512,512]{1,0:T(8,128)(2,1)S(1)} %get-tuple-element.31.ge_hi, bf16[512,512]{1,0:T(8,128)(2,1)S(1)} %get-tuple-element.32.ge_lo, ...), custom_call_target="tpu_custom_call" | custom-call | flops 67108864 | bytes 4194304 | tf_op jit(solution)/shard_map/pallas_call | solution.py:560
  168.1 6.0 %all-to-all-done.3 = f16[16,72,128]{2,1,0:T(8,128)(2,1)S(1)} async-done(((f16[16,72,128]{2,1,0:T(8,128)(2,1)}), f16[16,72,128]{2,1,0:T(8,128)(2,1)S(1)}, u32[]{:S(2)}, u32[]{:S(2)}) %all-to-all-start.3) | async-done | bytes 294944 | tf_op jit(solution)/shard_map/all_to_all | solution.py:559
  174.2 0.7 shard_map.97
  174.9 0.0 copy-done.1
  (3 shorter events, 0.1 us)
Async XLA Ops:
  0.6 19.1 %copy-start = (f32[4,4096]{1,0:T(4,128)S(1)}, f32[4,4096]{1,0:T(4,128)}, u32[]{:S(2)}) copy-start(f32[4,4096]{1,0:T(4,128)} %param.9) | copy-start | bytes 196612
  2.4 25.3 %all-to-all-start = ((bf16[16,16,512]{2,1,0:T(8,128)(2,1)}), bf16[16,16,512]{2,1,0:T(8,128)(2,1)S(1)}, u32[]{:S(2)}, u32[]{:S(2)}) async-start(bf16[16,16,512]{2,1,0:T(8,128)(2,1)} %shard_map.85), calls=%async_computation | async-start | bytes 524288 | tf_op jit(solution)/shard_map/all_to_all | solution.py:497
  16.6 6.0 %collective-permute-start = (bf16[16,512]{1,0:T(8,128)(2,1)S(1)}, bf16[16,512]{1,0:T(8,128)(2,1)S(1)}, u32[]{:S(2)}, u32[]{:S(2)}) collective-permute-start(bf16[16,512]{1,0:T(8,128)(2,1)S(1)} %slice.7), channel_id=1, source_target_pairs={{0,32},{32,64},{64,96},{96,128},{128,160},{160,192},{192,224},{224... | collective-permute-start | bytes 49160 | tf_op jit(solution)/shard_map/ppermute | solution.py:480
  19.7 1.0 copy-start.2
  20.8 0.7 copy-start.10
  22.6 1.0 copy-start.7
  23.6 0.7 copy-start.8
  27.7 8.1 %collective-permute-start.2 = (bf16[16,512]{1,0:T(8,128)(2,1)S(1)}, bf16[16,512]{1,0:T(8,128)(2,1)S(1)}, u32[]{:S(2)}, u32[]{:S(2)}) collective-permute-start(bf16[16,512]{1,0:T(8,128)(2,1)S(1)} %slice_bitcast_fusion), channel_id=1, source_target_pairs={{1,33},{33,65},{65,97},{97,129},{129,161},{161,193},{193,225},{225... | collective-permute-start | bytes 49160 | tf_op jit(solution)/shard_map/ppermute | solution.py:513
  31.5 4.4 %collective-permute-start.1 = (bf16[16,512]{1,0:T(8,128)(2,1)S(1)}, bf16[16,512]{1,0:T(8,128)(2,1)S(1)}, u32[]{:S(2)}, u32[]{:S(2)}) collective-permute-start(bf16[16,512]{1,0:T(8,128)(2,1)S(1)} %slice_bitcast_fusion), channel_id=1, source_target_pairs={{1,32},{33,64},{65,96},{97,128},{129,160},{161,192},{193,224},{225... | collective-permute-start | bytes 49160 | tf_op jit(solution)/shard_map/ppermute | solution.py:513
  37.7 0.8 copy-start.5
  39.3 23.0 %all-to-all-start.1 = ((f16[16,136,128]{2,1,0:T(8,128)(2,1)}), f16[16,136,128]{2,1,0:T(8,128)(2,1)}, u32[]{:S(2)}, u32[]{:S(2)}) async-start(f16[16,136,128]{2,1,0:T(8,128)(2,1)} %convert_element_type.18), calls=%async_computation.1 | async-start | bytes 1114112 | tf_op jit(solution)/shard_map/all_to_all | solution.py:523
  47.1 1.0 copy-start.3
  48.1 1.0 copy-start.6
  49.2 21.0 %copy-start.4 = (bf16[512,512]{1,0:T(8,128)(2,1)S(1)}, bf16[512,512]{1,0:T(8,128)(2,1)}, u32[]{:S(2)}) copy-start(bf16[512,512]{1,0:T(8,128)(2,1)} %grad_ref.5) | copy-start | bytes 1572868
  65.5 69.4 %all-to-all-start.2 = ((f16[16,136,128]{2,1,0:T(8,128)(2,1)}), f16[16,136,128]{2,1,0:T(8,128)(2,1)}, u32[]{:S(2)}, u32[]{:S(2)}) async-start(f16[16,136,128]{2,1,0:T(8,128)(2,1)} %convert_element_type.20), calls=%async_computation.2 | async-start | bytes 1114112 | tf_op jit(solution)/shard_map/all_to_all | solution.py:537
  137.8 4.7 %collective-permute-start.3 = (f32[8,1024]{1,0:T(8,128)S(1)}, f32[8,1024]{1,0:T(8,128)S(1)}, u32[]{:S(2)}, u32[]{:S(2)}) collective-permute-start(f32[8,1024]{1,0:T(8,128)S(1)} %get-tuple-element.42), channel_id=1, source_target_pairs={{32,0},{64,32},{96,64},{128,96},{160,128},{192,160},{224,192},{256... | collective-permute-start | bytes 98312 | tf_op jit(solution)/shard_map/ppermute | solution.py:480
  139.1 22.7 %copy-start.9 = (f32[4,512]{1,0:T(4,128)S(1)}, f32[4,512]{1,0:T(4,128)}, u32[]{:S(2)}) copy-start(f32[4,512]{1,0:T(4,128)} %taps_ref.3) | copy-start | bytes 24580
  143.5 8.5 %collective-permute-start.4 = (f32[16,16,512]{2,1,0:T(8,128)S(1)}, f32[16,16,512]{2,1,0:T(8,128)S(1)}, u32[]{:S(2)}, u32[]{:S(2)}) collective-permute-start(f32[16,16,512]{2,1,0:T(8,128)S(1)} %get-tuple-element.45), channel_id=1, source_target_pairs={{0,1},{1,0},{2,3},{3,2},{4,5},{5,4},{6,7},{7,6},{8,9},{9,8},{10,11... | collective-permute-start | bytes 1572872 | tf_op jit(solution)/shard_map/ppermute | solution.py:557
  152.9 21.2 %all-to-all-start.3 = ((f16[16,72,128]{2,1,0:T(8,128)(2,1)}), f16[16,72,128]{2,1,0:T(8,128)(2,1)S(1)}, u32[]{:S(2)}, u32[]{:S(2)}) async-start(f16[16,72,128]{2,1,0:T(8,128)(2,1)} %convert_element_type.22), calls=%async_computation.3 | async-start | bytes 589824 | tf_op jit(solution)/shard_map/all_to_all | solution.py:559
  161.8 13.1 %copy-start.1 = (f32[4,4096]{1,0:T(4,128)S(1)}, f32[4,4096]{1,0:T(4,128)}, u32[]{:S(2)}) copy-start(f32[4,4096]{1,0:T(4,128)} %param.9) | copy-start | bytes 196612

commit v5 on v4

--- a/solution.py
+++ b/solution.py
@@ -324,14 +324,15 @@
 
 
 def second_kernel(features, early, grad_ref, cum_ref, cumt_ref, store,
-                  act_ref, dx_ref, dbc_ref, bc_act, dlog_ref, bc_hi, bc_lo, sems):
+                  act_ref, dx_ref, dbc_ref, slope_ref, bc_act, dlog_ref, bc_hi, bc_lo, sems):
     rows = slice(0, BLOCK)
     coming = begin(
         sems, (features.at[0], act_ref), (early.at[3], bc_act), (early.at[0, rows], dx_ref.at[rows]),
         (early.at[1, rows], dbc_ref.at[rows]), (early.at[4, rows, 0:LANES], dlog_ref.at[rows]),
-    )
-    leaving = begin(sems, (early.at[2], store.at[2]), (early.at[3], store.at[3]), first=5)
+        (early.at[2], slope_ref),
+    )
     finish(coming)
+    leaving = begin(sems, (slope_ref, store.at[2]), (bc_act, store.at[3]), first=6)
     bc_hi[...], bc_lo[...] = split2(bc_act[...])
     diagonal(1, act_ref, grad_ref, cum_ref, cumt_ref, bc_hi, bc_lo, dx_ref, dbc_ref, dlog_ref)
     row, col = row_col()
@@ -356,7 +357,7 @@
     dlog_ref[first, 0:HEADS] += exact_left(before, head_sums(faded * pulls, spread), NN)[:, 0:HEADS]
     dlog_ref[second, 0:HEADS] += exact_left(later, head_sums(grown * reads, spread), NN)[:, 0:HEADS]
     leaving += begin(
-        sems, (dx_ref, store.at[0]), (dbc_ref, store.at[1]), (dlog_ref, store.at[4, :, 0:LANES]), first=7
+        sems, (dx_ref, store.at[0]), (dbc_ref, store.at[1]), (dlog_ref, store.at[4, :, 0:LANES]), first=8
     )
     finish(leaving)
 
@@ -531,8 +532,8 @@
     early, back = lax.optimization_barrier((early, back))
     (blocks,) = call(
         second_kernel, [(store, F32)],
-        [(wide, F32)] * 4 + [((ROWS, LANES), F32)] + [(wide, BF16)] * 2,
-        hbm_in=(0, 1), hbm_out=(0,), count=5, sems=10, flops=1 << 32,
+        [(wide, F32)] * 5 + [((ROWS, LANES), F32)] + [(wide, BF16)] * 2,
+        hbm_in=(0, 1), hbm_out=(0,), count=5, sems=11, flops=1 << 32,
     )(features, early, grad_y, cum, cumt)
     carried = lax.all_to_all(back.astype(jnp.float16), CTX, 0, 0, tiled=True).astype(F32)
 

time: 178 us -> 127 us (0.71)
  Pallas kernels: 90.9 us -> 34.1 us
  waiting for transfers between devices: 17 us -> 22.6 us
    pallas_call x1, Pallas kernels: 64.7 us -> 7.96 us  [per_device(): call(second_kernel, [(store, F32)], [(wide, F32)] * 5 + [((ROWS, LANES),...]
    all_to_all x1, waiting for transfers between devices: 0.01 us -> 5.53 us  [per_device(): lax.all_to_all(back.astype(jnp.float16), CTX, 0, 0, tiled=True).astype(F32)]
  transfers between devices with their start and end apart: 9 -> 9, of which waited for: 4 -> 5; matrix products, arithmetic and copies ran while one was open for 0% -> 1% of each run, Pallas kernels for 47% -> 20%
where the time goes in v5:
time: 127 us; the launch traced here: 125 us
  starting transfers between devices  53.5 us (42%)
  Pallas kernels  34.1 us (27%)
  waiting for transfers between devices  22.6 us (18%)
  local copies, waits for them, and re-layouts  7.11 us (6%)
  other arithmetic  4.8 us (4%)
  blocking collectives  2.18 us (2%)
    all_to_all x1, starting transfers between devices, per_device(): mine = lax.all_to_all(spread, ('x', 'zh'), 0, 0, tiled=True)  13.4 us
    all_to_all x1, starting transfers between devices, per_device(): lax.all_to_all(summed.astype(jnp.float16), ('x', 'zh'), 0, 0, tiled=True)  8.87 us
    all_to_all x1, waiting for transfers between devices, per_device(): got = lax.all_to_all(sent.astype(jnp.float16), CTX, 0, 0, tiled=True)  8.5 us
    ppermute x1, starting transfers between devices, per_device(): lax.ppermute(give, 'core', swap)  8.44 us
    pallas_call x1, Pallas kernels, per_device(): call(second_kernel, [(store, F32)], [(wide, F32)] * 5 + [((ROWS, LANES),...  7.96 us
    all_to_all x1, starting transfers between devices, per_device(): got = lax.all_to_all(sent.astype(jnp.float16), CTX, 0, 0, tiled=True)  7.76 us
    unnamed x22, local copies, waits for them, and re-layouts  6.38 us
    pallas_call x1, Pallas kernels, per_device(): call(carry_kernel, [(wide, BF16), ((HEADS, ROWS), F32)], [padded, pair] +...  6.22 us
  transfers between devices with their start and end apart: 9, of which 5 were waited for; matrix products, arithmetic and copies ran while one was open for 1% of the time, Pallas kernels for 20%

profile of v5, /device:TPU:1, one launch (start us, length us, event | category | flops | bytes accessed | tf_op | source)
XLA Modules:
  0.0 125.2 jit_solution(17114467408906228060)
XLA Ops:
  0.6 0.0 copy-start
  0.6 1.8 %shard_map.85 = bf16[16,16,512]{2,1,0:T(8,128)(2,1)} custom-call(bf16[16,4096]{1,0:T(8,128)(2,1)} %rows_hbm.1), custom_call_target="tpu_custom_call" | custom-call | flops 67108864 | bytes 4194304 | tf_op jit(solution)/shard_map/pallas_call | solution.py:495
  2.4 13.4 %all-to-all-start = ((bf16[16,16,512]{2,1,0:T(8,128)(2,1)}), bf16[16,16,512]{2,1,0:T(8,128)(2,1)S(1)}, u32[]{:S(2)}, u32[]{:S(2)}) async-start(bf16[16,16,512]{2,1,0:T(8,128)(2,1)} %shard_map.85), calls=%async_computation | async-start | bytes 524288 | tf_op jit(solution)/shard_map/all_to_all | solution.py:498
  15.9 0.7 slice.7
  16.6 3.1 %collective-permute-start = (bf16[16,512]{1,0:T(8,128)(2,1)S(1)}, bf16[16,512]{1,0:T(8,128)(2,1)S(1)}, u32[]{:S(2)}, u32[]{:S(2)}) collective-permute-start(bf16[16,512]{1,0:T(8,128)(2,1)S(1)} %slice.7), channel_id=1, source_target_pairs={{0,32},{32,64},{64,96},{96,128},{128,160},{160,192},{192,224},{224... | collective-permute-start | bytes 49160 | tf_op jit(solution)/shard_map/ppermute | solution.py:481
  19.7 0.0 copy-done
  19.7 0.0 copy-start.2
  19.7 1.0 copy-done.2
  20.8 0.0 copy-start.10
  20.8 0.7 copy-done.10
  21.5 1.1 shard_map.86
  22.5 0.0 collective-permute-done.prev_ref
  22.6 0.0 copy-start.7
  22.6 1.0 copy-done.7
  23.6 0.0 copy-start.8
  23.6 0.7 copy-done.8
  24.3 3.4 %shard_map.87 = (f32[26,512,512]{2,1,0:T(8,128)}, bf16[512,512]{1,0:T(8,128)(2,1)S(1)}, bf16[512,512]{1,0:T(8,128)(2,1)S(1)}) custom-call(bf16[512,512]{1,0:T(8,128)(2,1)S(1)} %copy-done.7, bf16[16,512]{1,0:T(8,128)(2,1)S(1)} %collective-permute-done.prev_ref, f32[4,512]{1,0:T(4,128)S(1)} %copy-done.8, f32[512,128]{1,0:T(8,128)S(1)} %get-tuple-element.25.cum_ref), custom_call_target="tpu_custom_call" | custom-call | flops 67108864 | bytes 4194304 | tf_op jit(solution)/shard_map/pallas_call | solution.py:506
  27.7 0.0 all-to-all-done
  27.7 3.8 %collective-permute-start.2 = (bf16[16,512]{1,0:T(8,128)(2,1)S(1)}, bf16[16,512]{1,0:T(8,128)(2,1)S(1)}, u32[]{:S(2)}, u32[]{:S(2)}) collective-permute-start(bf16[16,512]{1,0:T(8,128)(2,1)S(1)} %slice_bitcast_fusion), channel_id=1, source_target_pairs={{1,33},{33,65},{65,97},{97,129},{129,161},{161,193},{193,225},{225... | collective-permute-start | bytes 49160 | tf_op jit(solution)/shard_map/ppermute | solution.py:514
  31.5 2.2 %collective-permute-start.1 = (bf16[16,512]{1,0:T(8,128)(2,1)S(1)}, bf16[16,512]{1,0:T(8,128)(2,1)S(1)}, u32[]{:S(2)}, u32[]{:S(2)}) collective-permute-start(bf16[16,512]{1,0:T(8,128)(2,1)S(1)} %slice_bitcast_fusion), channel_id=1, source_target_pairs={{1,32},{33,64},{65,96},{97,128},{129,160},{161,192},{193,224},{225... | collective-permute-start | bytes 49160 | tf_op jit(solution)/shard_map/ppermute | solution.py:514
  33.7 2.2 %all-gather = bf16[32,16,512]{2,1,0:T(8,128)(2,1)S(1)} all-gather(bf16[16,16,512]{2,1,0:T(8,128)(2,1)S(1)} %all-to-all-done), channel_id=2, replica_groups=mesh['y'=8,'zl'=2,'x'=4,'zh'=4,'core'=2] {'core'}, dimensions={0}, use_global_device_ids=true | all-gather | bytes 786432 | tf_op jit(solution)/shard_map/all_gather | solution.py:519
  35.8 0.0 collective-permute-done.2.prev_1
  35.8 0.0 collective-permute-done.1.prev_0
  35.8 1.8 %shard_map.88 = f32[16,136,128]{2,1,0:T(8,128)S(1)} custom-call(bf16[2,16,16,512]{3,2,1,0:T(8,128)(2,1)S(1)} %bitcast.6, bf16[16,512]{1,0:T(8,128)(2,1)S(1)} %collective-permute-done.1.prev_0, bf16[16,512]{1,0:T(8,128)(2,1)S(1)} %collective-permute-done.2.prev_1, f32[4,512]{1,0:T(4,128)S(1)} %constant_dynamic-slice_fusion.taps_ref, ...), custom_call_target="tpu_custom_call" | custom-call | flops 67108864 | bytes 4194304 | tf_op jit(solution)/shard_map/pallas_call | solution.py:521
  37.7 0.0 copy-start.5
  37.7 0.8 copy-done.5
  38.4 0.9 convert_element_type.18
  39.3 7.8 %all-to-all-start.1 = ((f16[16,136,128]{2,1,0:T(8,128)(2,1)}), f16[16,136,128]{2,1,0:T(8,128)(2,1)}, u32[]{:S(2)}, u32[]{:S(2)}) async-start(f16[16,136,128]{2,1,0:T(8,128)(2,1)} %convert_element_type.18), calls=%async_computation.1 | async-start | bytes 1114112 | tf_op jit(solution)/shard_map/all_to_all | solution.py:524
  47.1 0.0 copy-start.3
  47.1 1.0 copy-done.3
  48.1 0.0 copy-start.6
  48.1 1.0 copy-done.6
  49.2 0.0 copy-start.4
  49.2 4.6 %shard_map.89.early = f32[26,512,512]{2,1,0:T(8,128)} custom-call(f32[26,512,512]{2,1,0:T(8,128)} %get-tuple-element.33.features, bf16[512,512]{1,0:T(8,128)(2,1)S(1)} %copy-done.3, bf16[2,16,16,512]{3,2,1,0:T(8,128)(2,1)S(1)} %bitcast.7, bf16[16,512]{1,0:T(8,128)(2,1)S(1)} %collective-permute-done.1.prev_0, ...), custom_call_target="tpu_custom_call" | custom-call | flops 4294967296 | bytes 4194304 | tf_op jit(solution)/shard_map/pallas_call | solution.py:525
  53.8 8.5 %all-to-all-done.1 = f16[16,136,128]{2,1,0:T(8,128)(2,1)} async-done(((f16[16,136,128]{2,1,0:T(8,128)(2,1)}), f16[16,136,128]{2,1,0:T(8,128)(2,1)}, u32[]{:S(2)}, u32[]{:S(2)}) %all-to-all-start.1) | async-done | bytes 557088 | tf_op jit(solution)/shard_map/all_to_all | solution.py:524
  62.3 1.1 convert_element_type.19.got_ref
  63.4 1.2 shard_map.90
  64.6 0.9 convert_element_type.20
  65.5 4.6 %all-to-all-start.2 = ((f16[16,136,128]{2,1,0:T(8,128)(2,1)}), f16[16,136,128]{2,1,0:T(8,128)(2,1)}, u32[]{:S(2)}, u32[]{:S(2)}) async-start(f16[16,136,128]{2,1,0:T(8,128)(2,1)} %convert_element_type.20), calls=%async_computation.2 | async-start | bytes 1114112 | tf_op jit(solution)/shard_map/all_to_all | solution.py:538
  70.1 0.0 copy-done.4
  70.2 8.0 %shard_map.91.blocks = f32[26,512,512]{2,1,0:T(8,128)} custom-call(f32[26,512,512]{2,1,0:T(8,128)} %get-tuple-element.33.features, f32[26,512,512]{2,1,0:T(8,128)} %shard_map.89.early, bf16[512,512]{1,0:T(8,128)(2,1)S(1)} %copy-done.4, f32[512,128]{1,0:T(8,128)S(1)} %get-tuple-element.25.cum_ref, f32[2,8,256]{2,1,0:T(8,128)S(1)} %get-tuple-element.35.cumt_ref), custom_call_target="tpu_custom_call" | custom-call | flops 4294967296 | bytes 4194304 | tf_op jit(solution)/shard_map/pallas_call | solution.py:533
  78.1 5.5 %all-to-all-done.2 = f16[16,136,128]{2,1,0:T(8,128)(2,1)} async-done(((f16[16,136,128]{2,1,0:T(8,128)(2,1)}), f16[16,136,128]{2,1,0:T(8,128)(2,1)}, u32[]{:S(2)}, u32[]{:S(2)}) %all-to-all-start.2) | async-done | bytes 557088 | tf_op jit(solution)/shard_map/all_to_all | solution.py:538
  83.6 1.1 convert_element_type.21.got_ref
  84.8 1.8 %shard_map.92 = (bf16[52,512,512]{2,1,0:T(8,128)(2,1)}, f32[8,512]{1,0:T(8,128)S(1)}, f32[8,1024]{1,0:T(8,128)S(1)}) custom-call(f32[16,136,128]{2,1,0:T(8,128)S(1)} %convert_element_type.21.got_ref, bf16[512,512]{1,0:T(8,128)(2,1)S(1)} %get-tuple-element.29.xf_hi, bf16[512,512]{1,0:T(8,128)(2,1)S(1)} %get-tuple-element.30.xf_lo, ...), custom_call_target="tpu_custom_call" | custom-call | flops 67108864 | bytes 4194304 | tf_op jit(solution)/shard_map/pallas_call | solution.py:543
  86.6 1.3 %collective-permute-start.3 = (f32[8,1024]{1,0:T(8,128)S(1)}, f32[8,1024]{1,0:T(8,128)S(1)}, u32[]{:S(2)}, u32[]{:S(2)}) collective-permute-start(f32[8,1024]{1,0:T(8,128)S(1)} %get-tuple-element.42), channel_id=1, source_target_pairs={{32,0},{64,32},{96,64},{128,96},{160,128},{192,160},{224,192},{256... | collective-permute-start | bytes 98312 | tf_op jit(solution)/shard_map/ppermute | solution.py:481
  87.9 0.0 copy-start.9
  87.9 2.4 %shard_map.94.rows_ref = f32[512,512]{1,0:T(8,128)S(1)} custom-call(bf16[512,512]{1,0:T(8,128)(2,1)S(1)} %get-tuple-element.29.xf_hi, bf16[512,512]{1,0:T(8,128)(2,1)S(1)} %get-tuple-element.30.xf_lo, bf16[512,512]{1,0:T(8,128)(2,1)S(1)} %get-tuple-element.31.ge_hi, bf16[512,512]{1,0:T(8,128)(2,1)S(1)} %get-tuple-element.32.ge_lo, ...), custom_call_target="tpu_custom_call" | custom-call | flops 67108864 | bytes 4194304 | tf_op jit(solution)/shard_map/pallas_call | solution.py:550
  90.3 0.9 collective-permute-done.3.halo_ref
  91.2 1.0 shard_map.95
  92.2 8.4 %collective-permute-start.4 = (f32[16,16,512]{2,1,0:T(8,128)S(1)}, f32[16,16,512]{2,1,0:T(8,128)S(1)}, u32[]{:S(2)}, u32[]{:S(2)}) collective-permute-start(f32[16,16,512]{2,1,0:T(8,128)S(1)} %get-tuple-element.45), channel_id=1, source_target_pairs={{0,1},{1,0},{2,3},{3,2},{4,5},{5,4},{6,7},{7,6},{8,9},{9,8},{10,11... | collective-permute-start | bytes 1572872 | tf_op jit(solution)/shard_map/ppermute | solution.py:558
  100.7 1.5 %collective-permute-done.4.got_ref = f32[16,16,512]{2,1,0:T(8,128)S(1)} collective-permute-done((f32[16,16,512]{2,1,0:T(8,128)S(1)}, f32[16,16,512]{2,1,0:T(8,128)S(1)}, u32[]{:S(2)}, u32[]{:S(2)}) %collective-permute-start.4) | collective-permute-done | bytes 524320 | tf_op jit(solution)/shard_map/ppermute | solution.py:558
  102.2 0.2 shard_map.96
  102.3 0.8 convert_element_type.22
  103.1 8.9 %all-to-all-start.3 = ((f16[16,72,128]{2,1,0:T(8,128)(2,1)}), f16[16,72,128]{2,1,0:T(8,128)(2,1)S(1)}, u32[]{:S(2)}, u32[]{:S(2)}) async-start(f16[16,72,128]{2,1,0:T(8,128)(2,1)} %convert_element_type.22), calls=%async_computation.3 | async-start | bytes 589824 | tf_op jit(solution)/shard_map/all_to_all | solution.py:560
  112.0 0.0 copy-start.1
  112.0 0.0 copy-done.9
  112.0 6.2 %shard_map.93 = (bf16[512,512]{1,0:T(8,128)(2,1)}, f32[8,512]{1,0:T(8,128)}) custom-call(bf16[512,512]{1,0:T(8,128)(2,1)S(1)} %get-tuple-element.29.xf_hi, bf16[512,512]{1,0:T(8,128)(2,1)S(1)} %get-tuple-element.30.xf_lo, bf16[512,512]{1,0:T(8,128)(2,1)S(1)} %get-tuple-element.31.ge_hi, bf16[512,512]{1,0:T(8,128)(2,1)S(1)} %get-tuple-element.32.ge_lo, ...), custom_call_target="tpu_custom_call" | custom-call | flops 67108864 | bytes 4194304 | tf_op jit(solution)/shard_map/pallas_call | solution.py:561
  118.2 6.2 %all-to-all-done.3 = f16[16,72,128]{2,1,0:T(8,128)(2,1)S(1)} async-done(((f16[16,72,128]{2,1,0:T(8,128)(2,1)}), f16[16,72,128]{2,1,0:T(8,128)(2,1)S(1)}, u32[]{:S(2)}, u32[]{:S(2)}) %all-to-all-start.3) | async-done | bytes 294944 | tf_op jit(solution)/shard_map/all_to_all | solution.py:560
  124.4 0.7 shard_map.97
  125.2 0.0 copy-done.1
  (3 shorter events, 0.1 us)
Async XLA Ops:
  0.6 19.1 %copy-start = (f32[4,4096]{1,0:T(4,128)S(1)}, f32[4,4096]{1,0:T(4,128)}, u32[]{:S(2)}) copy-start(f32[4,4096]{1,0:T(4,128)} %param.9) | copy-start | bytes 196612
  2.4 25.3 %all-to-all-start = ((bf16[16,16,512]{2,1,0:T(8,128)(2,1)}), bf16[16,16,512]{2,1,0:T(8,128)(2,1)S(1)}, u32[]{:S(2)}, u32[]{:S(2)}) async-start(bf16[16,16,512]{2,1,0:T(8,128)(2,1)} %shard_map.85), calls=%async_computation | async-start | bytes 524288 | tf_op jit(solution)/shard_map/all_to_all | solution.py:498
  16.6 6.0 %collective-permute-start = (bf16[16,512]{1,0:T(8,128)(2,1)S(1)}, bf16[16,512]{1,0:T(8,128)(2,1)S(1)}, u32[]{:S(2)}, u32[]{:S(2)}) collective-permute-start(bf16[16,512]{1,0:T(8,128)(2,1)S(1)} %slice.7), channel_id=1, source_target_pairs={{0,32},{32,64},{64,96},{96,128},{128,160},{160,192},{192,224},{224... | collective-permute-start | bytes 49160 | tf_op jit(solution)/shard_map/ppermute | solution.py:481
  19.7 1.0 copy-start.2
  20.8 0.7 copy-start.10
  22.6 1.0 copy-start.7
  23.6 0.7 copy-start.8
  27.7 8.1 %collective-permute-start.2 = (bf16[16,512]{1,0:T(8,128)(2,1)S(1)}, bf16[16,512]{1,0:T(8,128)(2,1)S(1)}, u32[]{:S(2)}, u32[]{:S(2)}) collective-permute-start(bf16[16,512]{1,0:T(8,128)(2,1)S(1)} %slice_bitcast_fusion), channel_id=1, source_target_pairs={{1,33},{33,65},{65,97},{97,129},{129,161},{161,193},{193,225},{225... | collective-permute-start | bytes 49160 | tf_op jit(solution)/shard_map/ppermute | solution.py:514
  31.5 4.4 %collective-permute-start.1 = (bf16[16,512]{1,0:T(8,128)(2,1)S(1)}, bf16[16,512]{1,0:T(8,128)(2,1)S(1)}, u32[]{:S(2)}, u32[]{:S(2)}) collective-permute-start(bf16[16,512]{1,0:T(8,128)(2,1)S(1)} %slice_bitcast_fusion), channel_id=1, source_target_pairs={{1,32},{33,64},{65,96},{97,128},{129,160},{161,192},{193,224},{225... | collective-permute-start | bytes 49160 | tf_op jit(solution)/shard_map/ppermute | solution.py:514
  37.7 0.8 copy-start.5
  39.3 23.0 %all-to-all-start.1 = ((f16[16,136,128]{2,1,0:T(8,128)(2,1)}), f16[16,136,128]{2,1,0:T(8,128)(2,1)}, u32[]{:S(2)}, u32[]{:S(2)}) async-start(f16[16,136,128]{2,1,0:T(8,128)(2,1)} %convert_element_type.18), calls=%async_computation.1 | async-start | bytes 1114112 | tf_op jit(solution)/shard_map/all_to_all | solution.py:524
  47.1 1.0 copy-start.3
  48.1 1.0 copy-start.6
  49.2 21.0 %copy-start.4 = (bf16[512,512]{1,0:T(8,128)(2,1)S(1)}, bf16[512,512]{1,0:T(8,128)(2,1)}, u32[]{:S(2)}) copy-start(bf16[512,512]{1,0:T(8,128)(2,1)} %grad_ref.5) | copy-start | bytes 1572868
  65.5 18.1 %all-to-all-start.2 = ((f16[16,136,128]{2,1,0:T(8,128)(2,1)}), f16[16,136,128]{2,1,0:T(8,128)(2,1)}, u32[]{:S(2)}, u32[]{:S(2)}) async-start(f16[16,136,128]{2,1,0:T(8,128)(2,1)} %convert_element_type.20), calls=%async_computation.2 | async-start | bytes 1114112 | tf_op jit(solution)/shard_map/all_to_all | solution.py:538
  86.6 4.7 %collective-permute-start.3 = (f32[8,1024]{1,0:T(8,128)S(1)}, f32[8,1024]{1,0:T(8,128)S(1)}, u32[]{:S(2)}, u32[]{:S(2)}) collective-permute-start(f32[8,1024]{1,0:T(8,128)S(1)} %get-tuple-element.42), channel_id=1, source_target_pairs={{32,0},{64,32},{96,64},{128,96},{160,128},{192,160},{224,192},{256... | collective-permute-start | bytes 98312 | tf_op jit(solution)/shard_map/ppermute | solution.py:481
  87.9 24.2 %copy-start.9 = (f32[4,512]{1,0:T(4,128)S(1)}, f32[4,512]{1,0:T(4,128)}, u32[]{:S(2)}) copy-start(f32[4,512]{1,0:T(4,128)} %taps_ref.3) | copy-start | bytes 24580
  92.2 10.0 %collective-permute-start.4 = (f32[16,16,512]{2,1,0:T(8,128)S(1)}, f32[16,16,512]{2,1,0:T(8,128)S(1)}, u32[]{:S(2)}, u32[]{:S(2)}) collective-permute-start(f32[16,16,512]{2,1,0:T(8,128)S(1)} %get-tuple-element.45), channel_id=1, source_target_pairs={{0,1},{1,0},{2,3},{3,2},{4,5},{5,4},{6,7},{7,6},{8,9},{9,8},{10,11... | collective-permute-start | bytes 1572872 | tf_op jit(solution)/shard_map/ppermute | solution.py:558
  103.1 21.3 %all-to-all-start.3 = ((f16[16,72,128]{2,1,0:T(8,128)(2,1)}), f16[16,72,128]{2,1,0:T(8,128)(2,1)S(1)}, u32[]{:S(2)}, u32[]{:S(2)}) async-start(f16[16,72,128]{2,1,0:T(8,128)(2,1)} %convert_element_type.22), calls=%async_computation.3 | async-start | bytes 589824 | tf_op jit(solution)/shard_map/all_to_all | solution.py:560
  112.0 13.2 %copy-start.1 = (f32[4,4096]{1,0:T(4,128)S(1)}, f32[4,4096]{1,0:T(4,128)}, u32[]{:S(2)}) copy-start(f32[4,4096]{1,0:T(4,128)} %param.9) | copy-start | bytes 196612
